TPU v7x, 256 devices: a whole 4x4x8 slice. The times are simulated.
256 devices in a mesh: row: 8 (over z), col: 32 (over y, x, core).
Axes of the slice: x: 4, y: 4, z: 8, core: 2. Of those that a mesh axis runs over, the one named last changes fastest.
Arguments:
- psi: bfloat16 [1024, 128, 128], P(('row', 'col')), may hold values from -6 to 6
- right_env: bfloat16 [1024, 128, 32, 128], P(('row', 'col')), may hold values from -0.5 to 0.5
- left_env: bfloat16 [8, 128, 32, 128], P('row'), may hold values from -0.09375 to 0.09375
- env_index: int32 [8192], P(('row', 'col')), may hold values from 0 to 7
- source_block: int32 [8192], P(('row', 'col')), may hold values from 0 to 3
- target_slot: int32 [8192], P(('row', 'col')), may hold values from 0 to 63, as said below
- target_block: int32 [8192], P(('row', 'col')), may hold values from 0 to 3
Outputs:
- psi_next: bfloat16 [1024, 128, 128], P(('row', 'col'))
Inputs may be any that keep to these rules, and one draw needn't show every extreme that they name: `target_slot`: on each device's 32 pairs the entries are distinct; entry s is slot s % 2 toward col index s // 2. In every row one col index, drawn from the seed, receives all 2 slots from every device of that row. Every device's list holds slot 0 and slot 32 * 2 - 1.
All inputs are finite; a program needn't handle non-finite values.
Results may differ from a plain program's by a relative error of at most 0.01.
Values may be sent and summed in bfloat16 or wider, within the bound.
No kernel may reach another device: no remote copies, remote signals or barrier semaphores. Data moves between devices by JAX's collectives and lax.ppermute only.
A program may use at most 128 MiB of HBM per device.

v0:
```python
import jax
import jax.numpy as jnp
from jax import lax
from jax.sharding import PartitionSpec as P

step_size = 0.3


def on_device(psi, right_env, left_env, env_index, source_block, target_slot, target_block):
    nblocks = psi.shape[0]
    environment_side = psi.shape[1]
    width = right_env.shape[2]
    pair_count = env_index.shape[0]
    slot_count = 2 * pair_count
    env_total = left_env.shape[0] * lax.axis_size("row")
    combos = env_total * nblocks
    slot_positions = jnp.arange(slot_count, dtype=jnp.int32)
    send_match = target_slot[None, :] == slot_positions[:, None]
    send_index = jnp.sum(jnp.where(send_match, target_block[None, :] + 1, 0), axis=1) - 1
    pair_combo = env_index * nblocks + source_block
    combo_match = (pair_combo[:, None] == jnp.arange(combos, dtype=jnp.int32)[None, :]).astype(
        jnp.bfloat16
    )
    send_table = jnp.dot(
        send_match.astype(jnp.bfloat16), combo_match, preferred_element_type=jnp.float32
    ).astype(jnp.bfloat16)
    flat_right = right_env.reshape(nblocks, environment_side, width * environment_side)
    block_range = jnp.arange(nblocks, dtype=jnp.int32)
    state = psi
    gathered = lax.all_gather(left_env, "row", axis=0, tiled=True)
    for step in range(2):
        product = jnp.einsum("bkl,blm->bkm", state, flat_right, preferred_element_type=jnp.float32)
        product = product.astype(jnp.bfloat16).reshape(
            nblocks, environment_side, width, environment_side
        )
        combined = jnp.einsum(
            "eawk,bkwj->ebaj", gathered, product, preferred_element_type=jnp.float32
        )
        combined = combined.astype(jnp.bfloat16).reshape(
            combos, environment_side * environment_side
        )
        outbound_blocks = jnp.dot(send_table, combined, preferred_element_type=jnp.float32).astype(
            jnp.bfloat16
        )
        outbound_blocks = outbound_blocks.reshape(slot_count, environment_side, environment_side)
        inbound_blocks = lax.all_to_all(
            outbound_blocks, "col", split_axis=0, concat_axis=0, tiled=True
        )
        incoming_index = lax.all_to_all(send_index, "col", split_axis=0, concat_axis=0, tiled=True)
        receive_lookup = (incoming_index[None, :] == block_range[:, None]).astype(jnp.bfloat16)
        gradient = jnp.dot(
            receive_lookup,
            inbound_blocks.reshape(slot_count, environment_side * environment_side),
            preferred_element_type=jnp.float32,
        )
        gradient = gradient.reshape(nblocks, environment_side, environment_side)
        state = (state.astype(jnp.float32) - step_size * gradient).astype(jnp.bfloat16)
    return state


def solution(mesh):
    placed = (
        P(("row", "col"), None, None),
        P(("row", "col"), None, None, None),
        P("row", None, None, None),
        P(("row", "col")),
        P(("row", "col")),
        P(("row", "col")),
        P(("row", "col")),
    )
    return jax.shard_map(
        on_device,
        mesh=mesh,
        in_specs=placed,
        out_specs=P(("row", "col"), None, None),
        check_vma=False,
    )
```

profile of v0, /device:TPU:1, one launch (start us, length us, event | category | flops | bytes accessed | tf_op | source)
XLA Modules:
  0.0 223.5 jit_solution(676511187048603605)
XLA Ops:
  6.5 0.0 all-gather.2.cloned.1.call-start
  6.5 0.7 all-gather.2.cloned.1.call-update
  7.3 0.7 broadcast_add_fusion.1
  7.9 0.7 select_reduce_fusion
  8.7 0.7 sub.13
  9.4 8.6 %all-to-all-start = ((s32[32,2,1]{1,2,0:T(1,128)}), s32[32,2,1]{1,2,0:T(1,128)S(1)}, u32[]{:S(2)}, u32[]{:S(2)}) async-start(s32[32,2,1]{1,2,0:T(1,128)} %bitcast), calls=%async_computation | async-start | bytes 32768 | tf_op jit(solution)/shard_map/all_to_all | solution.py:49
  18.0 0.0 copy-start
  18.0 7.3 %reshape.51 = bf16[4,128,4096]{2,1,0:T(8,128)(2,1)} reshape(bf16[4,128,32,128]{3,2,1,0:T(8,128)(2,1)} %param.8) | data formatting | bytes 8388608 | tf_op jit(solution)/shard_map/reshape | solution.py:27
  25.3 0.0 copy-done
  25.3 3.4 %convolution_convert_fusion.3 = bf16[4,128,4096]{2,1,0:T(8,128)(2,1)S(1)} fusion(bf16[4,128,128]{2,1,0:T(8,128)(2,1)S(1)} %copy-done, bf16[4,128,4096]{2,1,0:T(8,128)(2,1)} %reshape.51), kind=kOutput, calls=%fused_computation.7 | convolution fusion | flops 538968064 | bytes 8519680 | tf_op jit(solution)/shard_map/bkl,blm->bkm/dot_general | solution.py:32
  28.8 0.0 copy-start.1
  28.8 0.0 copy-start.2
  28.8 0.0 copy-start.3
  28.8 3.2 %copy.59 = bf16[64,8,32,128]{3,2,1,0:T(8,128)(2,1)} copy(bf16[64,8,32,128]{3,1,2,0:T(8,128)(2,1)S(1)} %bitcast.108) | data formatting | bytes 8388608
  32.0 0.0 copy-done.1
  32.1 0.0 copy-done.2
  32.1 0.0 copy-done.3
  32.1 0.3 convolution_convert_fusion.4
  32.3 74.8 %all-gather.2.cloned.1.call-done = bf16[8,128,32,128]{3,2,1,0:T(8,128)(2,1)} async-done(((bf16[1,128,32,128]{3,2,1,0:T(8,128)(2,1)}), bf16[8,128,32,128]{3,2,1,0:T(8,128)(2,1)}) %all-gather.2.cloned.1.call-update) | async-done | bytes 8388624 | tf_op jit(solution)/shard_map/all_gather | solution.py:30
  107.1 13.3 %copy.45 = bf16[8,128,32,128]{1,2,3,0:T(8,128)(2,1)} copy(bf16[8,128,32,128]{3,2,1,0:T(8,128)(2,1)} %all-gather.2.cloned.1.call-done) | data formatting | bytes 16777216 | tf_op jit(solution)/shard_map/all_gather | solution.py:30
  120.4 9.2 %fusion.22 = bf16[8,4,128,128]{2,3,0,1:T(8,128)(2,1)S(1)} fusion(bf16[8,128,32,128]{1,2,3,0:T(8,128)(2,1)} %copy.45, bf16[4,128,32,128,1]{3,2,1,0,4:T(8,128)(2,1)} %bitcast.114), kind=kOutput, calls=%fused_computation.22 | convolution fusion | flops 4295491584 | bytes 13631488 | tf_op jit(solution)/shard_map/eawk,bkwj->ebaj/dot_general | solution.py:36
  129.6 0.7 copy.46
  130.2 0.8 fusion.20
  131.1 1.9 copy.61
  133.0 0.0 all-to-all-done
  133.0 7.5 %all-to-all-start.1 = ((bf16[64,128,128]{2,1,0:T(8,128)(2,1)}), bf16[64,128,128]{2,1,0:T(8,128)(2,1)S(1)}, u32[]{:S(2)}, u32[]{:S(2)}) async-start(bf16[64,128,128]{2,1,0:T(8,128)(2,1)} %bitcast.28), calls=%async_computation.1 | async-start | bytes 4194304 | tf_op jit(solution)/shard_map/all_to_all | solution.py:46
  140.6 0.5 broadcast.30
  141.1 0.7 reduce.3
  141.8 0.1 eq.23
  141.9 26.5 %all-to-all-done.1 = bf16[64,128,128]{2,1,0:T(8,128)(2,1)S(1)} async-done(((bf16[64,128,128]{2,1,0:T(8,128)(2,1)}), bf16[64,128,128]{2,1,0:T(8,128)(2,1)S(1)}, u32[]{:S(2)}, u32[]{:S(2)}) %all-to-all-start.1) | async-done | bytes 2097184 | tf_op jit(solution)/shard_map/all_to_all | solution.py:46
  168.4 0.0 slice-start
  168.4 1.2 fusion.9
  169.6 0.0 slice-start.1
  169.6 3.6 %convolution_convert_fusion.2 = bf16[4,128,4096]{2,1,0:T(8,128)(2,1)S(1)} fusion(bf16[4,128,4096]{2,1,0:T(8,128)(2,1)} %reshape.51, f32[4,128,128]{2,0,1:T(4,128)S(1)} %fusion.9, bf16[4,128,128]{2,1,0:T(8,128)(2,1)S(1)} %copy-done), kind=kOutput, calls=%fused_computation.6 | convolution fusion | flops 539230208 | bytes 8781824 | tf_op jit(solution)/shard_map/bkl,blm->bkm/dot_general | solution.py:32
  173.2 1.3 copy.63
  174.4 0.0 slice-done
  174.4 0.0 slice-done.1
  174.5 4.5 %fusion.27 = bf16[8,4,128,128]{2,3,0,1:T(8,128)(2,1)S(1)} fusion(bf16[8,128,32,128]{1,2,3,0:T(8,128)(2,1)S(1)} %bitcast.110, bf16[4,128,32,128,1]{3,2,1,0,4:T(8,128)(2,1)S(1)} %bitcast.115), kind=kOutput, calls=%fused_computation.23 | convolution fusion | flops 4295491584 | bytes 13631488 | tf_op jit(solution)/shard_map/eawk,bkwj->ebaj/dot_general | solution.py:36
  179.0 0.7 copy.50
  179.6 0.8 fusion.21
  180.5 0.6 copy.65
  181.1 33.6 %all_to_all.17 = bf16[64,128,128]{2,1,0:T(8,128)(2,1)S(1)} all-to-all(bf16[64,128,128]{2,1,0:T(8,128)(2,1)S(1)} %bitcast.111), channel_id=1, replica_groups=mesh['row'=8,'col'=32] {'col'}, dimensions={0} | all-to-all | bytes 4194304 | tf_op jit(solution)/shard_map/all_to_all | solution.py:46
  214.7 1.2 fusion.6
  215.9 0.7 fusion.37
  (3 shorter events, 0.0 us)
Async XLA Ops:
  6.5 100.6 %all-gather.2.cloned.1.call-start = ((), (), s32[]{:S(2)}) async-start(), calls=%async_computation.3 | async-start | bytes 9437184 | tf_op jit(solution)/shard_map/all_gather | solution.py:30
  9.4 123.6 %all-to-all-start = ((s32[32,2,1]{1,2,0:T(1,128)}), s32[32,2,1]{1,2,0:T(1,128)S(1)}, u32[]{:S(2)}, u32[]{:S(2)}) async-start(s32[32,2,1]{1,2,0:T(1,128)} %bitcast), calls=%async_computation | async-start | bytes 32768 | tf_op jit(solution)/shard_map/all_to_all | solution.py:49
  18.0 7.3 %copy-start = (bf16[4,128,128]{2,1,0:T(8,128)(2,1)S(1)}, bf16[4,128,128]{2,1,0:T(8,128)(2,1)}, u32[]{:S(2)}) copy-start(bf16[4,128,128]{2,1,0:T(8,128)(2,1)} %param.7) | copy-start | bytes 393220
  28.8 3.3 %copy-start.1 = (s32[32]{0:T(128)S(1)}, s32[32]{0:T(128)}, u32[]{:S(2)}) copy-start(s32[32]{0:T(128)} %param.11) | copy-start | bytes 388
  28.8 3.3 %copy-start.2 = (s32[32]{0:T(128)S(1)}, s32[32]{0:T(128)}, u32[]{:S(2)}) copy-start(s32[32]{0:T(128)} %param.10) | copy-start | bytes 388
  28.8 3.3 %copy-start.3 = (s32[32]{0:T(128)S(1)}, s32[32]{0:T(128)}, u32[]{:S(2)}) copy-start(s32[32]{0:T(128)} %param.12) | copy-start | bytes 388
  133.0 35.3 %all-to-all-start.1 = ((bf16[64,128,128]{2,1,0:T(8,128)(2,1)}), bf16[64,128,128]{2,1,0:T(8,128)(2,1)S(1)}, u32[]{:S(2)}, u32[]{:S(2)}) async-start(bf16[64,128,128]{2,1,0:T(8,128)(2,1)} %bitcast.28), calls=%async_computation.1 | async-start | bytes 4194304 | tf_op jit(solution)/shard_map/all_to_all | solution.py:46
  168.4 6.1 %slice-start = ((s8[8388608]{0:T(1024)(128)(4,1)}), s8[4194304]{0:T(1024)(128)(4,1)S(1)}, s32[]{:S(2)}) async-start(s8[8388608]{0:T(1024)(128)(4,1)} %bitcast.109), calls=%async_computation.4 | async-start | bytes 8388608
  169.6 4.9 %slice-start.1 = ((s8[8388608]{0:T(1024)(128)(4,1)}), s8[4194304]{0:T(1024)(128)(4,1)S(1)}, s32[]{:S(2)}) async-start(s8[8388608]{0:T(1024)(128)(4,1)} %bitcast.109), calls=%async_computation.5 | async-start | bytes 8388608
Sparse Core Ops, SparseCore 0:
  9.1 97.9 all-gather.1
where the time goes:
time: 224 us; the launch traced here: 223 us
  waiting for transfers between devices  102 us (46%)
  blocking collectives  33.6 us (15%)
  local copies, waits for them, and re-layouts  30.3 us (14%)
  matrix products  25 us (11%)
  starting transfers between devices  16.1 us (7%)
  between operations  13.6 us (6%)
  other arithmetic  2.82 us (1%)
    all_gather x1, waiting for transfers between devices, on_device(): gathered = lax.all_gather(left_env, 'row', axis=0, tiled=True)  74.8 us
    all_to_all x1, blocking collectives, on_device(): lax.all_to_all(outbound_blocks, 'col', split_axis=0, concat_axis=0, tiled...  33.6 us
    all_to_all x1, waiting for transfers between devices, on_device(): lax.all_to_all(outbound_blocks, 'col', split_axis=0, concat_axis=0, tiled...  26.5 us
    dot_general x2, matrix products, on_device(): jnp.einsum('eawk,bkwj->ebaj', gathered, product, preferred_element_type=j...  13.7 us
    all_gather x1, local copies, waits for them, and re-layouts, on_device(): gathered = lax.all_gather(left_env, 'row', axis=0, tiled=True)  13.3 us
    all_to_all x1, starting transfers between devices, on_device(): lax.all_to_all(send_index, 'col', split_axis=0, concat_axis=0, tiled=True)  8.59 us
    all_to_all x1, starting transfers between devices, on_device(): lax.all_to_all(outbound_blocks, 'col', split_axis=0, concat_axis=0, tiled...  7.55 us
    reshape x1, local copies, waits for them, and re-layouts, on_device(): right_env.reshape(nblocks, environment_side, width * environment_side)  7.33 us
  transfers between devices with their start and end apart: 3, of which 2 were waited for; matrix products, arithmetic and copies ran while one was open for 19% of the time, Pallas kernels for 0%

commit v1 on v0

v1 whole, which is shorter than its diff:
```python
import jax
import jax.numpy as jnp
from jax import lax
from jax.experimental import pallas as pl
from jax.experimental.pallas import tpu as pltpu
from jax.sharding import PartitionSpec as P

step_size = 0.3
NX = 4
NY = 4

other_core = [(i, i ^ 1) for i in range(2 * NX * NY)]


def col_of(y, x, core):
    return (y * NX + x) * 2 + core


x_lines = [[[col_of(y, x, c) for x in range(NX)] for y in range(NY)] for c in range(2)]
y_lines = [[[col_of(y, x, c) for y in range(NY)] for x in range(NX)] for c in range(2)]
first_groups = x_lines[0] + y_lines[1]
second_groups = y_lines[0] + x_lines[1]


def contract_kernel(
    pairs, own_rows, other_rows, right_own, right_other, left, out,
    right_v, left_v, state, product, partial, right_sem, left_sem,
):
    nb, side, wide = right_own.shape
    half = side // 2
    blocks = 2 * nb
    pair_count = pairs.shape[1]
    core = pairs[3, 0]
    copies = []
    for b in range(blocks):
        src = right_own.at[b] if b < nb else right_other.at[b - nb]
        copies.append(pltpu.make_async_copy(src, right_v.at[b], right_sem.at[b]))
    left_copy = pltpu.make_async_copy(left, left_v, left_sem)
    for c in copies:
        c.start()
    left_copy.start()
    mine = pl.multiple_of(core * half, half)
    theirs = pl.multiple_of((1 - core) * half, half)
    state[:, pl.ds(mine, half), :] = own_rows[...]
    state[:, pl.ds(theirs, half), :] = other_rows[...]
    out[...] = jnp.zeros_like(out)
    step = 512
    for b in range(blocks):
        copies[b].wait()
        at = core * nb + b if b < nb else (1 - core) * nb + b - nb
        s = state[at]
        for n in range(wide // step):
            r = jnp.dot(
                s, right_v[b, :, n * step:(n + 1) * step], preferred_element_type=jnp.float32
            ).astype(jnp.bfloat16)
            for q in range(step // side):
                w = n * (step // side) + q
                product[w * side:(w + 1) * side, b * side:(b + 1) * side] = r[
                    :, q * side:(q + 1) * side
                ]
    left_copy.wait()
    for n in range(blocks // 2):
        r = jnp.dot(
            left_v[...], product[:, n * 2 * side:(n + 1) * 2 * side],
            preferred_element_type=jnp.float32,
        ).astype(jnp.bfloat16)
        partial[2 * n] = r[:, :side]
        partial[2 * n + 1] = r[:, side:]

    def place(p, carry):
        rows = pl.multiple_of(pairs[0, p] * half, half)
        to = pairs[2, p]
        value = partial[pairs[1, p], pl.ds(rows, half), :].astype(jnp.float32)
        out[to] = (out[to].astype(jnp.float32) + value).astype(jnp.bfloat16)
        return carry

    lax.fori_loop(0, pair_count, place, 0)


def contract(pairs, own_rows, other_rows, right_own, right_other, left):
    nb, side, wide = right_own.shape
    blocks = 2 * nb
    dests = NX * NY * blocks
    vmem = pl.BlockSpec(memory_space=pltpu.VMEM)
    anywhere = pl.BlockSpec(memory_space=pl.ANY)
    flops = 2 * (blocks * side * side * wide + left.shape[0] * wide * blocks * side)
    moved = 2 * (2 * right_own.size + left.size + dests * side * side // 2)
    return pl.pallas_call(
        contract_kernel,
        out_shape=jax.ShapeDtypeStruct((dests, side // 2, side), jnp.bfloat16),
        in_specs=[
            pl.BlockSpec(memory_space=pltpu.SMEM), vmem, vmem, anywhere, anywhere, anywhere
        ],
        out_specs=vmem,
        scratch_shapes=[
            pltpu.VMEM((blocks, side, wide), jnp.bfloat16),
            pltpu.VMEM(left.shape, jnp.bfloat16),
            pltpu.VMEM((blocks, side, side), jnp.bfloat16),
            pltpu.VMEM((wide, blocks * side), jnp.bfloat16),
            pltpu.VMEM((blocks, left.shape[0], side), jnp.bfloat16),
            pltpu.SemaphoreType.DMA((blocks,)),
            pltpu.SemaphoreType.DMA,
        ],
        compiler_params=pltpu.CompilerParams(vmem_limit_bytes=48 * 1024 * 1024),
        cost_estimate=pl.CostEstimate(flops=flops, bytes_accessed=moved, transcendentals=0),
        name="contract",
    )(pairs, own_rows, other_rows, right_own, right_other, left)


def on_device(psi, right_env, left_env, env_index, source_block, target_slot, target_block):
    nb, side, width, _ = right_env.shape
    half = side // 2
    blocks = 2 * nb
    core = lax.axis_index("col") % 2

    def swap(a):
        return lax.ppermute(a, "col", other_core)

    own_left = lax.dynamic_slice_in_dim(left_env[0], core * half, half, 0)
    left = lax.all_gather(
        own_left.reshape(half, width * side), "row", axis=0, tiled=True
    )

    owner = target_slot // 2
    y, x, c = owner // (2 * NX), (owner // 2) % NX, owner % 2
    x_first = ((x * NY + y) * 2 + c) * nb + target_block
    y_first = ((y * NX + x) * 2 + c) * nb + target_block
    lists = jnp.stack([env_index, source_block, x_first, y_first])
    theirs = swap(lists)
    both = jnp.concatenate([lists, theirs + jnp.array([[0], [nb], [0], [0]], jnp.int32)], axis=1)
    to = jnp.where(core == 0, both[2], both[3])
    pairs = jnp.stack([both[0], both[1], to, jnp.full_like(to, core)])

    right_own = right_env.reshape(nb, side, width * side)
    right_other = swap(right_own)
    psi_other = swap(psi)
    lower = jnp.where(core == 0, psi, psi_other)
    upper = jnp.where(core == 0, psi_other, psi)
    state = jnp.concatenate([lower, upper], axis=0)
    own_rows = jnp.where(core == 0, state[:, :half], state[:, half:])
    other_rows = jnp.where(core == 0, state[:, half:], state[:, :half])
    for step in range(2):
        sums = contract(pairs, own_rows, other_rows, right_own, right_other, left)
        got = lax.all_to_all(
            sums.reshape(4, 4 * blocks, half, side), "col", 0, 0,
            axis_index_groups=first_groups, tiled=True,
        )
        line = jnp.sum(got.astype(jnp.float32), axis=0).astype(jnp.bfloat16)
        got = lax.all_to_all(
            line.reshape(4, blocks, half, side), "col", 0, 0,
            axis_index_groups=second_groups, tiled=True,
        )
        gradient = jnp.sum(got.astype(jnp.float32), axis=0)
        own_rows = (own_rows.astype(jnp.float32) - step_size * gradient).astype(jnp.bfloat16)
        if step == 0:
            other_rows = swap(own_rows)
    keep = jnp.where(core == 0, own_rows[:nb], own_rows[nb:])
    send = jnp.where(core == 0, own_rows[nb:], own_rows[:nb])
    come = swap(send)
    top = jnp.where(core == 0, keep, come)
    bottom = jnp.where(core == 0, come, keep)
    return jnp.concatenate([top, bottom], axis=1)


def solution(mesh):
    placed = (
        P(("row", "col"), None, None),
        P(("row", "col"), None, None, None),
        P("row", None, None, None),
        P(("row", "col")),
        P(("row", "col")),
        P(("row", "col")),
        P(("row", "col")),
    )
    return jax.shard_map(
        on_device,
        mesh=mesh,
        in_specs=placed,
        out_specs=P(("row", "col"), None, None),
        check_vma=False,
    )
```

time: 224 us -> 167 us (0.75)
  waiting for transfers between devices: 102 us -> 49 us
  blocking collectives: 33.6 us -> 58.9 us
  matrix products: 25 us -> 0 us
  Pallas kernels: 0 us -> 21.9 us
  local copies, waits for them, and re-layouts: 30.3 us -> 9.81 us
  starting transfers between devices: 16.1 us -> 9.78 us
    all_gather x1, waiting for transfers between devices: 74.8 us -> 40.9 us  [on_device(): lax.all_gather(own_left.reshape(half, width * side), 'row', axis=0, tiled...]
    all_to_all x2 -> x0, waiting for transfers between devices: 26.5 us -> none  [the longest x1 26.5 us: on_device(): lax.all_to_all(outbound_blocks, 'col', split_axis=0, concat_axis=0, tiled...]
    all_to_all x1 -> x4, blocking collectives: 33.6 us -> 58.9 us  [the longest x2 37.6 us: on_device(): lax.all_to_all(sums.reshape(4, 4 * blocks, half, side), 'col', 0, 0, axis...]
    dot_general x9 -> x0, matrix products: 25 us -> none  [the longest x2 13.7 us: on_device(): jnp.einsum('eawk,bkwj->ebaj', gathered, product, preferred_element_type=j...]
    pallas_call x0 -> x2, Pallas kernels: none -> 21.9 us  [contract(): pl.pallas_call(contract_kernel, out_shape=jax.ShapeDtypeStruct((dests, si...]
    all_to_all x2 -> x0, starting transfers between devices: 16.1 us -> none  [the longest x1 8.59 us: on_device(): lax.all_to_all(send_index, 'col', split_axis=0, concat_axis=0, tiled=True)]
    all_gather x1 -> x0, local copies, waits for them, and re-layouts: 13.3 us -> none  [on_device(): gathered = lax.all_gather(left_env, 'row', axis=0, tiled=True)]
    ppermute x0 -> x5, starting transfers between devices: none -> 9.78 us  [swap(): return lax.ppermute(a, 'col', other_core)]
  transfers between devices with their start and end apart: 3 -> 6, of which waited for: 2 -> 5; matrix products, arithmetic and copies ran while one was open for 19% -> 5% of each run, Pallas kernels for 0% -> 0%
where the time goes in v1:
time: 167 us
  blocking collectives  58.9 us (35%)
  waiting for transfers between devices  49 us (29%)
  Pallas kernels  21.9 us (13%)
  between operations  13.6 us (8%)
  local copies, waits for them, and re-layouts  9.81 us (6%)
  starting transfers between devices  9.78 us (6%)
  other arithmetic  3.94 us (2%)
    all_gather x1, waiting for transfers between devices, on_device(): lax.all_gather(own_left.reshape(half, width * side), 'row', axis=0, tiled...  40.9 us
    all_to_all x2, blocking collectives, on_device(): lax.all_to_all(sums.reshape(4, 4 * blocks, half, side), 'col', 0, 0, axis...  37.6 us
    pallas_call x2, Pallas kernels, contract(): pl.pallas_call(contract_kernel, out_shape=jax.ShapeDtypeStruct((dests, si...  21.9 us
    all_to_all x2, blocking collectives, on_device(): lax.all_to_all(line.reshape(4, blocks, half, side), 'col', 0, 0, axis_ind...  21.3 us
    ppermute x5, starting transfers between devices, swap(): return lax.ppermute(a, 'col', other_core)  9.78 us
    ppermute x5, waiting for transfers between devices, swap(): return lax.ppermute(a, 'col', other_core)  8.11 us
    reshape x1, local copies, waits for them, and re-layouts, on_device(): right_own = right_env.reshape(nb, side, width * side)  7.4 us
  transfers between devices with their start and end apart: 6, of which 5 were waited for; matrix products, arithmetic and copies ran while one was open for 5% of the time, Pallas kernels for 0%

profile of v1, /device:TPU:1, one launch (start us, length us, event | category | flops | bytes accessed | tf_op | source)
XLA Modules:
  0.0 166.9 jit_solution(18399145610373162215)
XLA Ops:
  6.5 0.0 copy-start
  6.5 0.0 all-gather.2.cloned.1.call-start
  6.5 1.2 copy-done
  7.8 1.0 copy.11
  8.8 0.0 all-gather.2.cloned.1.call-update
  8.9 0.0 copy-start.2
  8.9 0.0 copy-start.6
  8.9 0.0 copy-start.3
  8.9 0.0 copy-start.4
  8.9 0.0 copy-start.1
  8.9 0.0 copy-start.5
  8.9 7.4 %reshape.20.right_own = bf16[4,128,4096]{2,1,0:T(8,128)(2,1)} reshape(bf16[4,128,32,128]{3,2,1,0:T(8,128)(2,1)} %param.9) | data formatting | bytes 8388608 | tf_op jit(solution)/shard_map/reshape | solution.py:134
  16.3 3.2 %collective-permute-start.2 = (bf16[4,128,4096]{2,1,0:T(8,128)(2,1)}, bf16[4,128,4096]{2,1,0:T(8,128)(2,1)}, u32[]{:S(2)}, u32[]{:S(2)}) collective-permute-start(bf16[4,128,4096]{2,1,0:T(8,128)(2,1)} %reshape.20.right_own), channel_id=1, source_target_pairs={{0,1},{1,0},{2,3},{3,2},{4,5},{5,4},{6,7},{7,6},{8,9},{9,8},{10,11... | collective-permute-start | bytes 12582920 | tf_op jit(solution)/shard_map/ppermute | solution.py:117
  19.6 0.0 copy-done.2
  19.6 0.0 copy-done.6
  19.6 0.0 copy-done.3
  19.6 0.0 copy-done.4
  19.7 0.1 collective-permute-start.1
  19.8 0.0 copy-done.1
  19.8 0.5 collective-permute-start
  20.3 0.1 pad.4.clone
  20.3 5.9 %collective-permute-done.1 = s32[4,32]{1,0:T(4,128)S(1)} collective-permute-done((s32[4,32]{1,0:T(4,128)S(1)}, s32[4,32]{1,0:T(4,128)S(1)}, u32[]{:S(2)}, u32[]{:S(2)}) %collective-permute-start.1) | collective-permute-done | bytes 544 | tf_op jit(solution)/shard_map/ppermute | solution.py:117
  26.2 0.0 copy-done.5
  26.2 0.1 broadcast_add_fusion
  26.3 0.1 pad_add_fusion.1
  26.4 0.1 add_add_fusion.pairs
  26.5 0.0 collective-permute-done
  26.5 0.1 broadcast_select_fusion.2
  26.6 0.3 collective-permute-done.2.right_other
  26.9 40.9 %all-gather.2.cloned.1.call-done.left = bf16[512,4096]{1,0:T(8,128)(2,1)} async-done(((bf16[64,4096]{1,0:T(8,128)(2,1)}), bf16[512,4096]{1,0:T(8,128)(2,1)}) %all-gather.2.cloned.1.call-update) | async-done | bytes 4194320 | tf_op jit(solution)/shard_map/all_gather | solution.py:120
  67.8 11.0 %contract.2 = bf16[128,64,128]{2,1,0:T(8,128)(2,1)S(1)} custom-call(s32[4,64]{1,0:T(4,128)S(1)} %add_add_fusion.pairs, bf16[8,64,128]{2,1,0:T(8,128)(2,1)S(1)} %get-tuple-element.10.own_rows, bf16[8,64,128]{2,1,0:T(8,128)(2,1)S(1)} %get-tuple-element.9.other_rows, bf16[4,128,4096]{2,1,0:T(8,128)(2,1)} %reshape.20.right_own, ...), custom_call_target="tpu_custom_call" | custom-call | flops 5368709120 | bytes 14680064 | tf_op jit(solution)/shard_map/contract/pallas_call | solution.py:88
  78.8 19.4 %all_to_all.20 = bf16[4,32,64,128]{3,2,1,0:T(8,128)(2,1)S(1)} all-to-all(bf16[4,32,64,128]{3,2,1,0:T(8,128)(2,1)S(1)} %bitcast.19), channel_id=1, replica_groups={{0,2,4,6},{8,10,12,14},{16,18,20,22},{24,26,28,30},{1,9,17,25},{3,11,19..., dimensions={0} | all-to-all | bytes 4194304 | tf_op jit(solution)/shard_map/all_to_all | solution.py:144
  98.2 1.3 reduce_sum.42
  99.6 10.6 %all_to_all.21 = bf16[4,8,64,128]{3,2,1,0:T(8,128)(2,1)S(1)} all-to-all(bf16[4,8,64,128]{3,2,1,0:T(8,128)(2,1)} %bitcast.23), channel_id=1, replica_groups={{0,8,16,24},{2,10,18,26},{4,12,20,28},{6,14,22,30},{1,3,5,7},{9,11,13,1..., dimensions={0} | all-to-all | bytes 1048576 | tf_op jit(solution)/shard_map/all_to_all | solution.py:149
  110.2 0.1 convert_reduce_fusion.1
  110.3 3.8 %collective-permute-start.3 = (bf16[8,64,128]{2,1,0:T(8,128)(2,1)S(1)}, bf16[8,64,128]{2,1,0:T(8,128)(2,1)S(1)}, u32[]{:S(2)}, u32[]{:S(2)}) collective-permute-start(bf16[8,64,128]{2,1,0:T(8,128)(2,1)S(1)} %subtract_convert_fusion.1.own_rows), channel_id=1, source_target_pairs={{0,1},{1,0},{2,3},{3,2},{4,5},{5,4},{6,7},{7,6},{8,9},{9,8},{10,11... | collective-permute-start | bytes 393224 | tf_op jit(solution)/shard_map/ppermute | solution.py:117
  114.1 1.0 collective-permute-done.3.other_rows
  115.1 11.0 %contract.3 = bf16[128,64,128]{2,1,0:T(8,128)(2,1)S(1)} custom-call(s32[4,64]{1,0:T(4,128)S(1)} %add_add_fusion.pairs, bf16[8,64,128]{2,1,0:T(8,128)(2,1)S(1)} %subtract_convert_fusion.1.own_rows, bf16[8,64,128]{2,1,0:T(8,128)(2,1)S(1)} %collective-permute-done.3.other_rows, bf16[4,128,4096]{2,1,0:T(8,128)(2,1)} %reshape.20.right_own, ...), custom_call_target="tpu_custom_call" | custom-call | flops 5368709120 | bytes 14680064 | tf_op jit(solution)/shard_map/contract/pallas_call | solution.py:88
  126.1 18.1 %all_to_all.22 = bf16[4,32,64,128]{3,2,1,0:T(8,128)(2,1)S(1)} all-to-all(bf16[4,32,64,128]{3,2,1,0:T(8,128)(2,1)S(1)} %bitcast.18), channel_id=1, replica_groups={{0,2,4,6},{8,10,12,14},{16,18,20,22},{24,26,28,30},{1,9,17,25},{3,11,19..., dimensions={0} | all-to-all | bytes 4194304 | tf_op jit(solution)/shard_map/all_to_all | solution.py:144
  144.2 1.3 reduce_sum.44
  145.5 10.7 %all_to_all.23 = bf16[4,8,64,128]{3,2,1,0:T(8,128)(2,1)S(1)} all-to-all(bf16[4,8,64,128]{3,2,1,0:T(8,128)(2,1)} %bitcast.22), channel_id=1, replica_groups={{0,8,16,24},{2,10,18,26},{4,12,20,28},{6,14,22,30},{1,3,5,7},{9,11,13,1..., dimensions={0} | all-to-all | bytes 1048576 | tf_op jit(solution)/shard_map/all_to_all | solution.py:149
  156.2 0.1 convert_reduce_fusion
  156.3 2.2 %collective-permute-start.4 = (bf16[4,64,128]{2,1,0:T(8,128)(2,1)S(1)}, bf16[4,64,128]{2,1,0:T(8,128)(2,1)S(1)}, u32[]{:S(2)}, u32[]{:S(2)}) collective-permute-start(bf16[4,64,128]{2,1,0:T(8,128)(2,1)S(1)} %broadcast_select_fusion.6), channel_id=1, source_target_pairs={{0,1},{1,0},{2,3},{3,2},{4,5},{5,4},{6,7},{7,6},{8,9},{9,8},{10,11... | collective-permute-start | bytes 196616 | tf_op jit(solution)/shard_map/ppermute | solution.py:117
  158.5 0.9 collective-permute-done.4
  159.4 0.7 pad_maximum_fusion.1
  (11 shorter events, 0.2 us)
Async XLA Ops:
  6.5 1.2 copy-start
  6.5 61.3 %all-gather.2.cloned.1.call-start = ((), (), s32[]{:S(2)}) async-start(), calls=%async_computation.4 | async-start | bytes 4718592 | tf_op jit(solution)/shard_map/all_gather | solution.py:120
  8.9 10.7 %copy-start.2 = (s32[32]{0:T(128)S(1)}, s32[32]{0:T(128)}, u32[]{:S(2)}) copy-start(s32[32]{0:T(128)} %param.14) | copy-start | bytes 388
  8.9 10.7 %copy-start.6 = (s32[32]{0:T(128)S(1)}, s32[32]{0:T(128)}, u32[]{:S(2)}) copy-start(s32[32]{0:T(128)} %param.13) | copy-start | bytes 388
  8.9 10.7 %copy-start.3 = (s32[32]{0:T(128)S(1)}, s32[32]{0:T(128)}, u32[]{:S(2)}) copy-start(s32[32]{0:T(128)} %param.12) | copy-start | bytes 388
  8.9 10.7 %copy-start.4 = (s32[32]{0:T(128)S(1)}, s32[32]{0:T(128)}, u32[]{:S(2)}) copy-start(s32[32]{0:T(128)} %param.11) | copy-start | bytes 388
  8.9 10.9 %copy-start.1 = (bf16[4,128,128]{2,1,0:T(8,128)(2,1)S(1)}, bf16[4,128,128]{2,1,0:T(8,128)(2,1)}, u32[]{:S(2)}) copy-start(bf16[4,128,128]{2,1,0:T(8,128)(2,1)} %param.8) | copy-start | bytes 393220
  8.9 17.3 %copy-start.5 = (s32[4]{0:T(128)S(1)}, s32[4]{0:T(128)}, u32[]{:S(2)}) copy-start(s32[4]{0:T(128)} %constant.89) | copy-start | bytes 52
  16.3 10.6 %collective-permute-start.2 = (bf16[4,128,4096]{2,1,0:T(8,128)(2,1)}, bf16[4,128,4096]{2,1,0:T(8,128)(2,1)}, u32[]{:S(2)}, u32[]{:S(2)}) collective-permute-start(bf16[4,128,4096]{2,1,0:T(8,128)(2,1)} %reshape.20.right_own), channel_id=1, source_target_pairs={{0,1},{1,0},{2,3},{3,2},{4,5},{5,4},{6,7},{7,6},{8,9},{9,8},{10,11... | collective-permute-start | bytes 12582920 | tf_op jit(solution)/shard_map/ppermute | solution.py:117
  19.7 6.6 %collective-permute-start.1 = (s32[4,32]{1,0:T(4,128)S(1)}, s32[4,32]{1,0:T(4,128)S(1)}, u32[]{:S(2)}, u32[]{:S(2)}) collective-permute-start(s32[4,32]{1,0:T(4,128)S(1)} %pad_add_fusion), channel_id=1, source_target_pairs={{0,1},{1,0},{2,3},{3,2},{4,5},{5,4},{6,7},{7,6},{8,9},{9,8},{10,11... | collective-permute-start | bytes 1544 | tf_op jit(solution)/shard_map/ppermute | solution.py:117
  19.8 6.7 %collective-permute-start = (bf16[4,128,128]{2,1,0:T(8,128)(2,1)S(1)}, bf16[4,128,128]{2,1,0:T(8,128)(2,1)S(1)}, u32[]{:S(2)}, u32[]{:S(2)}) collective-permute-start(bf16[4,128,128]{2,1,0:T(8,128)(2,1)S(1)} %copy-done.1), channel_id=1, source_target_pairs={{0,1},{1,0},{2,3},{3,2},{4,5},{5,4},{6,7},{7,6},{8,9},{9,8},{10,11... | collective-permute-start | bytes 393224 | tf_op jit(solution)/shard_map/ppermute | solution.py:117
  110.3 4.8 %collective-permute-start.3 = (bf16[8,64,128]{2,1,0:T(8,128)(2,1)S(1)}, bf16[8,64,128]{2,1,0:T(8,128)(2,1)S(1)}, u32[]{:S(2)}, u32[]{:S(2)}) collective-permute-start(bf16[8,64,128]{2,1,0:T(8,128)(2,1)S(1)} %subtract_convert_fusion.1.own_rows), channel_id=1, source_target_pairs={{0,1},{1,0},{2,3},{3,2},{4,5},{5,4},{6,7},{7,6},{8,9},{9,8},{10,11... | collective-permute-start | bytes 393224 | tf_op jit(solution)/shard_map/ppermute | solution.py:117
  156.3 3.1 %collective-permute-start.4 = (bf16[4,64,128]{2,1,0:T(8,128)(2,1)S(1)}, bf16[4,64,128]{2,1,0:T(8,128)(2,1)S(1)}, u32[]{:S(2)}, u32[]{:S(2)}) collective-permute-start(bf16[4,64,128]{2,1,0:T(8,128)(2,1)S(1)} %broadcast_select_fusion.6), channel_id=1, source_target_pairs={{0,1},{1,0},{2,3},{3,2},{4,5},{5,4},{6,7},{7,6},{8,9},{9,8},{10,11... | collective-permute-start | bytes 196616 | tf_op jit(solution)/shard_map/ppermute | solution.py:117
Sparse Core Ops, SparseCore 0:
  9.1 58.6 all-gather.1

commit v2 on v0

v2 whole, which is shorter than its diff:
```python
import jax
import jax.numpy as jnp
from jax import lax
from jax.experimental import pallas as pl
from jax.experimental.pallas import tpu as pltpu
from jax.sharding import PartitionSpec as P

step_size = 0.3
NZ, NY, NX = 8, 4, 4
axes = ("row", "col")

far = (2, -2, 3, -3, 4)
thirds = 3
third_w = 11
near = 3


def device(z, y, x, c):
    return ((z % NZ * NY + y % NY) * NX + x % NX) * 2 + c


def permutation(to):
    return [
        (device(z, y, x, c), device(*to(z, y, x, c)))
        for z in range(NZ) for y in range(NY) for x in range(NX) for c in range(2)
    ]


swap_cores = permutation(lambda z, y, x, c: (z, y, x, 1 - c))


def first(d):
    return permutation(lambda z, y, x, c: (z, y, x + d, c) if c == 0 else (z, y + d, x, c))


def second(d):
    return permutation(lambda z, y, x, c: (z, y + d, x, c) if c == 0 else (z, y, x + d, c))


def along_z(d):
    return permutation(lambda z, y, x, c: (z + d, y, x, c))


def fetch_place(z, y, x, c):
    group = min((y * NX + x) // thirds, len(far) - 1)
    d = far[group] if c == 0 else -far[group]
    return z - d, y, x, c


fetch_far = permutation(fetch_place)
shifts = (1, 2, -1)


def send(a, perm):
    return lax.ppermute(a, axes, perm)


def table(values, index):
    out = jnp.full_like(index, values[0])
    for k, v in enumerate(values[1:], 1):
        out = jnp.where(index == k, v, out)
    return out


vmem = pl.BlockSpec(memory_space=pltpu.VMEM)
smem = pl.BlockSpec(memory_space=pltpu.SMEM)


def params(mib):
    return pltpu.CompilerParams(vmem_limit_bytes=mib * 1024 * 1024)


def multiply_state(core, own_rows, other_rows, right_own, right_other, state, product):
    nb, side, wide = right_own.shape
    half = side // 2
    mine = pl.multiple_of(core * half, half)
    theirs = pl.multiple_of((1 - core) * half, half)
    state[:, pl.ds(mine, half), :] = own_rows[...]
    state[:, pl.ds(theirs, half), :] = other_rows[...]
    step = 512
    for b in range(2 * nb):
        at = core * nb + b if b < nb else (1 - core) * nb + b - nb
        right = right_own.at[b] if b < nb else right_other.at[b - nb]
        s = state[at]
        for n in range(wide // step):
            r = jnp.dot(
                s, right[:, n * step:(n + 1) * step], preferred_element_type=jnp.float32
            ).astype(jnp.bfloat16)
            for q in range(step // side):
                w = n * (step // side) + q
                product[w * side:(w + 1) * side, b * side:(b + 1) * side] = r[
                    :, q * side:(q + 1) * side
                ]


def multiply_left(pairs, left, product, partial, total, outs):
    half, side = total.shape[1:]
    wide = product.shape[0]
    rows = partial.shape[1]
    total[...] = jnp.zeros_like(total)
    for n in range(partial.shape[0] // 2):
        r = jnp.dot(
            left[:rows, :wide], product[:, n * 2 * side:(n + 1) * 2 * side],
            preferred_element_type=jnp.float32,
        ).astype(jnp.bfloat16)
        partial[2 * n] = r[:, :side]
        partial[2 * n + 1] = r[:, side:]

    def place(p, carry):
        at = pl.multiple_of(pairs[0, p] * half, half)
        to = pairs[2, p]
        value = partial[pairs[1, p], pl.ds(at, half), :].astype(jnp.float32)
        total[to] = (total[to].astype(jnp.float32) + value).astype(jnp.bfloat16)
        return carry

    lax.fori_loop(0, pairs.shape[1], place, 0, unroll=4)
    count = outs[0].shape[0]
    for i, out in enumerate(outs):
        out[...] = total[i * count:(i + 1) * count]


def product_kernel(pairs, own_rows, other_rows, right_own, right_other, product, state):
    multiply_state(pairs[3, 0], own_rows, other_rows, right_own, right_other, state, product)


def first_kernel(
    pairs, places, own, below, above, part0, part1, part2, part3, product,
    out0, out1, out2, out3, left, partial, total, sems, near_sems,
):
    half = own.shape[0]
    copies = []
    for i, ref in enumerate((own, below, above)):
        copies.append(
            pltpu.make_async_copy(
                ref, left.at[i * half:(i + 1) * half, 0:own.shape[1]], near_sems.at[i]
            )
        )
    for i, ref in enumerate((part0, part1, part2, part3)):
        for j in range(4):
            row = pl.multiple_of(places[0, i * 4 + j], half)
            column = pl.multiple_of(places[1, i * 4 + j], 128)
            copies.append(
                pltpu.make_async_copy(
                    ref.at[j], left.at[pl.ds(row, half), pl.ds(column, ref.shape[2])],
                    sems.at[i * 4 + j],
                )
            )
    for c in copies:
        c.start()
    for c in copies:
        c.wait()
    multiply_left(pairs, left, product, partial, total, (out0, out1, out2, out3))


def second_kernel(
    pairs, own_rows, other_rows, right_own, right_other, left,
    out0, out1, out2, out3, state, product, partial, total,
):
    multiply_state(pairs[3, 0], own_rows, other_rows, right_own, right_other, state, product)
    multiply_left(pairs, left, product, partial, total, (out0, out1, out2, out3))


def on_device(psi, right_env, left_env, env_index, source_block, target_slot, target_block):
    nb, side, width, _ = right_env.shape
    half = side // 2
    blocks = 2 * nb
    envs = NZ
    wide = width * side
    third = third_w * side
    bf16, f32 = jnp.bfloat16, jnp.float32
    z = lax.axis_index("row")
    col = lax.axis_index("col")
    core, x, y = col % 2, col // 2 % NX, col // (2 * NX)
    lower = core == 0
    chip = y * NX + x

    own = lax.dynamic_slice_in_dim(left_env[0], core * half, half, 0).reshape(half, wide)
    padded = jnp.pad(own, ((0, 0), (0, thirds * third - wide)))
    mine = lax.dynamic_slice_in_dim(padded, chip % thirds * third, third, 1)
    held = send(mine, fetch_far)
    env_index, target_slot, right_env, _ = lax.optimization_barrier(
        (env_index, target_slot, right_env, mine)
    )
    offset = (env_index - z) % envs
    slot_lower = table([0, 2, 3, 5, 7, 6, 4, 1], offset)
    slot_upper = table([0, 2, 4, 6, 7, 5, 3, 1], offset)
    owner = target_slot // 2
    to_y, to_x, to_c = owner // (2 * NX), owner // 2 % NX, owner % 2
    ry, rx = (to_y - y) % NY, (to_x - x) % NX
    block = to_c * nb + target_block
    x_first = (rx * 4 + ry) * blocks + block
    y_first = (ry * 4 + rx) * blocks + block
    lists = jnp.stack([slot_lower, slot_upper, source_block, x_first, y_first])
    right_own = right_env.reshape(nb, side, wide)
    psi_other = send(psi, swap_cores)
    their_lists = send(lists, swap_cores)
    held, own, right_own, psi_other, their_lists = lax.optimization_barrier(
        (held, own, right_own, psi_other, their_lists)
    )
    right_other = send(right_own, swap_cores)
    below = send(own, along_z(1))
    above = send(own, along_z(-1))
    line = jnp.stack([held] + [send(held, first(d)) for d in shifts])
    line, right_other = lax.optimization_barrier((line, right_other))
    last_line, below, above = lax.optimization_barrier((line, below, above))
    parts = [line] + [send(last_line if d < 0 else line, second(d)) for d in shifts]

    back = jnp.array([0, -1, -2, 1], jnp.int32)
    by_first, by_second = back[None, :], back[:, None]
    px = (x + jnp.where(lower, by_first, by_second)) % NX
    py = (y + jnp.where(lower, by_second, by_first)) % NY
    at = (py * NX + px).reshape(-1)
    places = jnp.stack([(near + at // thirds) * half, at % thirds * third])

    theirs = their_lists + jnp.array([[0], [0], [nb], [0], [0]], jnp.int32)
    both = jnp.concatenate([lists, theirs], axis=1)
    pairs = jnp.stack([
        jnp.where(lower, both[0], both[1]), both[2],
        jnp.where(lower, both[3], both[4]), jnp.broadcast_to(core, both[2].shape),
    ])

    state = jnp.concatenate(
        [jnp.where(lower, psi, psi_other), jnp.where(lower, psi_other, psi)], axis=0
    )
    own_rows = jnp.where(lower, state[:, :half], state[:, half:])
    other_rows = jnp.where(lower, state[:, half:], state[:, :half])

    pair_count = pairs.shape[1]
    left_shape = ((envs + 1) * half, thirds * third)
    sums_shape = [jax.ShapeDtypeStruct((4 * blocks, half, side), bf16)] * 4
    state_scratch = pltpu.VMEM((blocks, side, side), bf16)
    product_scratch = pltpu.VMEM((wide, blocks * side), bf16)
    left_scratch = [
        pltpu.VMEM((blocks, envs * half, side), bf16),
        pltpu.VMEM((16 * blocks, half, side), bf16),
    ]
    state_flops = 2 * blocks * side * side * wide
    left_flops = 2 * envs * half * wide * blocks * side

    product = pl.pallas_call(
        product_kernel,
        out_shape=jax.ShapeDtypeStruct((wide, blocks * side), bf16),
        in_specs=[smem] + [vmem] * 4,
        out_specs=vmem,
        scratch_shapes=[state_scratch],
        compiler_params=params(8),
        cost_estimate=pl.CostEstimate(flops=state_flops, bytes_accessed=0, transcendentals=0),
        name="product",
    )(pairs, own_rows, other_rows, right_own, right_other)

    for step in range(2):
        if step == 0:
            *sums, left = pl.pallas_call(
                first_kernel,
                out_shape=sums_shape + [jax.ShapeDtypeStruct(left_shape, bf16)],
                in_specs=[smem] * 2 + [vmem] * 8,
                out_specs=[vmem] * 5,
                scratch_shapes=left_scratch + [
                    pltpu.SemaphoreType.DMA((16,)), pltpu.SemaphoreType.DMA((near,))
                ],
                compiler_params=params(12),
                cost_estimate=pl.CostEstimate(
                    flops=left_flops, bytes_accessed=0, transcendentals=0
                ),
                name="contract_first",
            )(pairs, places, own, below, above, *parts, product)
        else:
            sums = pl.pallas_call(
                second_kernel,
                out_shape=sums_shape,
                in_specs=[smem] + [vmem] * 5,
                out_specs=[vmem] * 4,
                scratch_shapes=[state_scratch, product_scratch] + left_scratch,
                compiler_params=params(24),
                cost_estimate=pl.CostEstimate(
                    flops=left_flops + state_flops, bytes_accessed=0, transcendentals=0
                ),
                name="contract_second",
            )(pairs, own_rows, other_rows, right_own, right_other, left)
        got = [send(sums[k + 1], first(d)) for k, d in enumerate(shifts)]
        summed = sums[0].astype(f32)
        for g in got:
            summed = summed + g.astype(f32)
        summed = summed.astype(bf16).reshape(4, blocks, half, side)
        got = [send(summed[k + 1], second(d)) for k, d in enumerate(shifts)]
        gradient = summed[0].astype(f32)
        for g in got:
            gradient = gradient + g.astype(f32)
        own_rows = (own_rows.astype(f32) - step_size * gradient).astype(bf16)
        if step == 0:
            other_rows = send(own_rows, swap_cores)
    keep = jnp.where(lower, own_rows[:nb], own_rows[nb:])
    give = jnp.where(lower, own_rows[nb:], own_rows[:nb])
    come = send(give, swap_cores)
    return jnp.concatenate(
        [jnp.where(lower, keep, come), jnp.where(lower, come, keep)], axis=1
    )


def solution(mesh):
    placed = (
        P(("row", "col"), None, None),
        P(("row", "col"), None, None, None),
        P("row", None, None, None),
        P(("row", "col")),
        P(("row", "col")),
        P(("row", "col")),
        P(("row", "col")),
    )
    return jax.shard_map(
        on_device,
        mesh=mesh,
        in_specs=placed,
        out_specs=P(("row", "col"), None, None),
        check_vma=False,
    )
```

time: 224 us -> 132 us (0.59)
  waiting for transfers between devices: 102 us -> 54.3 us
  blocking collectives: 33.6 us -> 0 us
  matrix products: 25 us -> 0 us
  starting transfers between devices: 16.1 us -> 40.9 us
  Pallas kernels: 0 us -> 22.3 us
  local copies, waits for them, and re-layouts: 30.3 us -> 10.7 us
  between operations: 13.6 us -> 0.23 us
    all_gather x1 -> x0, waiting for transfers between devices: 74.8 us -> none  [on_device(): gathered = lax.all_gather(left_env, 'row', axis=0, tiled=True)]
    ppermute x0 -> x26, waiting for transfers between devices: none -> 54.3 us  [send(): return lax.ppermute(a, axes, perm)]
    ppermute x0 -> x26, starting transfers between devices: none -> 40.9 us  [send(): return lax.ppermute(a, axes, perm)]
    all_to_all x1 -> x0, blocking collectives: 33.6 us -> none  [on_device(): lax.all_to_all(outbound_blocks, 'col', split_axis=0, concat_axis=0, tiled...]
    all_to_all x2 -> x0, waiting for transfers between devices: 26.5 us -> none  [the longest x1 26.5 us: on_device(): lax.all_to_all(outbound_blocks, 'col', split_axis=0, concat_axis=0, tiled...]
    dot_general x9 -> x0, matrix products: 25 us -> none  [the longest x2 13.7 us: on_device(): jnp.einsum('eawk,bkwj->ebaj', gathered, product, preferred_element_type=j...]
    pallas_call x0 -> x3, Pallas kernels: none -> 22.3 us  [the longest x1 10.4 us: on_device(): pl.pallas_call(second_kernel, out_shape=sums_shape, in_specs=[smem] + [vm...]
    all_to_all x2 -> x0, starting transfers between devices: 16.1 us -> none  [the longest x1 8.59 us: on_device(): lax.all_to_all(send_index, 'col', split_axis=0, concat_axis=0, tiled=True)]
  transfers between devices with their start and end apart: 3 -> 26, of which waited for: 2 -> 16; matrix products, arithmetic and copies ran while one was open for 19% -> 8% of each run, Pallas kernels for 0% -> 4%
where the time goes in v2:
time: 132 us
  waiting for transfers between devices  54.3 us (41%)
  starting transfers between devices  40.9 us (31%)
  Pallas kernels  22.3 us (17%)
  local copies, waits for them, and re-layouts  10.7 us (8%)
  other arithmetic  3.51 us (3%)
    ppermute x26, waiting for transfers between devices, send(): return lax.ppermute(a, axes, perm)  54.3 us
    ppermute x26, starting transfers between devices, send(): return lax.ppermute(a, axes, perm)  40.9 us
    pallas_call x1, Pallas kernels, on_device(): pl.pallas_call(second_kernel, out_shape=sums_shape, in_specs=[smem] + [vm...  10.4 us
    reshape x1, local copies, waits for them, and re-layouts, on_device(): right_own = right_env.reshape(nb, side, wide)  7.29 us
    pallas_call x1, Pallas kernels, on_device(): pl.pallas_call(first_kernel, out_shape=sums_shape + [jax.ShapeDtypeStruct...  6.87 us
    pallas_call x1, Pallas kernels, on_device(): pl.pallas_call(product_kernel, out_shape=jax.ShapeDtypeStruct((wide, bloc...  5 us
  transfers between devices with their start and end apart: 26, of which 16 were waited for; matrix products, arithmetic and copies ran while one was open for 8% of the time, Pallas kernels for 4%

profile of v2, /device:TPU:1, one launch (start us, length us, event | category | flops | bytes accessed | tf_op | source)
XLA Modules:
  0.0 132.0 jit_solution(59608109111927047)
XLA Ops:
  0.0 3.2 %collective-permute-start.1 = (bf16[4,128,128]{2,1,0:T(8,128)(2,1)}, bf16[4,128,128]{2,1,0:T(8,128)(2,1)S(1)}, u32[]{:S(2)}, u32[]{:S(2)}) collective-permute-start(bf16[4,128,128]{2,1,0:T(8,128)(2,1)} %param.9), channel_id=1, source_target_pairs={{0,1},{1,0},{2,3},{3,2},{4,5},{5,4},{6,7},{7,6},{8,9},{9,8},{10,11... | collective-permute-start | bytes 393224 | tf_op jit(solution)/shard_map/ppermute | solution.py:55
  3.3 0.2 copy.12
  3.5 1.9 %collective-permute-start = (bf16[64,1408]{1,0:T(8,128)(2,1)S(1)}, bf16[64,1408]{1,0:T(8,128)(2,1)S(1)}, u32[]{:S(2)}, u32[]{:S(2)}) collective-permute-start(bf16[64,1408]{1,0:T(8,128)(2,1)S(1)} %pad_dynamic-slice_fusion), channel_id=1, source_target_pairs={{0,192},{1,65},{2,194},{3,67},{4,196},{5,69},{6,70},{7,199},{8,72}... | collective-permute-start | bytes 540680 | tf_op jit(solution)/shard_map/ppermute | solution.py:55
  5.4 0.7 fusion.3
  6.1 0.7 add_bitcast_fusion
  6.8 0.7 stack.48
  7.5 0.0 copy-start.3
  7.5 0.0 copy-start.5
  7.5 4.1 %collective-permute-start.2 = (s32[5,32]{1,0:T(8,128)S(1)}, s32[5,32]{1,0:T(8,128)S(1)}, u32[]{:S(2)}, u32[]{:S(2)}) collective-permute-start(s32[5,32]{1,0:T(8,128)S(1)} %stack.48), channel_id=1, source_target_pairs={{0,1},{1,0},{2,3},{3,2},{4,5},{5,4},{6,7},{7,6},{8,9},{9,8},{10,11... | collective-permute-start | bytes 1928 | tf_op jit(solution)/shard_map/ppermute | solution.py:55
  11.6 7.3 %reshape.215.right_own = bf16[4,128,4096]{2,1,0:T(8,128)(2,1)} reshape(bf16[4,128,32,128]{3,2,1,0:T(8,128)(2,1)} %param.10) | data formatting | bytes 8388608 | tf_op jit(solution)/shard_map/reshape | solution.py:194
  18.9 0.1 collective-permute-start.6
  19.0 0.1 pad.16.clone
  19.1 0.1 select_add_fusion.1
  19.2 0.1 add.252
  19.2 0.1 add.256
  19.4 3.7 %collective-permute-start.5 = (bf16[64,1408]{1,0:T(8,128)(2,1)S(1)}, bf16[64,1408]{1,0:T(8,128)(2,1)S(1)}, u32[]{:S(2)}, u32[]{:S(2)}) collective-permute-start(bf16[64,1408]{1,0:T(8,128)(2,1)S(1)} %collective-permute-done), channel_id=1, source_target_pairs={{0,6},{1,25},{2,0},{3,27},{4,2},{5,29},{6,4},{7,31},{8,14},{9,1},{... | collective-permute-start | bytes 540680 | tf_op jit(solution)/shard_map/ppermute | solution.py:55
  23.1 1.8 %collective-permute-start.8 = (bf16[64,4096]{1,0:T(8,128)(2,1)S(1)}, bf16[64,4096]{1,0:T(8,128)(2,1)S(1)}, u32[]{:S(2)}, u32[]{:S(2)}) collective-permute-start(bf16[64,4096]{1,0:T(8,128)(2,1)S(1)} %bitcast.22), channel_id=1, source_target_pairs={{0,224},{1,225},{2,226},{3,227},{4,228},{5,229},{6,230},{7,231},{8... | collective-permute-start | bytes 1572872 | tf_op jit(solution)/shard_map/ppermute | solution.py:55
  24.9 2.5 %collective-permute-done.5 = bf16[64,1408]{1,0:T(8,128)(2,1)S(1)} collective-permute-done((bf16[64,1408]{1,0:T(8,128)(2,1)S(1)}, bf16[64,1408]{1,0:T(8,128)(2,1)S(1)}, u32[]{:S(2)}, u32[]{:S(2)}) %collective-permute-start.5) | collective-permute-done | bytes 180256 | tf_op jit(solution)/shard_map/ppermute | solution.py:55
  27.5 0.1 broadcast_add_fusion
  27.5 1.4 %collective-permute-done.4 = bf16[64,1408]{1,0:T(8,128)(2,1)S(1)} collective-permute-done((bf16[64,1408]{1,0:T(8,128)(2,1)S(1)}, bf16[64,1408]{1,0:T(8,128)(2,1)S(1)}, u32[]{:S(2)}, u32[]{:S(2)}) %collective-permute-start.4) | collective-permute-done | bytes 180256 | tf_op jit(solution)/shard_map/ppermute | solution.py:55
  28.9 4.8 %collective-permute-done.3 = bf16[64,1408]{1,0:T(8,128)(2,1)S(1)} collective-permute-done((bf16[64,1408]{1,0:T(8,128)(2,1)S(1)}, bf16[64,1408]{1,0:T(8,128)(2,1)S(1)}, u32[]{:S(2)}, u32[]{:S(2)}) %collective-permute-start.3) | collective-permute-done | bytes 180256 | tf_op jit(solution)/shard_map/ppermute | solution.py:55
  33.7 0.1 pad_maximum_fusion.part0
  33.9 3.0 %collective-permute-start.10 = (bf16[4,64,1408]{2,1,0:T(8,128)(2,1)S(1)}, bf16[4,64,1408]{2,1,0:T(8,128)(2,1)S(1)}, u32[]{:S(2)}, u32[]{:S(2)}) collective-permute-start(bf16[4,64,1408]{2,1,0:T(8,128)(2,1)S(1)} %pad_maximum_fusion.part0), channel_id=1, source_target_pairs={{0,16},{1,5},{2,18},{3,7},{4,20},{5,1},{6,22},{7,3},{8,24},{9,13},... | collective-permute-start | bytes 2162696 | tf_op jit(solution)/shard_map/ppermute | solution.py:55
  36.8 0.5 collective-permute-start.9
  37.3 2.6 %collective-permute-done.7.below = bf16[64,4096]{1,0:T(8,128)(2,1)S(1)} collective-permute-done((bf16[64,4096]{1,0:T(8,128)(2,1)S(1)}, bf16[64,4096]{1,0:T(8,128)(2,1)S(1)}, u32[]{:S(2)}, u32[]{:S(2)}) %collective-permute-start.7) | collective-permute-done | bytes 524320 | tf_op jit(solution)/shard_map/ppermute | solution.py:55
  39.9 1.0 collective-permute-start.11
  41.0 0.1 pad_add_fusion
  41.1 0.1 broadcast_select_fusion.2
  41.1 0.1 add_add_fusion.pairs
  41.2 2.2 %copy-done.1 = bf16[4,128,4096]{2,1,0:T(8,128)(2,1)S(1)} copy-done((bf16[4,128,4096]{2,1,0:T(8,128)(2,1)S(1)}, bf16[4,128,4096]{2,1,0:T(8,128)(2,1)}, u32[]{:S(2)}) %copy-start.1) | copy-done | bytes 4194328
  43.4 5.0 %product.1 = bf16[4096,1024]{1,0:T(8,128)(2,1)S(1)} custom-call(s32[4,64]{1,0:T(4,128)S(1)} %add_add_fusion.pairs, bf16[8,64,128]{2,1,0:T(8,128)(2,1)S(1)} %get-tuple-element.64.own_rows, bf16[8,64,128]{2,1,0:T(8,128)(2,1)S(1)} %get-tuple-element.63.other_rows, bf16[4,128,4096]{2,1,0:T(8,128)(2,1)S(1)} %copy-done.1, ...), custom_call_target="tpu_custom_call" | custom-call | flops 1073741824 | tf_op jit(solution)/shard_map/product/pallas_call | solution.py:240
  48.4 5.6 %collective-permute-done.11.part3 = bf16[4,64,1408]{2,1,0:T(8,128)(2,1)S(1)} collective-permute-done((bf16[4,64,1408]{2,1,0:T(8,128)(2,1)S(1)}, bf16[4,64,1408]{2,1,0:T(8,128)(2,1)S(1)}, u32[]{:S(2)}, u32[]{:S(2)}) %collective-permute-start.11) | collective-permute-done | bytes 720928 | tf_op jit(solution)/shard_map/ppermute | solution.py:55
  54.1 6.9 %contract_first.1 = (bf16[32,64,128]{2,1,0:T(8,128)(2,1)S(1)}, bf16[32,64,128]{2,1,0:T(8,128)(2,1)S(1)}, bf16[32,64,128]{2,1,0:T(8,128)(2,1)S(1)}, bf16[32,64,128]{2,1,0:T(8,128)(2,1)S(1)}, bf16[576,4224]{1,0:T(8,128)(2,1)S(1)}) custom-call(s32[4,64]{1,0:T(4,128)S(1)} %add_add_fusion.pairs, s32[2,16]{1,0:T(2,128)S(1)} %pad_add_fusion.1.places, ...), custom_call_target="tpu_custom_call" | custom-call | flops 4294967296 | tf_op jit(solution)/shard_map/contract_first/pallas_call | solution.py:253
  60.9 0.1 collective-permute-start.12
  61.0 2.6 %collective-permute-start.13 = (bf16[32,64,128]{2,1,0:T(8,128)(2,1)S(1)}, bf16[32,64,128]{2,1,0:T(8,128)(2,1)S(1)}, u32[]{:S(2)}, u32[]{:S(2)}) collective-permute-start(bf16[32,64,128]{2,1,0:T(8,128)(2,1)S(1)} %get-tuple-element.42), channel_id=1, source_target_pairs={{0,4},{1,17},{2,6},{3,19},{4,0},{5,21},{6,2},{7,23},{8,12},{9,25},... | collective-permute-start | bytes 1572872 | tf_op jit(solution)/shard_map/ppermute | solution.py:55
  63.7 0.0 collective-permute-start.14
  63.7 6.9 %collective-permute-done.12 = bf16[32,64,128]{2,1,0:T(8,128)(2,1)S(1)} collective-permute-done((bf16[32,64,128]{2,1,0:T(8,128)(2,1)S(1)}, bf16[32,64,128]{2,1,0:T(8,128)(2,1)S(1)}, u32[]{:S(2)}, u32[]{:S(2)}) %collective-permute-start.12) | collective-permute-done | bytes 524320 | tf_op jit(solution)/shard_map/ppermute | solution.py:55
  70.6 5.6 %collective-permute-done.13 = bf16[32,64,128]{2,1,0:T(8,128)(2,1)S(1)} collective-permute-done((bf16[32,64,128]{2,1,0:T(8,128)(2,1)S(1)}, bf16[32,64,128]{2,1,0:T(8,128)(2,1)S(1)}, u32[]{:S(2)}, u32[]{:S(2)}) %collective-permute-start.13) | collective-permute-done | bytes 524320 | tf_op jit(solution)/shard_map/ppermute | solution.py:55
  76.1 0.7 collective-permute-done.14
  76.8 0.4 add_convert_fusion.1
  77.2 0.8 collective-permute-start.15
  78.0 2.0 %collective-permute-start.17 = (bf16[8,64,128]{2,1,0:T(8,128)(2,1)S(1)}, bf16[8,64,128]{2,1,0:T(8,128)(2,1)S(1)}, u32[]{:S(2)}, u32[]{:S(2)}) collective-permute-start(bf16[8,64,128]{2,1,0:T(8,128)(2,1)S(1)} %get-tuple-element.61), channel_id=1, source_target_pairs={{0,24},{1,7},{2,26},{3,1},{4,28},{5,3},{6,30},{7,5},{8,0},{9,15},{... | collective-permute-start | bytes 393224 | tf_op jit(solution)/shard_map/ppermute | solution.py:55
  79.9 0.6 collective-permute-start.16
  80.5 1.8 %collective-permute-done.15 = bf16[8,64,128]{2,1,0:T(8,128)(2,1)S(1)} collective-permute-done((bf16[8,64,128]{2,1,0:T(8,128)(2,1)S(1)}, bf16[8,64,128]{2,1,0:T(8,128)(2,1)S(1)}, u32[]{:S(2)}, u32[]{:S(2)}) %collective-permute-start.15) | collective-permute-done | bytes 131104 | tf_op jit(solution)/shard_map/ppermute | solution.py:55
  82.3 3.0 %collective-permute-done.16 = bf16[8,64,128]{2,1,0:T(8,128)(2,1)S(1)} collective-permute-done((bf16[8,64,128]{2,1,0:T(8,128)(2,1)S(1)}, bf16[8,64,128]{2,1,0:T(8,128)(2,1)S(1)}, u32[]{:S(2)}, u32[]{:S(2)}) %collective-permute-start.16) | collective-permute-done | bytes 131104 | tf_op jit(solution)/shard_map/ppermute | solution.py:55
  85.3 0.1 subtract_convert_fusion.1.own_rows
  85.4 5.9 %collective-permute-start.18 = (bf16[8,64,128]{2,1,0:T(8,128)(2,1)S(1)}, bf16[8,64,128]{2,1,0:T(8,128)(2,1)S(1)}, u32[]{:S(2)}, u32[]{:S(2)}) collective-permute-start(bf16[8,64,128]{2,1,0:T(8,128)(2,1)S(1)} %subtract_convert_fusion.1.own_rows), channel_id=1, source_target_pairs={{0,1},{1,0},{2,3},{3,2},{4,5},{5,4},{6,7},{7,6},{8,9},{9,8},{10,11... | collective-permute-start | bytes 393224 | tf_op jit(solution)/shard_map/ppermute | solution.py:55
  91.3 1.0 collective-permute-done.18.other_rows
  92.3 10.4 %contract_second.1 = (bf16[32,64,128]{2,1,0:T(8,128)(2,1)S(1)}, bf16[32,64,128]{2,1,0:T(8,128)(2,1)S(1)}, bf16[32,64,128]{2,1,0:T(8,128)(2,1)S(1)}, bf16[32,64,128]{2,1,0:T(8,128)(2,1)S(1)}) custom-call(s32[4,64]{1,0:T(4,128)S(1)} %add_add_fusion.pairs, bf16[8,64,128]{2,1,0:T(8,128)(2,1)S(1)} %subtract_convert_fusion.1.own_rows, ...), custom_call_target="tpu_custom_call" | custom-call | flops 5368709120 | tf_op jit(solution)/shard_map/contract_second/pallas_call | solution.py:268
  102.7 0.1 collective-permute-start.19
  102.8 2.3 %collective-permute-start.20 = (bf16[32,64,128]{2,1,0:T(8,128)(2,1)S(1)}, bf16[32,64,128]{2,1,0:T(8,128)(2,1)S(1)}, u32[]{:S(2)}, u32[]{:S(2)}) collective-permute-start(bf16[32,64,128]{2,1,0:T(8,128)(2,1)S(1)} %get-tuple-element.47), channel_id=1, source_target_pairs={{0,4},{1,17},{2,6},{3,19},{4,0},{5,21},{6,2},{7,23},{8,12},{9,25},... | collective-permute-start | bytes 1572872 | tf_op jit(solution)/shard_map/ppermute | solution.py:55
  105.1 0.4 collective-permute-start.21
  105.5 12.5 %collective-permute-done.19 = bf16[32,64,128]{2,1,0:T(8,128)(2,1)S(1)} collective-permute-done((bf16[32,64,128]{2,1,0:T(8,128)(2,1)S(1)}, bf16[32,64,128]{2,1,0:T(8,128)(2,1)S(1)}, u32[]{:S(2)}, u32[]{:S(2)}) %collective-permute-start.19) | collective-permute-done | bytes 524320 | tf_op jit(solution)/shard_map/ppermute | solution.py:55
  117.9 0.6 collective-permute-done.21
  118.6 0.4 add_convert_fusion
  119.0 0.2 collective-permute-start.22
  119.1 2.6 %collective-permute-start.24 = (bf16[8,64,128]{2,1,0:T(8,128)(2,1)S(1)}, bf16[8,64,128]{2,1,0:T(8,128)(2,1)S(1)}, u32[]{:S(2)}, u32[]{:S(2)}) collective-permute-start(bf16[8,64,128]{2,1,0:T(8,128)(2,1)S(1)} %get-tuple-element.58), channel_id=1, source_target_pairs={{0,24},{1,7},{2,26},{3,1},{4,28},{5,3},{6,30},{7,5},{8,0},{9,15},{... | collective-permute-start | bytes 393224 | tf_op jit(solution)/shard_map/ppermute | solution.py:55
  121.7 0.9 collective-permute-start.23
  122.6 1.5 %collective-permute-done.22 = bf16[8,64,128]{2,1,0:T(8,128)(2,1)S(1)} collective-permute-done((bf16[8,64,128]{2,1,0:T(8,128)(2,1)S(1)}, bf16[8,64,128]{2,1,0:T(8,128)(2,1)S(1)}, u32[]{:S(2)}, u32[]{:S(2)}) %collective-permute-start.22) | collective-permute-done | bytes 131104 | tf_op jit(solution)/shard_map/ppermute | solution.py:55
  124.1 3.0 %collective-permute-done.23 = bf16[8,64,128]{2,1,0:T(8,128)(2,1)S(1)} collective-permute-done((bf16[8,64,128]{2,1,0:T(8,128)(2,1)S(1)}, bf16[8,64,128]{2,1,0:T(8,128)(2,1)S(1)}, u32[]{:S(2)}, u32[]{:S(2)}) %collective-permute-start.23) | collective-permute-done | bytes 131104 | tf_op jit(solution)/shard_map/ppermute | solution.py:55
  127.0 0.1 subtract_convert_fusion
  127.2 3.3 %collective-permute-start.25 = (bf16[4,64,128]{2,1,0:T(8,128)(2,1)S(1)}, bf16[4,64,128]{2,1,0:T(8,128)(2,1)S(1)}, u32[]{:S(2)}, u32[]{:S(2)}) collective-permute-start(bf16[4,64,128]{2,1,0:T(8,128)(2,1)S(1)} %broadcast_select_fusion.6), channel_id=1, source_target_pairs={{0,1},{1,0},{2,3},{3,2},{4,5},{5,4},{6,7},{7,6},{8,9},{9,8},{10,11... | collective-permute-start | bytes 196616 | tf_op jit(solution)/shard_map/ppermute | solution.py:55
  130.4 0.9 collective-permute-done.25
  131.4 0.7 pad_maximum_fusion.2
  (35 shorter events, 0.3 us)
Async XLA Ops:
  0.0 3.2 %copy-start = (bf16[1,128,32,128]{3,2,1,0:T(8,128)(2,1)S(1)}, bf16[1,128,32,128]{3,2,1,0:T(8,128)(2,1)}, u32[]{:S(2)}) copy-start(bf16[1,128,32,128]{3,2,1,0:T(8,128)(2,1)} %param.11) | copy-start | bytes 3145732
  0.0 18.9 %collective-permute-start.1 = (bf16[4,128,128]{2,1,0:T(8,128)(2,1)}, bf16[4,128,128]{2,1,0:T(8,128)(2,1)S(1)}, u32[]{:S(2)}, u32[]{:S(2)}) collective-permute-start(bf16[4,128,128]{2,1,0:T(8,128)(2,1)} %param.9), channel_id=1, source_target_pairs={{0,1},{1,0},{2,3},{3,2},{4,5},{5,4},{6,7},{7,6},{8,9},{9,8},{10,11... | collective-permute-start | bytes 393224 | tf_op jit(solution)/shard_map/ppermute | solution.py:55
  3.5 15.4 %collective-permute-start = (bf16[64,1408]{1,0:T(8,128)(2,1)S(1)}, bf16[64,1408]{1,0:T(8,128)(2,1)S(1)}, u32[]{:S(2)}, u32[]{:S(2)}) collective-permute-start(bf16[64,1408]{1,0:T(8,128)(2,1)S(1)} %pad_dynamic-slice_fusion), channel_id=1, source_target_pairs={{0,192},{1,65},{2,194},{3,67},{4,196},{5,69},{6,70},{7,199},{8,72}... | collective-permute-start | bytes 540680 | tf_op jit(solution)/shard_map/ppermute | solution.py:55
  7.5 11.6 %copy-start.4 = (s32[4]{0:T(128)S(1)}, s32[4]{0:T(128)}, u32[]{:S(2)}) copy-start(s32[4]{0:T(128)} %constant.176.clone) | copy-start | bytes 52
  7.5 17.4 %copy-start.3 = (bf16[4,128,128]{2,1,0:T(8,128)(2,1)S(1)}, bf16[4,128,128]{2,1,0:T(8,128)(2,1)}, u32[]{:S(2)}) copy-start(bf16[4,128,128]{2,1,0:T(8,128)(2,1)} %param.9) | copy-start | bytes 393220
  7.5 19.9 %copy-start.5 = (s32[5]{0:T(128)S(1)}, s32[5]{0:T(128)}, u32[]{:S(2)}) copy-start(s32[5]{0:T(128)} %constant.187) | copy-start | bytes 64
  7.5 11.4 %collective-permute-start.2 = (s32[5,32]{1,0:T(8,128)S(1)}, s32[5,32]{1,0:T(8,128)S(1)}, u32[]{:S(2)}, u32[]{:S(2)}) collective-permute-start(s32[5,32]{1,0:T(8,128)S(1)} %stack.48), channel_id=1, source_target_pairs={{0,1},{1,0},{2,3},{3,2},{4,5},{5,4},{6,7},{7,6},{8,9},{9,8},{10,11... | collective-permute-start | bytes 1928 | tf_op jit(solution)/shard_map/ppermute | solution.py:55
  18.9 15.0 %collective-permute-start.6 = (bf16[4,128,4096]{2,1,0:T(8,128)(2,1)}, bf16[4,128,4096]{2,1,0:T(8,128)(2,1)}, u32[]{:S(2)}, u32[]{:S(2)}) collective-permute-start(bf16[4,128,4096]{2,1,0:T(8,128)(2,1)} %reshape.215.right_own), channel_id=1, source_target_pairs={{0,1},{1,0},{2,3},{3,2},{4,5},{5,4},{6,7},{7,6},{8,9},{9,8},{10,11... | collective-permute-start | bytes 12582920 | tf_op jit(solution)/shard_map/ppermute | solution.py:55
  19.4 8.1 %collective-permute-start.5 = (bf16[64,1408]{1,0:T(8,128)(2,1)S(1)}, bf16[64,1408]{1,0:T(8,128)(2,1)S(1)}, u32[]{:S(2)}, u32[]{:S(2)}) collective-permute-start(bf16[64,1408]{1,0:T(8,128)(2,1)S(1)} %collective-permute-done), channel_id=1, source_target_pairs={{0,6},{1,25},{2,0},{3,27},{4,2},{5,29},{6,4},{7,31},{8,14},{9,1},{... | collective-permute-start | bytes 540680 | tf_op jit(solution)/shard_map/ppermute | solution.py:55
  23.1 5.8 %collective-permute-start.4 = (bf16[64,1408]{1,0:T(8,128)(2,1)S(1)}, bf16[64,1408]{1,0:T(8,128)(2,1)S(1)}, u32[]{:S(2)}, u32[]{:S(2)}) collective-permute-start(bf16[64,1408]{1,0:T(8,128)(2,1)S(1)} %collective-permute-done), channel_id=1, source_target_pairs={{0,4},{1,17},{2,6},{3,19},{4,0},{5,21},{6,2},{7,23},{8,12},{9,25},... | collective-permute-start | bytes 540680 | tf_op jit(solution)/shard_map/ppermute | solution.py:55
  23.1 14.2 %collective-permute-start.8 = (bf16[64,4096]{1,0:T(8,128)(2,1)S(1)}, bf16[64,4096]{1,0:T(8,128)(2,1)S(1)}, u32[]{:S(2)}, u32[]{:S(2)}) collective-permute-start(bf16[64,4096]{1,0:T(8,128)(2,1)S(1)} %bitcast.22), channel_id=1, source_target_pairs={{0,224},{1,225},{2,226},{3,227},{4,228},{5,229},{6,230},{7,231},{8... | collective-permute-start | bytes 1572872 | tf_op jit(solution)/shard_map/ppermute | solution.py:55
  24.9 15.1 %collective-permute-start.7 = (bf16[64,4096]{1,0:T(8,128)(2,1)S(1)}, bf16[64,4096]{1,0:T(8,128)(2,1)S(1)}, u32[]{:S(2)}, u32[]{:S(2)}) collective-permute-start(bf16[64,4096]{1,0:T(8,128)(2,1)S(1)} %bitcast.23), channel_id=1, source_target_pairs={{0,32},{1,33},{2,34},{3,35},{4,36},{5,37},{6,38},{7,39},{8,40},{9,... | collective-permute-start | bytes 1572872 | tf_op jit(solution)/shard_map/ppermute | solution.py:55
  27.5 6.3 %collective-permute-start.3 = (bf16[64,1408]{1,0:T(8,128)(2,1)S(1)}, bf16[64,1408]{1,0:T(8,128)(2,1)S(1)}, u32[]{:S(2)}, u32[]{:S(2)}) collective-permute-start(bf16[64,1408]{1,0:T(8,128)(2,1)S(1)} %collective-permute-done), channel_id=1, source_target_pairs={{0,2},{1,9},{2,4},{3,11},{4,6},{5,13},{6,0},{7,15},{8,10},{9,17},{... | collective-permute-start | bytes 540680 | tf_op jit(solution)/shard_map/ppermute | solution.py:55
  33.9 20.2 %collective-permute-start.10 = (bf16[4,64,1408]{2,1,0:T(8,128)(2,1)S(1)}, bf16[4,64,1408]{2,1,0:T(8,128)(2,1)S(1)}, u32[]{:S(2)}, u32[]{:S(2)}) collective-permute-start(bf16[4,64,1408]{2,1,0:T(8,128)(2,1)S(1)} %pad_maximum_fusion.part0), channel_id=1, source_target_pairs={{0,16},{1,5},{2,18},{3,7},{4,20},{5,1},{6,22},{7,3},{8,24},{9,13},... | collective-permute-start | bytes 2162696 | tf_op jit(solution)/shard_map/ppermute | solution.py:55
  36.8 17.2 %collective-permute-start.9 = (bf16[4,64,1408]{2,1,0:T(8,128)(2,1)S(1)}, bf16[4,64,1408]{2,1,0:T(8,128)(2,1)S(1)}, u32[]{:S(2)}, u32[]{:S(2)}) collective-permute-start(bf16[4,64,1408]{2,1,0:T(8,128)(2,1)S(1)} %pad_maximum_fusion.part0), channel_id=1, source_target_pairs={{0,8},{1,3},{2,10},{3,5},{4,12},{5,7},{6,14},{7,1},{8,16},{9,11},{... | collective-permute-start | bytes 2162696 | tf_op jit(solution)/shard_map/ppermute | solution.py:55
  39.9 14.1 %collective-permute-start.11 = (bf16[4,64,1408]{2,1,0:T(8,128)(2,1)S(1)}, bf16[4,64,1408]{2,1,0:T(8,128)(2,1)S(1)}, u32[]{:S(2)}, u32[]{:S(2)}) collective-permute-start(bf16[4,64,1408]{2,1,0:T(8,128)(2,1)S(1)} %pad_maximum_fusion.part0), channel_id=1, source_target_pairs={{0,24},{1,7},{2,26},{3,1},{4,28},{5,3},{6,30},{7,5},{8,0},{9,15},{... | collective-permute-start | bytes 2162696 | tf_op jit(solution)/shard_map/ppermute | solution.py:55
  41.2 2.2 %copy-start.1 = (bf16[4,128,4096]{2,1,0:T(8,128)(2,1)S(1)}, bf16[4,128,4096]{2,1,0:T(8,128)(2,1)}, u32[]{:S(2)}) copy-start(bf16[4,128,4096]{2,1,0:T(8,128)(2,1)} %reshape.215.right_own) | copy-start | bytes 12582916
  60.9 31.4 %copy-start.2 = (bf16[4,128,4096]{2,1,0:T(8,128)(2,1)S(1)}, bf16[4,128,4096]{2,1,0:T(8,128)(2,1)}, u32[]{:S(2)}) copy-start(bf16[4,128,4096]{2,1,0:T(8,128)(2,1)} %reshape.215.right_own) | copy-start | bytes 12582916
  60.9 9.6 %collective-permute-start.12 = (bf16[32,64,128]{2,1,0:T(8,128)(2,1)S(1)}, bf16[32,64,128]{2,1,0:T(8,128)(2,1)S(1)}, u32[]{:S(2)}, u32[]{:S(2)}) collective-permute-start(bf16[32,64,128]{2,1,0:T(8,128)(2,1)S(1)} %get-tuple-element.41), channel_id=1, source_target_pairs={{0,2},{1,9},{2,4},{3,11},{4,6},{5,13},{6,0},{7,15},{8,10},{9,17},{... | collective-permute-start | bytes 1572872 | tf_op jit(solution)/shard_map/ppermute | solution.py:55
  61.0 15.1 %collective-permute-start.13 = (bf16[32,64,128]{2,1,0:T(8,128)(2,1)S(1)}, bf16[32,64,128]{2,1,0:T(8,128)(2,1)S(1)}, u32[]{:S(2)}, u32[]{:S(2)}) collective-permute-start(bf16[32,64,128]{2,1,0:T(8,128)(2,1)S(1)} %get-tuple-element.42), channel_id=1, source_target_pairs={{0,4},{1,17},{2,6},{3,19},{4,0},{5,21},{6,2},{7,23},{8,12},{9,25},... | collective-permute-start | bytes 1572872 | tf_op jit(solution)/shard_map/ppermute | solution.py:55
  63.7 13.1 %collective-permute-start.14 = (bf16[32,64,128]{2,1,0:T(8,128)(2,1)S(1)}, bf16[32,64,128]{2,1,0:T(8,128)(2,1)S(1)}, u32[]{:S(2)}, u32[]{:S(2)}) collective-permute-start(bf16[32,64,128]{2,1,0:T(8,128)(2,1)S(1)} %get-tuple-element.43), channel_id=1, source_target_pairs={{0,6},{1,25},{2,0},{3,27},{4,2},{5,29},{6,4},{7,31},{8,14},{9,1},{... | collective-permute-start | bytes 1572872 | tf_op jit(solution)/shard_map/ppermute | solution.py:55
  77.2 5.1 %collective-permute-start.15 = (bf16[8,64,128]{2,1,0:T(8,128)(2,1)S(1)}, bf16[8,64,128]{2,1,0:T(8,128)(2,1)S(1)}, u32[]{:S(2)}, u32[]{:S(2)}) collective-permute-start(bf16[8,64,128]{2,1,0:T(8,128)(2,1)S(1)} %get-tuple-element.60), channel_id=1, source_target_pairs={{0,8},{1,3},{2,10},{3,5},{4,12},{5,7},{6,14},{7,1},{8,16},{9,11},{... | collective-permute-start | bytes 393224 | tf_op jit(solution)/shard_map/ppermute | solution.py:55
  78.0 4.3 %collective-permute-start.17 = (bf16[8,64,128]{2,1,0:T(8,128)(2,1)S(1)}, bf16[8,64,128]{2,1,0:T(8,128)(2,1)S(1)}, u32[]{:S(2)}, u32[]{:S(2)}) collective-permute-start(bf16[8,64,128]{2,1,0:T(8,128)(2,1)S(1)} %get-tuple-element.61), channel_id=1, source_target_pairs={{0,24},{1,7},{2,26},{3,1},{4,28},{5,3},{6,30},{7,5},{8,0},{9,15},{... | collective-permute-start | bytes 393224 | tf_op jit(solution)/shard_map/ppermute | solution.py:55
  79.9 5.3 %collective-permute-start.16 = (bf16[8,64,128]{2,1,0:T(8,128)(2,1)S(1)}, bf16[8,64,128]{2,1,0:T(8,128)(2,1)S(1)}, u32[]{:S(2)}, u32[]{:S(2)}) collective-permute-start(bf16[8,64,128]{2,1,0:T(8,128)(2,1)S(1)} %get-tuple-element.62), channel_id=1, source_target_pairs={{0,16},{1,5},{2,18},{3,7},{4,20},{5,1},{6,22},{7,3},{8,24},{9,13},... | collective-permute-start | bytes 393224 | tf_op jit(solution)/shard_map/ppermute | solution.py:55
  85.4 6.9 %collective-permute-start.18 = (bf16[8,64,128]{2,1,0:T(8,128)(2,1)S(1)}, bf16[8,64,128]{2,1,0:T(8,128)(2,1)S(1)}, u32[]{:S(2)}, u32[]{:S(2)}) collective-permute-start(bf16[8,64,128]{2,1,0:T(8,128)(2,1)S(1)} %subtract_convert_fusion.1.own_rows), channel_id=1, source_target_pairs={{0,1},{1,0},{2,3},{3,2},{4,5},{5,4},{6,7},{7,6},{8,9},{9,8},{10,11... | collective-permute-start | bytes 393224 | tf_op jit(solution)/shard_map/ppermute | solution.py:55
  102.7 15.2 %collective-permute-start.19 = (bf16[32,64,128]{2,1,0:T(8,128)(2,1)S(1)}, bf16[32,64,128]{2,1,0:T(8,128)(2,1)S(1)}, u32[]{:S(2)}, u32[]{:S(2)}) collective-permute-start(bf16[32,64,128]{2,1,0:T(8,128)(2,1)S(1)} %get-tuple-element.46), channel_id=1, source_target_pairs={{0,2},{1,9},{2,4},{3,11},{4,6},{5,13},{6,0},{7,15},{8,10},{9,17},{... | collective-permute-start | bytes 1572872 | tf_op jit(solution)/shard_map/ppermute | solution.py:55
  102.8 15.1 %collective-permute-start.20 = (bf16[32,64,128]{2,1,0:T(8,128)(2,1)S(1)}, bf16[32,64,128]{2,1,0:T(8,128)(2,1)S(1)}, u32[]{:S(2)}, u32[]{:S(2)}) collective-permute-start(bf16[32,64,128]{2,1,0:T(8,128)(2,1)S(1)} %get-tuple-element.47), channel_id=1, source_target_pairs={{0,4},{1,17},{2,6},{3,19},{4,0},{5,21},{6,2},{7,23},{8,12},{9,25},... | collective-permute-start | bytes 1572872 | tf_op jit(solution)/shard_map/ppermute | solution.py:55
  105.1 13.5 %collective-permute-start.21 = (bf16[32,64,128]{2,1,0:T(8,128)(2,1)S(1)}, bf16[32,64,128]{2,1,0:T(8,128)(2,1)S(1)}, u32[]{:S(2)}, u32[]{:S(2)}) collective-permute-start(bf16[32,64,128]{2,1,0:T(8,128)(2,1)S(1)} %get-tuple-element.48), channel_id=1, source_target_pairs={{0,6},{1,25},{2,0},{3,27},{4,2},{5,29},{6,4},{7,31},{8,14},{9,1},{... | collective-permute-start | bytes 1572872 | tf_op jit(solution)/shard_map/ppermute | solution.py:55
  119.0 5.1 %collective-permute-start.22 = (bf16[8,64,128]{2,1,0:T(8,128)(2,1)S(1)}, bf16[8,64,128]{2,1,0:T(8,128)(2,1)S(1)}, u32[]{:S(2)}, u32[]{:S(2)}) collective-permute-start(bf16[8,64,128]{2,1,0:T(8,128)(2,1)S(1)} %get-tuple-element.57), channel_id=1, source_target_pairs={{0,8},{1,3},{2,10},{3,5},{4,12},{5,7},{6,14},{7,1},{8,16},{9,11},{... | collective-permute-start | bytes 393224 | tf_op jit(solution)/shard_map/ppermute | solution.py:55
  119.1 5.0 %collective-permute-start.24 = (bf16[8,64,128]{2,1,0:T(8,128)(2,1)S(1)}, bf16[8,64,128]{2,1,0:T(8,128)(2,1)S(1)}, u32[]{:S(2)}, u32[]{:S(2)}) collective-permute-start(bf16[8,64,128]{2,1,0:T(8,128)(2,1)S(1)} %get-tuple-element.58), channel_id=1, source_target_pairs={{0,24},{1,7},{2,26},{3,1},{4,28},{5,3},{6,30},{7,5},{8,0},{9,15},{... | collective-permute-start | bytes 393224 | tf_op jit(solution)/shard_map/ppermute | solution.py:55
  121.7 5.3 %collective-permute-start.23 = (bf16[8,64,128]{2,1,0:T(8,128)(2,1)S(1)}, bf16[8,64,128]{2,1,0:T(8,128)(2,1)S(1)}, u32[]{:S(2)}, u32[]{:S(2)}) collective-permute-start(bf16[8,64,128]{2,1,0:T(8,128)(2,1)S(1)} %get-tuple-element.59), channel_id=1, source_target_pairs={{0,16},{1,5},{2,18},{3,7},{4,20},{5,1},{6,22},{7,3},{8,24},{9,13},... | collective-permute-start | bytes 393224 | tf_op jit(solution)/shard_map/ppermute | solution.py:55
  127.2 4.2 %collective-permute-start.25 = (bf16[4,64,128]{2,1,0:T(8,128)(2,1)S(1)}, bf16[4,64,128]{2,1,0:T(8,128)(2,1)S(1)}, u32[]{:S(2)}, u32[]{:S(2)}) collective-permute-start(bf16[4,64,128]{2,1,0:T(8,128)(2,1)S(1)} %broadcast_select_fusion.6), channel_id=1, source_target_pairs={{0,1},{1,0},{2,3},{3,2},{4,5},{5,4},{6,7},{7,6},{8,9},{9,8},{10,11... | collective-permute-start | bytes 196616 | tf_op jit(solution)/shard_map/ppermute | solution.py:55

commit v3 on v2

--- a/solution.py
+++ b/solution.py
@@ -64,23 +64,36 @@
 
 vmem = pl.BlockSpec(memory_space=pltpu.VMEM)
 smem = pl.BlockSpec(memory_space=pltpu.SMEM)
+anywhere = pl.BlockSpec(memory_space=pl.ANY)
 
 
 def params(mib):
     return pltpu.CompilerParams(vmem_limit_bytes=mib * 1024 * 1024)
 
 
-def multiply_state(core, own_rows, other_rows, right_own, right_other, state, product):
-    nb, side, wide = right_own.shape
+def multiply_state(
+    core, own_rows, other_rows, right_own, right_other, right_v, right_sems, state, product
+):
+    count, side, wide = right_own.shape
+    copies = [
+        pltpu.make_async_copy(right_other.at[b], right_v.at[b], right_sems.at[b])
+        for b in range(count)
+    ]
+    for c in copies:
+        c.start()
     half = side // 2
+    blocks = state.shape[0]
+    nb = blocks // 2
     mine = pl.multiple_of(core * half, half)
     theirs = pl.multiple_of((1 - core) * half, half)
     state[:, pl.ds(mine, half), :] = own_rows[...]
     state[:, pl.ds(theirs, half), :] = other_rows[...]
     step = 512
-    for b in range(2 * nb):
+    for b in range(blocks):
         at = core * nb + b if b < nb else (1 - core) * nb + b - nb
-        right = right_own.at[b] if b < nb else right_other.at[b - nb]
+        if b >= count:
+            copies[b - count].wait()
+        right = right_own.at[b] if b < count else right_v.at[b - count]
         s = state[at]
         for n in range(wide // step):
             r = jnp.dot(
@@ -93,18 +106,20 @@
                 ]
 
 
-def multiply_left(pairs, left, product, partial, total, outs):
-    half, side = total.shape[1:]
+def multiply_left(left, product, partial, start, stop):
     wide = product.shape[0]
-    rows = partial.shape[1]
-    total[...] = jnp.zeros_like(total)
+    side = partial.shape[2]
     for n in range(partial.shape[0] // 2):
         r = jnp.dot(
-            left[:rows, :wide], product[:, n * 2 * side:(n + 1) * 2 * side],
+            left[:, :wide], product[:, n * 2 * side:(n + 1) * 2 * side],
             preferred_element_type=jnp.float32,
         ).astype(jnp.bfloat16)
-        partial[2 * n] = r[:, :side]
-        partial[2 * n + 1] = r[:, side:]
+        partial[2 * n, start:stop] = r[:, :side]
+        partial[2 * n + 1, start:stop] = r[:, side:]
+
+
+def place_pairs(pairs, partial, total, outs):
+    half = total.shape[1]
 
     def place(p, carry):
         at = pl.multiple_of(pairs[0, p] * half, half)
@@ -119,22 +134,31 @@
         out[...] = total[i * count:(i + 1) * count]
 
 
-def product_kernel(pairs, own_rows, other_rows, right_own, right_other, product, state):
-    multiply_state(pairs[3, 0], own_rows, other_rows, right_own, right_other, state, product)
+def product_kernel(
+    core, own_rows, other_rows, right_own, right_other, own, below, above,
+    product, partial, state, right_v, right_sems,
+):
+    multiply_state(
+        core[0], own_rows, other_rows, right_own, right_other, right_v, right_sems, state, product
+    )
+    stacked = jnp.concatenate([own[...], below[...], above[...]], axis=0)
+    multiply_left(stacked, product, partial, 0, stacked.shape[0])
 
 
 def first_kernel(
-    pairs, places, own, below, above, part0, part1, part2, part3, product,
+    pairs, places, own, below, above, part0, part1, part2, part3, product, partial_near,
     out0, out1, out2, out3, left, partial, total, sems, near_sems,
 ):
-    half = own.shape[0]
+    half, wide = own.shape
+    near_rows = near * half
+    rows = partial.shape[1]
+    near_copies = [
+        pltpu.make_async_copy(
+            ref, left.at[i * half:(i + 1) * half, 0:wide], near_sems.at[i]
+        )
+        for i, ref in enumerate((own, below, above))
+    ]
     copies = []
-    for i, ref in enumerate((own, below, above)):
-        copies.append(
-            pltpu.make_async_copy(
-                ref, left.at[i * half:(i + 1) * half, 0:own.shape[1]], near_sems.at[i]
-            )
-        )
     for i, ref in enumerate((part0, part1, part2, part3)):
         for j in range(4):
             row = pl.multiple_of(places[0, i * 4 + j], half)
@@ -145,19 +169,27 @@
                     sems.at[i * 4 + j],
                 )
             )
-    for c in copies:
+    for c in copies + near_copies:
         c.start()
-    for c in copies:
+    total[...] = jnp.zeros_like(total)
+    partial[:, :near_rows] = partial_near[...]
+    for c in copies + near_copies:
         c.wait()
-    multiply_left(pairs, left, product, partial, total, (out0, out1, out2, out3))
+    multiply_left(left.at[near_rows:rows], product, partial, near_rows, rows)
+    place_pairs(pairs, partial, total, (out0, out1, out2, out3))
 
 
 def second_kernel(
     pairs, own_rows, other_rows, right_own, right_other, left,
-    out0, out1, out2, out3, state, product, partial, total,
+    out0, out1, out2, out3, state, right_v, right_sems, product, partial, total,
 ):
-    multiply_state(pairs[3, 0], own_rows, other_rows, right_own, right_other, state, product)
-    multiply_left(pairs, left, product, partial, total, (out0, out1, out2, out3))
+    rows = partial.shape[1]
+    total[...] = jnp.zeros_like(total)
+    multiply_state(
+        pairs[3, 0], own_rows, other_rows, right_own, right_other, right_v, right_sems, state, product
+    )
+    multiply_left(left.at[:rows], product, partial, 0, rows)
+    place_pairs(pairs, partial, total, (out0, out1, out2, out3))
 
 
 def on_device(psi, right_env, left_env, env_index, source_block, target_slot, target_block):
@@ -204,6 +236,7 @@
     line, right_other = lax.optimization_barrier((line, right_other))
     last_line, below, above = lax.optimization_barrier((line, below, above))
     parts = [line] + [send(last_line if d < 0 else line, second(d)) for d in shifts]
+    rights = (right_own, right_other)
 
     back = jnp.array([0, -1, -2, 1], jnp.int32)
     by_first, by_second = back[None, :], back[:, None]
@@ -228,7 +261,11 @@
     pair_count = pairs.shape[1]
     left_shape = ((envs + 1) * half, thirds * third)
     sums_shape = [jax.ShapeDtypeStruct((4 * blocks, half, side), bf16)] * 4
-    state_scratch = pltpu.VMEM((blocks, side, side), bf16)
+    state_scratch = [
+        pltpu.VMEM((blocks, side, side), bf16),
+        pltpu.VMEM((nb, side, wide), bf16),
+        pltpu.SemaphoreType.DMA((nb,)),
+    ]
     product_scratch = pltpu.VMEM((wide, blocks * side), bf16)
     left_scratch = [
         pltpu.VMEM((blocks, envs * half, side), bf16),
@@ -237,46 +274,53 @@
     state_flops = 2 * blocks * side * side * wide
     left_flops = 2 * envs * half * wide * blocks * side
 
-    product = pl.pallas_call(
+    near_flops = left_flops * near // envs
+    core_index = jnp.broadcast_to(core, (1,)).astype(jnp.int32)
+    product, partial_near = pl.pallas_call(
         product_kernel,
-        out_shape=jax.ShapeDtypeStruct((wide, blocks * side), bf16),
-        in_specs=[smem] + [vmem] * 4,
-        out_specs=vmem,
-        scratch_shapes=[state_scratch],
-        compiler_params=params(8),
-        cost_estimate=pl.CostEstimate(flops=state_flops, bytes_accessed=0, transcendentals=0),
+        out_shape=[
+            jax.ShapeDtypeStruct((wide, blocks * side), bf16),
+            jax.ShapeDtypeStruct((blocks, near * half, side), bf16),
+        ],
+        in_specs=[smem] + [vmem] * 3 + [anywhere] + [vmem] * 3,
+        out_specs=[vmem] * 2,
+        scratch_shapes=state_scratch,
+        compiler_params=params(22),
+        cost_estimate=pl.CostEstimate(
+            flops=state_flops + near_flops, bytes_accessed=0, transcendentals=0
+        ),
         name="product",
-    )(pairs, own_rows, other_rows, right_own, right_other)
+    )(core_index, own_rows, other_rows, *rights, own, below, above)
 
     for step in range(2):
         if step == 0:
             *sums, left = pl.pallas_call(
                 first_kernel,
                 out_shape=sums_shape + [jax.ShapeDtypeStruct(left_shape, bf16)],
-                in_specs=[smem] * 2 + [vmem] * 8,
+                in_specs=[smem] * 2 + [vmem] * 9,
                 out_specs=[vmem] * 5,
                 scratch_shapes=left_scratch + [
                     pltpu.SemaphoreType.DMA((16,)), pltpu.SemaphoreType.DMA((near,))
                 ],
-                compiler_params=params(12),
+                compiler_params=params(16),
                 cost_estimate=pl.CostEstimate(
-                    flops=left_flops, bytes_accessed=0, transcendentals=0
+                    flops=left_flops - near_flops, bytes_accessed=0, transcendentals=0
                 ),
                 name="contract_first",
-            )(pairs, places, own, below, above, *parts, product)
+            )(pairs, places, own, below, above, *parts, product, partial_near)
         else:
             sums = pl.pallas_call(
                 second_kernel,
                 out_shape=sums_shape,
-                in_specs=[smem] + [vmem] * 5,
+                in_specs=[smem] + [vmem] * 3 + [anywhere, vmem],
                 out_specs=[vmem] * 4,
-                scratch_shapes=[state_scratch, product_scratch] + left_scratch,
-                compiler_params=params(24),
+                scratch_shapes=state_scratch + [product_scratch] + left_scratch,
+                compiler_params=params(30),
                 cost_estimate=pl.CostEstimate(
                     flops=left_flops + state_flops, bytes_accessed=0, transcendentals=0
                 ),
                 name="contract_second",
-            )(pairs, own_rows, other_rows, right_own, right_other, left)
+            )(pairs, own_rows, other_rows, *rights, left)
         got = [send(sums[k + 1], first(d)) for k, d in enumerate(shifts)]
         summed = sums[0].astype(f32)
         for g in got:

time: 132 us -> 131 us (level)
    pallas_call x1, Pallas kernels: 6.87 us -> 5.3 us  [on_device(): pl.pallas_call(first_kernel, out_shape=sums_shape + [jax.ShapeDtypeStruct...]
  transfers between devices with their start and end apart: 26 -> 26, of which waited for: 16 -> 16; matrix products, arithmetic and copies ran while one was open for 8% -> 8% of each run, Pallas kernels for 4% -> 5%
where the time goes in v3:
time: 131 us; the launch traced here: 130 us
  waiting for transfers between devices  53.2 us (41%)
  starting transfers between devices  40.9 us (31%)
  Pallas kernels  21.8 us (17%)
  local copies, waits for them, and re-layouts  10.7 us (8%)
  other arithmetic  3.52 us (3%)
    ppermute x26, waiting for transfers between devices, send(): return lax.ppermute(a, axes, perm)  53.2 us
    ppermute x26, starting transfers between devices, send(): return lax.ppermute(a, axes, perm)  40.9 us
    pallas_call x1, Pallas kernels, on_device(): pl.pallas_call(second_kernel, out_shape=sums_shape, in_specs=[smem] + [vm...  10.4 us
    reshape x1, local copies, waits for them, and re-layouts, on_device(): right_own = right_env.reshape(nb, side, wide)  7.29 us
    pallas_call x1, Pallas kernels, on_device(): pl.pallas_call(product_kernel, out_shape=[jax.ShapeDtypeStruct((wide, blo...  6.09 us
    pallas_call x1, Pallas kernels, on_device(): pl.pallas_call(first_kernel, out_shape=sums_shape + [jax.ShapeDtypeStruct...  5.3 us
  transfers between devices with their start and end apart: 26, of which 16 were waited for; matrix products, arithmetic and copies ran while one was open for 8% of the time, Pallas kernels for 5%

profile of v3, /device:TPU:1, one launch (start us, length us, event | category | flops | bytes accessed | tf_op | source)
XLA Modules:
  0.0 130.4 jit_solution(2707975820690227446)
XLA Ops:
  0.0 3.2 %collective-permute-start.1 = (bf16[4,128,128]{2,1,0:T(8,128)(2,1)}, bf16[4,128,128]{2,1,0:T(8,128)(2,1)S(1)}, u32[]{:S(2)}, u32[]{:S(2)}) collective-permute-start(bf16[4,128,128]{2,1,0:T(8,128)(2,1)} %param.9), channel_id=1, source_target_pairs={{0,1},{1,0},{2,3},{3,2},{4,5},{5,4},{6,7},{7,6},{8,9},{9,8},{10,11... | collective-permute-start | bytes 393224 | tf_op jit(solution)/shard_map/ppermute | solution.py:55
  3.3 0.2 copy.12
  3.5 1.9 %collective-permute-start = (bf16[64,1408]{1,0:T(8,128)(2,1)S(1)}, bf16[64,1408]{1,0:T(8,128)(2,1)S(1)}, u32[]{:S(2)}, u32[]{:S(2)}) collective-permute-start(bf16[64,1408]{1,0:T(8,128)(2,1)S(1)} %pad_dynamic-slice_fusion), channel_id=1, source_target_pairs={{0,192},{1,65},{2,194},{3,67},{4,196},{5,69},{6,70},{7,199},{8,72}... | collective-permute-start | bytes 540680 | tf_op jit(solution)/shard_map/ppermute | solution.py:55
  5.4 0.7 fusion.3
  6.1 0.7 add_bitcast_fusion
  6.8 0.7 stack.48
  7.5 0.0 copy-start.3
  7.5 0.0 copy-start.5
  7.5 4.1 %collective-permute-start.2 = (s32[5,32]{1,0:T(8,128)S(1)}, s32[5,32]{1,0:T(8,128)S(1)}, u32[]{:S(2)}, u32[]{:S(2)}) collective-permute-start(s32[5,32]{1,0:T(8,128)S(1)} %stack.48), channel_id=1, source_target_pairs={{0,1},{1,0},{2,3},{3,2},{4,5},{5,4},{6,7},{7,6},{8,9},{9,8},{10,11... | collective-permute-start | bytes 1928 | tf_op jit(solution)/shard_map/ppermute | solution.py:55
  11.6 7.3 %reshape.215.right_own = bf16[4,128,4096]{2,1,0:T(8,128)(2,1)} reshape(bf16[4,128,32,128]{3,2,1,0:T(8,128)(2,1)} %param.10) | data formatting | bytes 8388608 | tf_op jit(solution)/shard_map/reshape | solution.py:226
  18.9 0.1 collective-permute-start.6
  19.0 0.1 pad.16.clone
  19.1 0.1 select_add_fusion.1
  19.2 0.1 add.252
  19.2 0.1 add.256
  19.4 3.7 %collective-permute-start.5 = (bf16[64,1408]{1,0:T(8,128)(2,1)S(1)}, bf16[64,1408]{1,0:T(8,128)(2,1)S(1)}, u32[]{:S(2)}, u32[]{:S(2)}) collective-permute-start(bf16[64,1408]{1,0:T(8,128)(2,1)S(1)} %collective-permute-done), channel_id=1, source_target_pairs={{0,6},{1,25},{2,0},{3,27},{4,2},{5,29},{6,4},{7,31},{8,14},{9,1},{... | collective-permute-start | bytes 540680 | tf_op jit(solution)/shard_map/ppermute | solution.py:55
  23.1 1.8 %collective-permute-start.8 = (bf16[64,4096]{1,0:T(8,128)(2,1)S(1)}, bf16[64,4096]{1,0:T(8,128)(2,1)S(1)}, u32[]{:S(2)}, u32[]{:S(2)}) collective-permute-start(bf16[64,4096]{1,0:T(8,128)(2,1)S(1)} %bitcast.23), channel_id=1, source_target_pairs={{0,224},{1,225},{2,226},{3,227},{4,228},{5,229},{6,230},{7,231},{8... | collective-permute-start | bytes 1572872 | tf_op jit(solution)/shard_map/ppermute | solution.py:55
  24.9 0.1 broadcast_select_fusion.2
  25.0 2.5 %collective-permute-done.5 = bf16[64,1408]{1,0:T(8,128)(2,1)S(1)} collective-permute-done((bf16[64,1408]{1,0:T(8,128)(2,1)S(1)}, bf16[64,1408]{1,0:T(8,128)(2,1)S(1)}, u32[]{:S(2)}, u32[]{:S(2)}) %collective-permute-start.5) | collective-permute-done | bytes 180256 | tf_op jit(solution)/shard_map/ppermute | solution.py:55
  27.5 0.1 broadcast_add_fusion
  27.5 1.4 %collective-permute-done.4 = bf16[64,1408]{1,0:T(8,128)(2,1)S(1)} collective-permute-done((bf16[64,1408]{1,0:T(8,128)(2,1)S(1)}, bf16[64,1408]{1,0:T(8,128)(2,1)S(1)}, u32[]{:S(2)}, u32[]{:S(2)}) %collective-permute-start.4) | collective-permute-done | bytes 180256 | tf_op jit(solution)/shard_map/ppermute | solution.py:55
  28.9 4.8 %collective-permute-done.3 = bf16[64,1408]{1,0:T(8,128)(2,1)S(1)} collective-permute-done((bf16[64,1408]{1,0:T(8,128)(2,1)S(1)}, bf16[64,1408]{1,0:T(8,128)(2,1)S(1)}, u32[]{:S(2)}, u32[]{:S(2)}) %collective-permute-start.3) | collective-permute-done | bytes 180256 | tf_op jit(solution)/shard_map/ppermute | solution.py:55
  33.8 0.1 pad_maximum_fusion.part0
  33.9 3.0 %collective-permute-start.10 = (bf16[4,64,1408]{2,1,0:T(8,128)(2,1)S(1)}, bf16[4,64,1408]{2,1,0:T(8,128)(2,1)S(1)}, u32[]{:S(2)}, u32[]{:S(2)}) collective-permute-start(bf16[4,64,1408]{2,1,0:T(8,128)(2,1)S(1)} %pad_maximum_fusion.part0), channel_id=1, source_target_pairs={{0,16},{1,5},{2,18},{3,7},{4,20},{5,1},{6,22},{7,3},{8,24},{9,13},... | collective-permute-start | bytes 2162696 | tf_op jit(solution)/shard_map/ppermute | solution.py:55
  36.8 0.5 collective-permute-start.9
  37.3 2.6 %collective-permute-done.7.below = bf16[64,4096]{1,0:T(8,128)(2,1)S(1)} collective-permute-done((bf16[64,4096]{1,0:T(8,128)(2,1)S(1)}, bf16[64,4096]{1,0:T(8,128)(2,1)S(1)}, u32[]{:S(2)}, u32[]{:S(2)}) %collective-permute-start.7) | collective-permute-done | bytes 524320 | tf_op jit(solution)/shard_map/ppermute | solution.py:55
  39.9 1.1 collective-permute-start.11
  41.0 0.1 pad_add_fusion
  41.1 0.1 add_add_fusion.pairs
  41.2 2.2 %copy-done.1 = bf16[4,128,4096]{2,1,0:T(8,128)(2,1)S(1)} copy-done((bf16[4,128,4096]{2,1,0:T(8,128)(2,1)S(1)}, bf16[4,128,4096]{2,1,0:T(8,128)(2,1)}, u32[]{:S(2)}) %copy-start.1) | copy-done | bytes 4194328
  43.3 6.1 %product.1 = (bf16[4096,1024]{1,0:T(8,128)(2,1)S(1)}, bf16[8,192,128]{2,1,0:T(8,128)(2,1)S(1)}) custom-call(s32[1]{0:T(128)} %bitcast.10.core, bf16[8,64,128]{2,1,0:T(8,128)(2,1)S(1)} %get-tuple-element.68.own_rows, bf16[8,64,128]{2,1,0:T(8,128)(2,1)S(1)} %get-tuple-element.67.other_rows, bf16[4,128,4096]{2,1,0:T(8,128)(2,1)S(1)} %copy-done.1, ...), custom_call_target="tpu_custom_call" | custom-call | flops 2684354560 | tf_op jit(solution)/shard_map/product/pallas_call | solution.py:279
  49.4 4.6 %collective-permute-done.11.part3 = bf16[4,64,1408]{2,1,0:T(8,128)(2,1)S(1)} collective-permute-done((bf16[4,64,1408]{2,1,0:T(8,128)(2,1)S(1)}, bf16[4,64,1408]{2,1,0:T(8,128)(2,1)S(1)}, u32[]{:S(2)}, u32[]{:S(2)}) %collective-permute-start.11) | collective-permute-done | bytes 720928 | tf_op jit(solution)/shard_map/ppermute | solution.py:55
  54.1 5.3 %contract_first.1 = (bf16[32,64,128]{2,1,0:T(8,128)(2,1)S(1)}, bf16[32,64,128]{2,1,0:T(8,128)(2,1)S(1)}, bf16[32,64,128]{2,1,0:T(8,128)(2,1)S(1)}, bf16[32,64,128]{2,1,0:T(8,128)(2,1)S(1)}, bf16[576,4224]{1,0:T(8,128)(2,1)S(1)}) custom-call(s32[4,64]{1,0:T(4,128)S(1)} %add_add_fusion.pairs, s32[2,16]{1,0:T(2,128)S(1)} %pad_add_fusion.1.places, ...), custom_call_target="tpu_custom_call" | custom-call | flops 2684354560 | tf_op jit(solution)/shard_map/contract_first/pallas_call | solution.py:297
  59.4 0.1 collective-permute-start.12
  59.5 2.6 %collective-permute-start.13 = (bf16[32,64,128]{2,1,0:T(8,128)(2,1)S(1)}, bf16[32,64,128]{2,1,0:T(8,128)(2,1)S(1)}, u32[]{:S(2)}, u32[]{:S(2)}) collective-permute-start(bf16[32,64,128]{2,1,0:T(8,128)(2,1)S(1)} %get-tuple-element.46), channel_id=1, source_target_pairs={{0,4},{1,17},{2,6},{3,19},{4,0},{5,21},{6,2},{7,23},{8,12},{9,25},... | collective-permute-start | bytes 1572872 | tf_op jit(solution)/shard_map/ppermute | solution.py:55
  62.1 0.0 collective-permute-start.14
  62.1 6.9 %collective-permute-done.12 = bf16[32,64,128]{2,1,0:T(8,128)(2,1)S(1)} collective-permute-done((bf16[32,64,128]{2,1,0:T(8,128)(2,1)S(1)}, bf16[32,64,128]{2,1,0:T(8,128)(2,1)S(1)}, u32[]{:S(2)}, u32[]{:S(2)}) %collective-permute-start.12) | collective-permute-done | bytes 524320 | tf_op jit(solution)/shard_map/ppermute | solution.py:55
  69.0 5.6 %collective-permute-done.13 = bf16[32,64,128]{2,1,0:T(8,128)(2,1)S(1)} collective-permute-done((bf16[32,64,128]{2,1,0:T(8,128)(2,1)S(1)}, bf16[32,64,128]{2,1,0:T(8,128)(2,1)S(1)}, u32[]{:S(2)}, u32[]{:S(2)}) %collective-permute-start.13) | collective-permute-done | bytes 524320 | tf_op jit(solution)/shard_map/ppermute | solution.py:55
  74.6 0.7 collective-permute-done.14
  75.2 0.4 add_convert_fusion.1
  75.6 0.8 collective-permute-start.15
  76.4 2.0 %collective-permute-start.17 = (bf16[8,64,128]{2,1,0:T(8,128)(2,1)S(1)}, bf16[8,64,128]{2,1,0:T(8,128)(2,1)S(1)}, u32[]{:S(2)}, u32[]{:S(2)}) collective-permute-start(bf16[8,64,128]{2,1,0:T(8,128)(2,1)S(1)} %get-tuple-element.65), channel_id=1, source_target_pairs={{0,24},{1,7},{2,26},{3,1},{4,28},{5,3},{6,30},{7,5},{8,0},{9,15},{... | collective-permute-start | bytes 393224 | tf_op jit(solution)/shard_map/ppermute | solution.py:55
  78.4 0.6 collective-permute-start.16
  78.9 1.8 %collective-permute-done.15 = bf16[8,64,128]{2,1,0:T(8,128)(2,1)S(1)} collective-permute-done((bf16[8,64,128]{2,1,0:T(8,128)(2,1)S(1)}, bf16[8,64,128]{2,1,0:T(8,128)(2,1)S(1)}, u32[]{:S(2)}, u32[]{:S(2)}) %collective-permute-start.15) | collective-permute-done | bytes 131104 | tf_op jit(solution)/shard_map/ppermute | solution.py:55
  80.7 3.0 %collective-permute-done.16 = bf16[8,64,128]{2,1,0:T(8,128)(2,1)S(1)} collective-permute-done((bf16[8,64,128]{2,1,0:T(8,128)(2,1)S(1)}, bf16[8,64,128]{2,1,0:T(8,128)(2,1)S(1)}, u32[]{:S(2)}, u32[]{:S(2)}) %collective-permute-start.16) | collective-permute-done | bytes 131104 | tf_op jit(solution)/shard_map/ppermute | solution.py:55
  83.7 0.1 subtract_convert_fusion.1.own_rows
  83.8 5.9 %collective-permute-start.18 = (bf16[8,64,128]{2,1,0:T(8,128)(2,1)S(1)}, bf16[8,64,128]{2,1,0:T(8,128)(2,1)S(1)}, u32[]{:S(2)}, u32[]{:S(2)}) collective-permute-start(bf16[8,64,128]{2,1,0:T(8,128)(2,1)S(1)} %subtract_convert_fusion.1.own_rows), channel_id=1, source_target_pairs={{0,1},{1,0},{2,3},{3,2},{4,5},{5,4},{6,7},{7,6},{8,9},{9,8},{10,11... | collective-permute-start | bytes 393224 | tf_op jit(solution)/shard_map/ppermute | solution.py:55
  89.7 1.0 collective-permute-done.18.other_rows
  90.7 10.4 %contract_second.1 = (bf16[32,64,128]{2,1,0:T(8,128)(2,1)S(1)}, bf16[32,64,128]{2,1,0:T(8,128)(2,1)S(1)}, bf16[32,64,128]{2,1,0:T(8,128)(2,1)S(1)}, bf16[32,64,128]{2,1,0:T(8,128)(2,1)S(1)}) custom-call(s32[4,64]{1,0:T(4,128)S(1)} %add_add_fusion.pairs, bf16[8,64,128]{2,1,0:T(8,128)(2,1)S(1)} %subtract_convert_fusion.1.own_rows, ...), custom_call_target="tpu_custom_call" | custom-call | flops 5368709120 | tf_op jit(solution)/shard_map/contract_second/pallas_call | solution.py:312
  101.1 0.1 collective-permute-start.19
  101.2 2.3 %collective-permute-start.20 = (bf16[32,64,128]{2,1,0:T(8,128)(2,1)S(1)}, bf16[32,64,128]{2,1,0:T(8,128)(2,1)S(1)}, u32[]{:S(2)}, u32[]{:S(2)}) collective-permute-start(bf16[32,64,128]{2,1,0:T(8,128)(2,1)S(1)} %get-tuple-element.51), channel_id=1, source_target_pairs={{0,4},{1,17},{2,6},{3,19},{4,0},{5,21},{6,2},{7,23},{8,12},{9,25},... | collective-permute-start | bytes 1572872 | tf_op jit(solution)/shard_map/ppermute | solution.py:55
  103.5 0.4 collective-permute-start.21
  103.9 12.5 %collective-permute-done.19 = bf16[32,64,128]{2,1,0:T(8,128)(2,1)S(1)} collective-permute-done((bf16[32,64,128]{2,1,0:T(8,128)(2,1)S(1)}, bf16[32,64,128]{2,1,0:T(8,128)(2,1)S(1)}, u32[]{:S(2)}, u32[]{:S(2)}) %collective-permute-start.19) | collective-permute-done | bytes 524320 | tf_op jit(solution)/shard_map/ppermute | solution.py:55
  116.3 0.6 collective-permute-done.21
  117.0 0.4 add_convert_fusion
  117.3 0.1 collective-permute-start.22
  117.5 2.6 %collective-permute-start.24 = (bf16[8,64,128]{2,1,0:T(8,128)(2,1)S(1)}, bf16[8,64,128]{2,1,0:T(8,128)(2,1)S(1)}, u32[]{:S(2)}, u32[]{:S(2)}) collective-permute-start(bf16[8,64,128]{2,1,0:T(8,128)(2,1)S(1)} %get-tuple-element.62), channel_id=1, source_target_pairs={{0,24},{1,7},{2,26},{3,1},{4,28},{5,3},{6,30},{7,5},{8,0},{9,15},{... | collective-permute-start | bytes 393224 | tf_op jit(solution)/shard_map/ppermute | solution.py:55
  120.1 0.9 collective-permute-start.23
  121.0 1.5 %collective-permute-done.22 = bf16[8,64,128]{2,1,0:T(8,128)(2,1)S(1)} collective-permute-done((bf16[8,64,128]{2,1,0:T(8,128)(2,1)S(1)}, bf16[8,64,128]{2,1,0:T(8,128)(2,1)S(1)}, u32[]{:S(2)}, u32[]{:S(2)}) %collective-permute-start.22) | collective-permute-done | bytes 131104 | tf_op jit(solution)/shard_map/ppermute | solution.py:55
  122.5 3.0 %collective-permute-done.23 = bf16[8,64,128]{2,1,0:T(8,128)(2,1)S(1)} collective-permute-done((bf16[8,64,128]{2,1,0:T(8,128)(2,1)S(1)}, bf16[8,64,128]{2,1,0:T(8,128)(2,1)S(1)}, u32[]{:S(2)}, u32[]{:S(2)}) %collective-permute-start.23) | collective-permute-done | bytes 131104 | tf_op jit(solution)/shard_map/ppermute | solution.py:55
  125.4 0.1 subtract_convert_fusion
  125.5 3.3 %collective-permute-start.25 = (bf16[4,64,128]{2,1,0:T(8,128)(2,1)S(1)}, bf16[4,64,128]{2,1,0:T(8,128)(2,1)S(1)}, u32[]{:S(2)}, u32[]{:S(2)}) collective-permute-start(bf16[4,64,128]{2,1,0:T(8,128)(2,1)S(1)} %broadcast_select_fusion.6), channel_id=1, source_target_pairs={{0,1},{1,0},{2,3},{3,2},{4,5},{5,4},{6,7},{7,6},{8,9},{9,8},{10,11... | collective-permute-start | bytes 196616 | tf_op jit(solution)/shard_map/ppermute | solution.py:55
  128.8 0.9 collective-permute-done.25
  129.8 0.7 pad_maximum_fusion.2
  (35 shorter events, 0.3 us)
Async XLA Ops:
  0.0 3.2 %copy-start = (bf16[1,128,32,128]{3,2,1,0:T(8,128)(2,1)S(1)}, bf16[1,128,32,128]{3,2,1,0:T(8,128)(2,1)}, u32[]{:S(2)}) copy-start(bf16[1,128,32,128]{3,2,1,0:T(8,128)(2,1)} %param.11) | copy-start | bytes 3145732
  0.0 18.9 %collective-permute-start.1 = (bf16[4,128,128]{2,1,0:T(8,128)(2,1)}, bf16[4,128,128]{2,1,0:T(8,128)(2,1)S(1)}, u32[]{:S(2)}, u32[]{:S(2)}) collective-permute-start(bf16[4,128,128]{2,1,0:T(8,128)(2,1)} %param.9), channel_id=1, source_target_pairs={{0,1},{1,0},{2,3},{3,2},{4,5},{5,4},{6,7},{7,6},{8,9},{9,8},{10,11... | collective-permute-start | bytes 393224 | tf_op jit(solution)/shard_map/ppermute | solution.py:55
  3.5 15.4 %collective-permute-start = (bf16[64,1408]{1,0:T(8,128)(2,1)S(1)}, bf16[64,1408]{1,0:T(8,128)(2,1)S(1)}, u32[]{:S(2)}, u32[]{:S(2)}) collective-permute-start(bf16[64,1408]{1,0:T(8,128)(2,1)S(1)} %pad_dynamic-slice_fusion), channel_id=1, source_target_pairs={{0,192},{1,65},{2,194},{3,67},{4,196},{5,69},{6,70},{7,199},{8,72}... | collective-permute-start | bytes 540680 | tf_op jit(solution)/shard_map/ppermute | solution.py:55
  7.5 11.6 %copy-start.4 = (s32[4]{0:T(128)S(1)}, s32[4]{0:T(128)}, u32[]{:S(2)}) copy-start(s32[4]{0:T(128)} %constant.176.clone) | copy-start | bytes 52
  7.5 17.4 %copy-start.3 = (bf16[4,128,128]{2,1,0:T(8,128)(2,1)S(1)}, bf16[4,128,128]{2,1,0:T(8,128)(2,1)}, u32[]{:S(2)}) copy-start(bf16[4,128,128]{2,1,0:T(8,128)(2,1)} %param.9) | copy-start | bytes 393220
  7.5 19.9 %copy-start.5 = (s32[5]{0:T(128)S(1)}, s32[5]{0:T(128)}, u32[]{:S(2)}) copy-start(s32[5]{0:T(128)} %constant.187) | copy-start | bytes 64
  7.5 11.4 %collective-permute-start.2 = (s32[5,32]{1,0:T(8,128)S(1)}, s32[5,32]{1,0:T(8,128)S(1)}, u32[]{:S(2)}, u32[]{:S(2)}) collective-permute-start(s32[5,32]{1,0:T(8,128)S(1)} %stack.48), channel_id=1, source_target_pairs={{0,1},{1,0},{2,3},{3,2},{4,5},{5,4},{6,7},{7,6},{8,9},{9,8},{10,11... | collective-permute-start | bytes 1928 | tf_op jit(solution)/shard_map/ppermute | solution.py:55
  18.9 15.0 %collective-permute-start.6 = (bf16[4,128,4096]{2,1,0:T(8,128)(2,1)}, bf16[4,128,4096]{2,1,0:T(8,128)(2,1)}, u32[]{:S(2)}, u32[]{:S(2)}) collective-permute-start(bf16[4,128,4096]{2,1,0:T(8,128)(2,1)} %reshape.215.right_own), channel_id=1, source_target_pairs={{0,1},{1,0},{2,3},{3,2},{4,5},{5,4},{6,7},{7,6},{8,9},{9,8},{10,11... | collective-permute-start | bytes 12582920 | tf_op jit(solution)/shard_map/ppermute | solution.py:55
  19.4 8.1 %collective-permute-start.5 = (bf16[64,1408]{1,0:T(8,128)(2,1)S(1)}, bf16[64,1408]{1,0:T(8,128)(2,1)S(1)}, u32[]{:S(2)}, u32[]{:S(2)}) collective-permute-start(bf16[64,1408]{1,0:T(8,128)(2,1)S(1)} %collective-permute-done), channel_id=1, source_target_pairs={{0,6},{1,25},{2,0},{3,27},{4,2},{5,29},{6,4},{7,31},{8,14},{9,1},{... | collective-permute-start | bytes 540680 | tf_op jit(solution)/shard_map/ppermute | solution.py:55
  23.1 5.8 %collective-permute-start.4 = (bf16[64,1408]{1,0:T(8,128)(2,1)S(1)}, bf16[64,1408]{1,0:T(8,128)(2,1)S(1)}, u32[]{:S(2)}, u32[]{:S(2)}) collective-permute-start(bf16[64,1408]{1,0:T(8,128)(2,1)S(1)} %collective-permute-done), channel_id=1, source_target_pairs={{0,4},{1,17},{2,6},{3,19},{4,0},{5,21},{6,2},{7,23},{8,12},{9,25},... | collective-permute-start | bytes 540680 | tf_op jit(solution)/shard_map/ppermute | solution.py:55
  23.1 14.2 %collective-permute-start.8 = (bf16[64,4096]{1,0:T(8,128)(2,1)S(1)}, bf16[64,4096]{1,0:T(8,128)(2,1)S(1)}, u32[]{:S(2)}, u32[]{:S(2)}) collective-permute-start(bf16[64,4096]{1,0:T(8,128)(2,1)S(1)} %bitcast.23), channel_id=1, source_target_pairs={{0,224},{1,225},{2,226},{3,227},{4,228},{5,229},{6,230},{7,231},{8... | collective-permute-start | bytes 1572872 | tf_op jit(solution)/shard_map/ppermute | solution.py:55
  24.9 15.1 %collective-permute-start.7 = (bf16[64,4096]{1,0:T(8,128)(2,1)S(1)}, bf16[64,4096]{1,0:T(8,128)(2,1)S(1)}, u32[]{:S(2)}, u32[]{:S(2)}) collective-permute-start(bf16[64,4096]{1,0:T(8,128)(2,1)S(1)} %bitcast.24), channel_id=1, source_target_pairs={{0,32},{1,33},{2,34},{3,35},{4,36},{5,37},{6,38},{7,39},{8,40},{9,... | collective-permute-start | bytes 1572872 | tf_op jit(solution)/shard_map/ppermute | solution.py:55
  27.5 6.3 %collective-permute-start.3 = (bf16[64,1408]{1,0:T(8,128)(2,1)S(1)}, bf16[64,1408]{1,0:T(8,128)(2,1)S(1)}, u32[]{:S(2)}, u32[]{:S(2)}) collective-permute-start(bf16[64,1408]{1,0:T(8,128)(2,1)S(1)} %collective-permute-done), channel_id=1, source_target_pairs={{0,2},{1,9},{2,4},{3,11},{4,6},{5,13},{6,0},{7,15},{8,10},{9,17},{... | collective-permute-start | bytes 540680 | tf_op jit(solution)/shard_map/ppermute | solution.py:55
  33.9 20.2 %collective-permute-start.10 = (bf16[4,64,1408]{2,1,0:T(8,128)(2,1)S(1)}, bf16[4,64,1408]{2,1,0:T(8,128)(2,1)S(1)}, u32[]{:S(2)}, u32[]{:S(2)}) collective-permute-start(bf16[4,64,1408]{2,1,0:T(8,128)(2,1)S(1)} %pad_maximum_fusion.part0), channel_id=1, source_target_pairs={{0,16},{1,5},{2,18},{3,7},{4,20},{5,1},{6,22},{7,3},{8,24},{9,13},... | collective-permute-start | bytes 2162696 | tf_op jit(solution)/shard_map/ppermute | solution.py:55
  36.8 17.2 %collective-permute-start.9 = (bf16[4,64,1408]{2,1,0:T(8,128)(2,1)S(1)}, bf16[4,64,1408]{2,1,0:T(8,128)(2,1)S(1)}, u32[]{:S(2)}, u32[]{:S(2)}) collective-permute-start(bf16[4,64,1408]{2,1,0:T(8,128)(2,1)S(1)} %pad_maximum_fusion.part0), channel_id=1, source_target_pairs={{0,8},{1,3},{2,10},{3,5},{4,12},{5,7},{6,14},{7,1},{8,16},{9,11},{... | collective-permute-start | bytes 2162696 | tf_op jit(solution)/shard_map/ppermute | solution.py:55
  39.9 14.1 %collective-permute-start.11 = (bf16[4,64,1408]{2,1,0:T(8,128)(2,1)S(1)}, bf16[4,64,1408]{2,1,0:T(8,128)(2,1)S(1)}, u32[]{:S(2)}, u32[]{:S(2)}) collective-permute-start(bf16[4,64,1408]{2,1,0:T(8,128)(2,1)S(1)} %pad_maximum_fusion.part0), channel_id=1, source_target_pairs={{0,24},{1,7},{2,26},{3,1},{4,28},{5,3},{6,30},{7,5},{8,0},{9,15},{... | collective-permute-start | bytes 2162696 | tf_op jit(solution)/shard_map/ppermute | solution.py:55
  41.2 2.2 %copy-start.1 = (bf16[4,128,4096]{2,1,0:T(8,128)(2,1)S(1)}, bf16[4,128,4096]{2,1,0:T(8,128)(2,1)}, u32[]{:S(2)}) copy-start(bf16[4,128,4096]{2,1,0:T(8,128)(2,1)} %reshape.215.right_own) | copy-start | bytes 12582916
  59.4 31.4 %copy-start.2 = (bf16[4,128,4096]{2,1,0:T(8,128)(2,1)S(1)}, bf16[4,128,4096]{2,1,0:T(8,128)(2,1)}, u32[]{:S(2)}) copy-start(bf16[4,128,4096]{2,1,0:T(8,128)(2,1)} %reshape.215.right_own) | copy-start | bytes 12582916
  59.4 9.6 %collective-permute-start.12 = (bf16[32,64,128]{2,1,0:T(8,128)(2,1)S(1)}, bf16[32,64,128]{2,1,0:T(8,128)(2,1)S(1)}, u32[]{:S(2)}, u32[]{:S(2)}) collective-permute-start(bf16[32,64,128]{2,1,0:T(8,128)(2,1)S(1)} %get-tuple-element.45), channel_id=1, source_target_pairs={{0,2},{1,9},{2,4},{3,11},{4,6},{5,13},{6,0},{7,15},{8,10},{9,17},{... | collective-permute-start | bytes 1572872 | tf_op jit(solution)/shard_map/ppermute | solution.py:55
  59.5 15.1 %collective-permute-start.13 = (bf16[32,64,128]{2,1,0:T(8,128)(2,1)S(1)}, bf16[32,64,128]{2,1,0:T(8,128)(2,1)S(1)}, u32[]{:S(2)}, u32[]{:S(2)}) collective-permute-start(bf16[32,64,128]{2,1,0:T(8,128)(2,1)S(1)} %get-tuple-element.46), channel_id=1, source_target_pairs={{0,4},{1,17},{2,6},{3,19},{4,0},{5,21},{6,2},{7,23},{8,12},{9,25},... | collective-permute-start | bytes 1572872 | tf_op jit(solution)/shard_map/ppermute | solution.py:55
  62.1 13.1 %collective-permute-start.14 = (bf16[32,64,128]{2,1,0:T(8,128)(2,1)S(1)}, bf16[32,64,128]{2,1,0:T(8,128)(2,1)S(1)}, u32[]{:S(2)}, u32[]{:S(2)}) collective-permute-start(bf16[32,64,128]{2,1,0:T(8,128)(2,1)S(1)} %get-tuple-element.47), channel_id=1, source_target_pairs={{0,6},{1,25},{2,0},{3,27},{4,2},{5,29},{6,4},{7,31},{8,14},{9,1},{... | collective-permute-start | bytes 1572872 | tf_op jit(solution)/shard_map/ppermute | solution.py:55
  75.6 5.1 %collective-permute-start.15 = (bf16[8,64,128]{2,1,0:T(8,128)(2,1)S(1)}, bf16[8,64,128]{2,1,0:T(8,128)(2,1)S(1)}, u32[]{:S(2)}, u32[]{:S(2)}) collective-permute-start(bf16[8,64,128]{2,1,0:T(8,128)(2,1)S(1)} %get-tuple-element.64), channel_id=1, source_target_pairs={{0,8},{1,3},{2,10},{3,5},{4,12},{5,7},{6,14},{7,1},{8,16},{9,11},{... | collective-permute-start | bytes 393224 | tf_op jit(solution)/shard_map/ppermute | solution.py:55
  76.4 4.3 %collective-permute-start.17 = (bf16[8,64,128]{2,1,0:T(8,128)(2,1)S(1)}, bf16[8,64,128]{2,1,0:T(8,128)(2,1)S(1)}, u32[]{:S(2)}, u32[]{:S(2)}) collective-permute-start(bf16[8,64,128]{2,1,0:T(8,128)(2,1)S(1)} %get-tuple-element.65), channel_id=1, source_target_pairs={{0,24},{1,7},{2,26},{3,1},{4,28},{5,3},{6,30},{7,5},{8,0},{9,15},{... | collective-permute-start | bytes 393224 | tf_op jit(solution)/shard_map/ppermute | solution.py:55
  78.4 5.3 %collective-permute-start.16 = (bf16[8,64,128]{2,1,0:T(8,128)(2,1)S(1)}, bf16[8,64,128]{2,1,0:T(8,128)(2,1)S(1)}, u32[]{:S(2)}, u32[]{:S(2)}) collective-permute-start(bf16[8,64,128]{2,1,0:T(8,128)(2,1)S(1)} %get-tuple-element.66), channel_id=1, source_target_pairs={{0,16},{1,5},{2,18},{3,7},{4,20},{5,1},{6,22},{7,3},{8,24},{9,13},... | collective-permute-start | bytes 393224 | tf_op jit(solution)/shard_map/ppermute | solution.py:55
  83.8 6.9 %collective-permute-start.18 = (bf16[8,64,128]{2,1,0:T(8,128)(2,1)S(1)}, bf16[8,64,128]{2,1,0:T(8,128)(2,1)S(1)}, u32[]{:S(2)}, u32[]{:S(2)}) collective-permute-start(bf16[8,64,128]{2,1,0:T(8,128)(2,1)S(1)} %subtract_convert_fusion.1.own_rows), channel_id=1, source_target_pairs={{0,1},{1,0},{2,3},{3,2},{4,5},{5,4},{6,7},{7,6},{8,9},{9,8},{10,11... | collective-permute-start | bytes 393224 | tf_op jit(solution)/shard_map/ppermute | solution.py:55
  101.1 15.2 %collective-permute-start.19 = (bf16[32,64,128]{2,1,0:T(8,128)(2,1)S(1)}, bf16[32,64,128]{2,1,0:T(8,128)(2,1)S(1)}, u32[]{:S(2)}, u32[]{:S(2)}) collective-permute-start(bf16[32,64,128]{2,1,0:T(8,128)(2,1)S(1)} %get-tuple-element.50), channel_id=1, source_target_pairs={{0,2},{1,9},{2,4},{3,11},{4,6},{5,13},{6,0},{7,15},{8,10},{9,17},{... | collective-permute-start | bytes 1572872 | tf_op jit(solution)/shard_map/ppermute | solution.py:55
  101.2 15.1 %collective-permute-start.20 = (bf16[32,64,128]{2,1,0:T(8,128)(2,1)S(1)}, bf16[32,64,128]{2,1,0:T(8,128)(2,1)S(1)}, u32[]{:S(2)}, u32[]{:S(2)}) collective-permute-start(bf16[32,64,128]{2,1,0:T(8,128)(2,1)S(1)} %get-tuple-element.51), channel_id=1, source_target_pairs={{0,4},{1,17},{2,6},{3,19},{4,0},{5,21},{6,2},{7,23},{8,12},{9,25},... | collective-permute-start | bytes 1572872 | tf_op jit(solution)/shard_map/ppermute | solution.py:55
  103.5 13.5 %collective-permute-start.21 = (bf16[32,64,128]{2,1,0:T(8,128)(2,1)S(1)}, bf16[32,64,128]{2,1,0:T(8,128)(2,1)S(1)}, u32[]{:S(2)}, u32[]{:S(2)}) collective-permute-start(bf16[32,64,128]{2,1,0:T(8,128)(2,1)S(1)} %get-tuple-element.52), channel_id=1, source_target_pairs={{0,6},{1,25},{2,0},{3,27},{4,2},{5,29},{6,4},{7,31},{8,14},{9,1},{... | collective-permute-start | bytes 1572872 | tf_op jit(solution)/shard_map/ppermute | solution.py:55
  117.3 5.1 %collective-permute-start.22 = (bf16[8,64,128]{2,1,0:T(8,128)(2,1)S(1)}, bf16[8,64,128]{2,1,0:T(8,128)(2,1)S(1)}, u32[]{:S(2)}, u32[]{:S(2)}) collective-permute-start(bf16[8,64,128]{2,1,0:T(8,128)(2,1)S(1)} %get-tuple-element.61), channel_id=1, source_target_pairs={{0,8},{1,3},{2,10},{3,5},{4,12},{5,7},{6,14},{7,1},{8,16},{9,11},{... | collective-permute-start | bytes 393224 | tf_op jit(solution)/shard_map/ppermute | solution.py:55
  117.5 5.0 %collective-permute-start.24 = (bf16[8,64,128]{2,1,0:T(8,128)(2,1)S(1)}, bf16[8,64,128]{2,1,0:T(8,128)(2,1)S(1)}, u32[]{:S(2)}, u32[]{:S(2)}) collective-permute-start(bf16[8,64,128]{2,1,0:T(8,128)(2,1)S(1)} %get-tuple-element.62), channel_id=1, source_target_pairs={{0,24},{1,7},{2,26},{3,1},{4,28},{5,3},{6,30},{7,5},{8,0},{9,15},{... | collective-permute-start | bytes 393224 | tf_op jit(solution)/shard_map/ppermute | solution.py:55
  120.1 5.3 %collective-permute-start.23 = (bf16[8,64,128]{2,1,0:T(8,128)(2,1)S(1)}, bf16[8,64,128]{2,1,0:T(8,128)(2,1)S(1)}, u32[]{:S(2)}, u32[]{:S(2)}) collective-permute-start(bf16[8,64,128]{2,1,0:T(8,128)(2,1)S(1)} %get-tuple-element.63), channel_id=1, source_target_pairs={{0,16},{1,5},{2,18},{3,7},{4,20},{5,1},{6,22},{7,3},{8,24},{9,13},... | collective-permute-start | bytes 393224 | tf_op jit(solution)/shard_map/ppermute | solution.py:55
  125.5 4.2 %collective-permute-start.25 = (bf16[4,64,128]{2,1,0:T(8,128)(2,1)S(1)}, bf16[4,64,128]{2,1,0:T(8,128)(2,1)S(1)}, u32[]{:S(2)}, u32[]{:S(2)}) collective-permute-start(bf16[4,64,128]{2,1,0:T(8,128)(2,1)S(1)} %broadcast_select_fusion.6), channel_id=1, source_target_pairs={{0,1},{1,0},{2,3},{3,2},{4,5},{5,4},{6,7},{7,6},{8,9},{9,8},{10,11... | collective-permute-start | bytes 196616 | tf_op jit(solution)/shard_map/ppermute | solution.py:55

commit v4 on v3

--- a/solution.py
+++ b/solution.py
@@ -210,8 +210,17 @@
     padded = jnp.pad(own, ((0, 0), (0, thirds * third - wide)))
     mine = lax.dynamic_slice_in_dim(padded, chip % thirds * third, third, 1)
     held = send(mine, fetch_far)
-    env_index, target_slot, right_env, _ = lax.optimization_barrier(
-        (env_index, target_slot, right_env, mine)
+    right_env, _ = lax.optimization_barrier((right_env, mine))
+    right_own = right_env.reshape(nb, side, wide)
+    psi_other = send(psi, swap_cores)
+    held, own, right_own, psi_other = lax.optimization_barrier((held, own, right_own, psi_other))
+    right_other = send(right_own, swap_cores)
+    below = send(own, along_z(1))
+    above = send(own, along_z(-1))
+    line = jnp.stack([held] + [send(held, first(d)) for d in shifts])
+    line, right_other = lax.optimization_barrier((line, right_other))
+    last_line, below, above, env_index, target_slot = lax.optimization_barrier(
+        (line, below, above, env_index, target_slot)
     )
     offset = (env_index - z) % envs
     slot_lower = table([0, 2, 3, 5, 7, 6, 4, 1], offset)
@@ -223,18 +232,7 @@
     x_first = (rx * 4 + ry) * blocks + block
     y_first = (ry * 4 + rx) * blocks + block
     lists = jnp.stack([slot_lower, slot_upper, source_block, x_first, y_first])
-    right_own = right_env.reshape(nb, side, wide)
-    psi_other = send(psi, swap_cores)
     their_lists = send(lists, swap_cores)
-    held, own, right_own, psi_other, their_lists = lax.optimization_barrier(
-        (held, own, right_own, psi_other, their_lists)
-    )
-    right_other = send(right_own, swap_cores)
-    below = send(own, along_z(1))
-    above = send(own, along_z(-1))
-    line = jnp.stack([held] + [send(held, first(d)) for d in shifts])
-    line, right_other = lax.optimization_barrier((line, right_other))
-    last_line, below, above = lax.optimization_barrier((line, below, above))
     parts = [line] + [send(last_line if d < 0 else line, second(d)) for d in shifts]
     rights = (right_own, right_other)
 

time: 131 us -> 131 us (level)
  waiting for transfers between devices: 53.2 us -> 44.3 us
  starting transfers between devices: 40.9 us -> 47 us
  local copies, waits for them, and re-layouts: 10.7 us -> 12.3 us
    ppermute x26, waiting for transfers between devices: 53.2 us -> 44.3 us  [send(): return lax.ppermute(a, axes, perm)]
    ppermute x26, starting transfers between devices: 40.9 us -> 47 us  [send(): return lax.ppermute(a, axes, perm)]
    unnamed x13 -> x27, local copies, waits for them, and re-layouts: 2.42 us -> 4.58 us
    another operation x4, other arithmetic: 1.38 us -> 0.06 us  [on_device(): lists = jnp.stack([slot_lower, slot_upper, source_block, x_first, y_first])]
  transfers between devices with their start and end apart: 26 -> 26, of which waited for: 16 -> 15; matrix products, arithmetic and copies ran while one was open for 8% -> 8% of each run, Pallas kernels for 5% -> 5%
where the time goes in v4:
time: 131 us; the launch traced here: 130 us
  starting transfers between devices  47 us (36%)
  waiting for transfers between devices  44.3 us (34%)
  Pallas kernels  22.5 us (17%)
  local copies, waits for them, and re-layouts  12.3 us (9%)
  other arithmetic  3.87 us (3%)
    ppermute x26, starting transfers between devices, send(): return lax.ppermute(a, axes, perm)  47 us
    ppermute x26, waiting for transfers between devices, send(): return lax.ppermute(a, axes, perm)  44.3 us
    pallas_call x1, Pallas kernels, on_device(): pl.pallas_call(second_kernel, out_shape=sums_shape, in_specs=[smem] + [vm...  10.4 us
    reshape x1, local copies, waits for them, and re-layouts, on_device(): right_own = right_env.reshape(nb, side, wide)  7.31 us
    pallas_call x1, Pallas kernels, on_device(): pl.pallas_call(product_kernel, out_shape=[jax.ShapeDtypeStruct((wide, blo...  6.08 us
    pallas_call x1, Pallas kernels, on_device(): pl.pallas_call(first_kernel, out_shape=sums_shape + [jax.ShapeDtypeStruct...  6.03 us
    unnamed x27, local copies, waits for them, and re-layouts  4.58 us
  transfers between devices with their start and end apart: 26, of which 15 were waited for; matrix products, arithmetic and copies ran while one was open for 8% of the time, Pallas kernels for 5%

profile of v4, /device:TPU:1, one launch (start us, length us, event | category | flops | bytes accessed | tf_op | source)
XLA Modules:
  0.0 130.2 jit_solution(17400116254002024644)
XLA Ops:
  0.0 1.2 copy-done
  1.3 0.2 copy.12
  1.5 0.0 copy-start.7
  1.6 0.0 copy-start.10
  1.6 3.9 %collective-permute-start = (bf16[64,1408]{1,0:T(8,128)(2,1)S(1)}, bf16[64,1408]{1,0:T(8,128)(2,1)S(1)}, u32[]{:S(2)}, u32[]{:S(2)}) collective-permute-start(bf16[64,1408]{1,0:T(8,128)(2,1)S(1)} %pad_dynamic-slice_fusion), channel_id=1, source_target_pairs={{0,192},{1,65},{2,194},{3,67},{4,196},{5,69},{6,70},{7,199},{8,72}... | collective-permute-start | bytes 540680 | tf_op jit(solution)/shard_map/ppermute | solution.py:55
  5.5 4.0 %collective-permute-start.1 = (bf16[4,128,128]{2,1,0:T(8,128)(2,1)}, bf16[4,128,128]{2,1,0:T(8,128)(2,1)S(1)}, u32[]{:S(2)}, u32[]{:S(2)}) collective-permute-start(bf16[4,128,128]{2,1,0:T(8,128)(2,1)} %param.9), channel_id=1, source_target_pairs={{0,1},{1,0},{2,3},{3,2},{4,5},{5,4},{6,7},{7,6},{8,9},{9,8},{10,11... | collective-permute-start | bytes 393224 | tf_op jit(solution)/shard_map/ppermute | solution.py:55
  9.5 7.3 %reshape.215.right_own = bf16[4,128,4096]{2,1,0:T(8,128)(2,1)} reshape(bf16[4,128,32,128]{3,2,1,0:T(8,128)(2,1)} %param.10) | data formatting | bytes 8388608 | tf_op jit(solution)/shard_map/reshape | solution.py:214
  16.8 0.1 collective-permute-start.5
  16.9 0.1 select_add_fusion.1
  17.0 0.1 add.252
  17.1 0.1 add.256
  17.2 3.7 %collective-permute-start.4 = (bf16[64,1408]{1,0:T(8,128)(2,1)S(1)}, bf16[64,1408]{1,0:T(8,128)(2,1)S(1)}, u32[]{:S(2)}, u32[]{:S(2)}) collective-permute-start(bf16[64,1408]{1,0:T(8,128)(2,1)S(1)} %collective-permute-done), channel_id=1, source_target_pairs={{0,6},{1,25},{2,0},{3,27},{4,2},{5,29},{6,4},{7,31},{8,14},{9,1},{... | collective-permute-start | bytes 540680 | tf_op jit(solution)/shard_map/ppermute | solution.py:55
  20.9 0.1 pad.12.clone
  21.0 0.1 collective-permute-start.3
  21.0 0.6 collective-permute-start.2
  21.6 4.0 %collective-permute-start.7 = (bf16[64,4096]{1,0:T(8,128)(2,1)S(1)}, bf16[64,4096]{1,0:T(8,128)(2,1)S(1)}, u32[]{:S(2)}, u32[]{:S(2)}) collective-permute-start(bf16[64,4096]{1,0:T(8,128)(2,1)S(1)} %bitcast.23), channel_id=1, source_target_pairs={{0,224},{1,225},{2,226},{3,227},{4,228},{5,229},{6,230},{7,231},{8... | collective-permute-start | bytes 1572872 | tf_op jit(solution)/shard_map/ppermute | solution.py:55
  25.6 0.8 collective-permute-start.6
  26.4 0.7 broadcast_select_fusion.2
  27.1 1.8 %collective-permute-done.2 = bf16[64,1408]{1,0:T(8,128)(2,1)S(1)} collective-permute-done((bf16[64,1408]{1,0:T(8,128)(2,1)S(1)}, bf16[64,1408]{1,0:T(8,128)(2,1)S(1)}, u32[]{:S(2)}, u32[]{:S(2)}) %collective-permute-start.2) | collective-permute-done | bytes 180256 | tf_op jit(solution)/shard_map/ppermute | solution.py:55
  28.9 1.1 pad_maximum_fusion.part0
  30.0 2.8 %collective-permute-start.10 = (bf16[4,64,1408]{2,1,0:T(8,128)(2,1)S(1)}, bf16[4,64,1408]{2,1,0:T(8,128)(2,1)}, u32[]{:S(2)}, u32[]{:S(2)}) collective-permute-start(bf16[4,64,1408]{2,1,0:T(8,128)(2,1)S(1)} %pad_maximum_fusion.part0), channel_id=1, source_target_pairs={{0,16},{1,5},{2,18},{3,7},{4,20},{5,1},{6,22},{7,3},{8,24},{9,13},... | collective-permute-start | bytes 2162696 | tf_op jit(solution)/shard_map/ppermute | solution.py:55
  32.9 0.3 collective-permute-start.9
  33.2 2.1 %collective-permute-done.7.above = bf16[64,4096]{1,0:T(8,128)(2,1)S(1)} collective-permute-done((bf16[64,4096]{1,0:T(8,128)(2,1)S(1)}, bf16[64,4096]{1,0:T(8,128)(2,1)S(1)}, u32[]{:S(2)}, u32[]{:S(2)}) %collective-permute-start.7) | collective-permute-done | bytes 524320 | tf_op jit(solution)/shard_map/ppermute | solution.py:55
  35.3 3.8 %collective-permute-done.6.below = bf16[64,4096]{1,0:T(8,128)(2,1)S(1)} collective-permute-done((bf16[64,4096]{1,0:T(8,128)(2,1)S(1)}, bf16[64,4096]{1,0:T(8,128)(2,1)S(1)}, u32[]{:S(2)}, u32[]{:S(2)}) %collective-permute-start.6) | collective-permute-done | bytes 524320 | tf_op jit(solution)/shard_map/ppermute | solution.py:55
  39.2 0.1 collective-permute-start.8
  39.3 2.9 %collective-permute-start.11 = (bf16[4,64,1408]{2,1,0:T(8,128)(2,1)S(1)}, bf16[4,64,1408]{2,1,0:T(8,128)(2,1)S(1)}, u32[]{:S(2)}, u32[]{:S(2)}) collective-permute-start(bf16[4,64,1408]{2,1,0:T(8,128)(2,1)S(1)} %pad_maximum_fusion.part0), channel_id=1, source_target_pairs={{0,24},{1,7},{2,26},{3,1},{4,28},{5,3},{6,30},{7,5},{8,0},{9,15},{... | collective-permute-start | bytes 2162696 | tf_op jit(solution)/shard_map/ppermute | solution.py:55
  42.2 2.2 %copy-done.1 = bf16[4,128,4096]{2,1,0:T(8,128)(2,1)S(1)} copy-done((bf16[4,128,4096]{2,1,0:T(8,128)(2,1)S(1)}, bf16[4,128,4096]{2,1,0:T(8,128)(2,1)}, u32[]{:S(2)}) %copy-start.1) | copy-done | bytes 4194328
  44.4 0.9 copy-done.3
  45.3 6.1 %product.1 = (bf16[4096,1024]{1,0:T(8,128)(2,1)S(1)}, bf16[8,192,128]{2,1,0:T(8,128)(2,1)S(1)}) custom-call(s32[1]{0:T(128)} %bitcast.10.core, bf16[8,64,128]{2,1,0:T(8,128)(2,1)S(1)} %get-tuple-element.66.own_rows, bf16[8,64,128]{2,1,0:T(8,128)(2,1)S(1)} %copy-done.3, bf16[4,128,4096]{2,1,0:T(8,128)(2,1)S(1)} %copy-done.1, ...), custom_call_target="tpu_custom_call" | custom-call | flops 2684354560 | tf_op jit(solution)/shard_map/product/pallas_call | solution.py:277
  51.4 0.1 broadcast_add_fusion
  51.5 0.1 pad_add_fusion
  51.6 0.1 add_add_fusion.pairs
  51.7 6.0 %contract_first.1 = (bf16[32,64,128]{2,1,0:T(8,128)(2,1)S(1)}, bf16[32,64,128]{2,1,0:T(8,128)(2,1)S(1)}, bf16[32,64,128]{2,1,0:T(8,128)(2,1)S(1)}, bf16[32,64,128]{2,1,0:T(8,128)(2,1)S(1)}, bf16[576,4224]{1,0:T(8,128)(2,1)S(1)}) custom-call(s32[4,64]{1,0:T(4,128)S(1)} %add_add_fusion.pairs, s32[2,16]{1,0:T(2,128)S(1)} %pad_add_fusion.1.places, ...), custom_call_target="tpu_custom_call" | custom-call | flops 2684354560 | tf_op jit(solution)/shard_map/contract_first/pallas_call | solution.py:295
  57.7 3.8 %collective-permute-start.12 = (bf16[32,64,128]{2,1,0:T(8,128)(2,1)S(1)}, bf16[32,64,128]{2,1,0:T(8,128)(2,1)S(1)}, u32[]{:S(2)}, u32[]{:S(2)}) collective-permute-start(bf16[32,64,128]{2,1,0:T(8,128)(2,1)S(1)} %get-tuple-element.43), channel_id=1, source_target_pairs={{0,2},{1,9},{2,4},{3,11},{4,6},{5,13},{6,0},{7,15},{8,10},{9,17},{... | collective-permute-start | bytes 1572872 | tf_op jit(solution)/shard_map/ppermute | solution.py:55
  61.5 3.5 %collective-permute-start.13 = (bf16[32,64,128]{2,1,0:T(8,128)(2,1)S(1)}, bf16[32,64,128]{2,1,0:T(8,128)(2,1)S(1)}, u32[]{:S(2)}, u32[]{:S(2)}) collective-permute-start(bf16[32,64,128]{2,1,0:T(8,128)(2,1)S(1)} %get-tuple-element.44), channel_id=1, source_target_pairs={{0,4},{1,17},{2,6},{3,19},{4,0},{5,21},{6,2},{7,23},{8,12},{9,25},... | collective-permute-start | bytes 1572872 | tf_op jit(solution)/shard_map/ppermute | solution.py:55
  65.0 5.7 %collective-permute-done.12 = bf16[32,64,128]{2,1,0:T(8,128)(2,1)S(1)} collective-permute-done((bf16[32,64,128]{2,1,0:T(8,128)(2,1)S(1)}, bf16[32,64,128]{2,1,0:T(8,128)(2,1)S(1)}, u32[]{:S(2)}, u32[]{:S(2)}) %collective-permute-start.12) | collective-permute-done | bytes 524320 | tf_op jit(solution)/shard_map/ppermute | solution.py:55
  70.7 6.8 %collective-permute-done.13 = bf16[32,64,128]{2,1,0:T(8,128)(2,1)S(1)} collective-permute-done((bf16[32,64,128]{2,1,0:T(8,128)(2,1)S(1)}, bf16[32,64,128]{2,1,0:T(8,128)(2,1)S(1)}, u32[]{:S(2)}, u32[]{:S(2)}) %collective-permute-start.13) | collective-permute-done | bytes 524320 | tf_op jit(solution)/shard_map/ppermute | solution.py:55
  77.5 0.4 add_convert_fusion.1
  77.9 0.1 collective-permute-start.15
  77.9 2.7 %collective-permute-start.17 = (bf16[8,64,128]{2,1,0:T(8,128)(2,1)S(1)}, bf16[8,64,128]{2,1,0:T(8,128)(2,1)S(1)}, u32[]{:S(2)}, u32[]{:S(2)}) collective-permute-start(bf16[8,64,128]{2,1,0:T(8,128)(2,1)S(1)} %get-tuple-element.63), channel_id=1, source_target_pairs={{0,24},{1,7},{2,26},{3,1},{4,28},{5,3},{6,30},{7,5},{8,0},{9,15},{... | collective-permute-start | bytes 393224 | tf_op jit(solution)/shard_map/ppermute | solution.py:55
  80.6 0.4 collective-permute-start.16
  81.0 2.0 %collective-permute-done.15 = bf16[8,64,128]{2,1,0:T(8,128)(2,1)S(1)} collective-permute-done((bf16[8,64,128]{2,1,0:T(8,128)(2,1)S(1)}, bf16[8,64,128]{2,1,0:T(8,128)(2,1)S(1)}, u32[]{:S(2)}, u32[]{:S(2)}) %collective-permute-start.15) | collective-permute-done | bytes 131104 | tf_op jit(solution)/shard_map/ppermute | solution.py:55
  83.0 1.0 collective-permute-done.17
  83.9 2.0 %collective-permute-done.16 = bf16[8,64,128]{2,1,0:T(8,128)(2,1)S(1)} collective-permute-done((bf16[8,64,128]{2,1,0:T(8,128)(2,1)S(1)}, bf16[8,64,128]{2,1,0:T(8,128)(2,1)S(1)}, u32[]{:S(2)}, u32[]{:S(2)}) %collective-permute-start.16) | collective-permute-done | bytes 131104 | tf_op jit(solution)/shard_map/ppermute | solution.py:55
  85.9 0.1 subtract_convert_fusion.1.own_rows
  86.0 3.4 %collective-permute-start.18 = (bf16[8,64,128]{2,1,0:T(8,128)(2,1)S(1)}, bf16[8,64,128]{2,1,0:T(8,128)(2,1)S(1)}, u32[]{:S(2)}, u32[]{:S(2)}) collective-permute-start(bf16[8,64,128]{2,1,0:T(8,128)(2,1)S(1)} %subtract_convert_fusion.1.own_rows), channel_id=1, source_target_pairs={{0,1},{1,0},{2,3},{3,2},{4,5},{5,4},{6,7},{7,6},{8,9},{9,8},{10,11... | collective-permute-start | bytes 393224 | tf_op jit(solution)/shard_map/ppermute | solution.py:55
  89.5 1.0 collective-permute-done.18.other_rows
  90.5 10.4 %contract_second.1 = (bf16[32,64,128]{2,1,0:T(8,128)(2,1)S(1)}, bf16[32,64,128]{2,1,0:T(8,128)(2,1)S(1)}, bf16[32,64,128]{2,1,0:T(8,128)(2,1)S(1)}, bf16[32,64,128]{2,1,0:T(8,128)(2,1)S(1)}) custom-call(s32[4,64]{1,0:T(4,128)S(1)} %add_add_fusion.pairs, bf16[8,64,128]{2,1,0:T(8,128)(2,1)S(1)} %subtract_convert_fusion.1.own_rows, ...), custom_call_target="tpu_custom_call" | custom-call | flops 5368709120 | tf_op jit(solution)/shard_map/contract_second/pallas_call | solution.py:310
  100.8 0.3 collective-permute-start.19
  101.2 2.5 %collective-permute-start.20 = (bf16[32,64,128]{2,1,0:T(8,128)(2,1)S(1)}, bf16[32,64,128]{2,1,0:T(8,128)(2,1)S(1)}, u32[]{:S(2)}, u32[]{:S(2)}) collective-permute-start(bf16[32,64,128]{2,1,0:T(8,128)(2,1)S(1)} %get-tuple-element.49), channel_id=1, source_target_pairs={{0,4},{1,17},{2,6},{3,19},{4,0},{5,21},{6,2},{7,23},{8,12},{9,25},... | collective-permute-start | bytes 1572872 | tf_op jit(solution)/shard_map/ppermute | solution.py:55
  103.6 0.3 collective-permute-start.21
  104.0 6.5 %collective-permute-done.19 = bf16[32,64,128]{2,1,0:T(8,128)(2,1)S(1)} collective-permute-done((bf16[32,64,128]{2,1,0:T(8,128)(2,1)S(1)}, bf16[32,64,128]{2,1,0:T(8,128)(2,1)S(1)}, u32[]{:S(2)}, u32[]{:S(2)}) %collective-permute-start.19) | collective-permute-done | bytes 524320 | tf_op jit(solution)/shard_map/ppermute | solution.py:55
  110.4 5.7 %collective-permute-done.20 = bf16[32,64,128]{2,1,0:T(8,128)(2,1)S(1)} collective-permute-done((bf16[32,64,128]{2,1,0:T(8,128)(2,1)S(1)}, bf16[32,64,128]{2,1,0:T(8,128)(2,1)S(1)}, u32[]{:S(2)}, u32[]{:S(2)}) %collective-permute-start.20) | collective-permute-done | bytes 524320 | tf_op jit(solution)/shard_map/ppermute | solution.py:55
  116.1 0.6 collective-permute-done.21
  116.7 0.4 add_convert_fusion
  117.1 1.1 collective-permute-start.22
  118.2 1.7 %collective-permute-start.24 = (bf16[8,64,128]{2,1,0:T(8,128)(2,1)S(1)}, bf16[8,64,128]{2,1,0:T(8,128)(2,1)S(1)}, u32[]{:S(2)}, u32[]{:S(2)}) collective-permute-start(bf16[8,64,128]{2,1,0:T(8,128)(2,1)S(1)} %get-tuple-element.60), channel_id=1, source_target_pairs={{0,24},{1,7},{2,26},{3,1},{4,28},{5,3},{6,30},{7,5},{8,0},{9,15},{... | collective-permute-start | bytes 393224 | tf_op jit(solution)/shard_map/ppermute | solution.py:55
  119.8 0.8 collective-permute-start.23
  120.6 1.6 %collective-permute-done.22 = bf16[8,64,128]{2,1,0:T(8,128)(2,1)S(1)} collective-permute-done((bf16[8,64,128]{2,1,0:T(8,128)(2,1)S(1)}, bf16[8,64,128]{2,1,0:T(8,128)(2,1)S(1)}, u32[]{:S(2)}, u32[]{:S(2)}) %collective-permute-start.22) | collective-permute-done | bytes 131104 | tf_op jit(solution)/shard_map/ppermute | solution.py:55
  122.2 3.0 %collective-permute-done.23 = bf16[8,64,128]{2,1,0:T(8,128)(2,1)S(1)} collective-permute-done((bf16[8,64,128]{2,1,0:T(8,128)(2,1)S(1)}, bf16[8,64,128]{2,1,0:T(8,128)(2,1)S(1)}, u32[]{:S(2)}, u32[]{:S(2)}) %collective-permute-start.23) | collective-permute-done | bytes 131104 | tf_op jit(solution)/shard_map/ppermute | solution.py:55
  125.2 0.1 subtract_convert_fusion
  125.3 3.3 %collective-permute-start.25 = (bf16[4,64,128]{2,1,0:T(8,128)(2,1)S(1)}, bf16[4,64,128]{2,1,0:T(8,128)(2,1)S(1)}, u32[]{:S(2)}, u32[]{:S(2)}) collective-permute-start(bf16[4,64,128]{2,1,0:T(8,128)(2,1)S(1)} %broadcast_select_fusion.6), channel_id=1, source_target_pairs={{0,1},{1,0},{2,3},{3,2},{4,5},{5,4},{6,7},{7,6},{8,9},{9,8},{10,11... | collective-permute-start | bytes 196616 | tf_op jit(solution)/shard_map/ppermute | solution.py:55
  128.6 0.9 collective-permute-done.25
  129.5 0.7 pad_maximum_fusion.2
  (49 shorter events, 0.4 us)
Async XLA Ops:
  0.0 1.2 copy-start
  1.5 15.4 %copy-start.7 = (s32[4]{0:T(128)S(1)}, s32[4]{0:T(128)}, u32[]{:S(2)}) copy-start(s32[4]{0:T(128)} %constant.176.clone) | copy-start | bytes 52
  1.5 24.8 %copy-start.6 = (bf16[4,128,128]{2,1,0:T(8,128)(2,1)S(1)}, bf16[4,128,128]{2,1,0:T(8,128)(2,1)}, u32[]{:S(2)}) copy-start(bf16[4,128,128]{2,1,0:T(8,128)(2,1)} %param.9) | copy-start | bytes 393220
  1.5 37.5 %copy-start.9 = (s32[32]{0:T(128)S(1)}, s32[32]{0:T(128)}, u32[]{:S(2)}) copy-start(s32[32]{0:T(128)} %param.12) | copy-start | bytes 388
  1.6 37.5 %copy-start.10 = (s32[32]{0:T(128)S(1)}, s32[32]{0:T(128)}, u32[]{:S(2)}) copy-start(s32[32]{0:T(128)} %param.14) | copy-start | bytes 388
  1.6 37.5 %copy-start.11 = (s32[32]{0:T(128)S(1)}, s32[32]{0:T(128)}, u32[]{:S(2)}) copy-start(s32[32]{0:T(128)} %param.15) | copy-start | bytes 388
  1.6 37.6 %copy-start.12 = (s32[32]{0:T(128)S(1)}, s32[32]{0:T(128)}, u32[]{:S(2)}) copy-start(s32[32]{0:T(128)} %param.13) | copy-start | bytes 388
  1.6 15.2 %collective-permute-start = (bf16[64,1408]{1,0:T(8,128)(2,1)S(1)}, bf16[64,1408]{1,0:T(8,128)(2,1)S(1)}, u32[]{:S(2)}, u32[]{:S(2)}) collective-permute-start(bf16[64,1408]{1,0:T(8,128)(2,1)S(1)} %pad_dynamic-slice_fusion), channel_id=1, source_target_pairs={{0,192},{1,65},{2,194},{3,67},{4,196},{5,69},{6,70},{7,199},{8,72}... | collective-permute-start | bytes 540680 | tf_op jit(solution)/shard_map/ppermute | solution.py:55
  5.5 11.3 %collective-permute-start.1 = (bf16[4,128,128]{2,1,0:T(8,128)(2,1)}, bf16[4,128,128]{2,1,0:T(8,128)(2,1)S(1)}, u32[]{:S(2)}, u32[]{:S(2)}) collective-permute-start(bf16[4,128,128]{2,1,0:T(8,128)(2,1)} %param.9), channel_id=1, source_target_pairs={{0,1},{1,0},{2,3},{3,2},{4,5},{5,4},{6,7},{7,6},{8,9},{9,8},{10,11... | collective-permute-start | bytes 393224 | tf_op jit(solution)/shard_map/ppermute | solution.py:55
  16.8 12.1 %copy-start.4 = (bf16[64,1408]{1,0:T(8,128)(2,1)}, bf16[64,1408]{1,0:T(8,128)(2,1)S(1)}, u32[]{:S(2)}) copy-start(bf16[64,1408]{1,0:T(8,128)(2,1)S(1)} %collective-permute-done) | copy-start | bytes 540676
  16.8 13.2 %collective-permute-start.5 = (bf16[4,128,4096]{2,1,0:T(8,128)(2,1)}, bf16[4,128,4096]{2,1,0:T(8,128)(2,1)}, u32[]{:S(2)}, u32[]{:S(2)}) collective-permute-start(bf16[4,128,4096]{2,1,0:T(8,128)(2,1)} %reshape.215.right_own), channel_id=1, source_target_pairs={{0,1},{1,0},{2,3},{3,2},{4,5},{5,4},{6,7},{7,6},{8,9},{9,8},{10,11... | collective-permute-start | bytes 12582920 | tf_op jit(solution)/shard_map/ppermute | solution.py:55
  17.2 8.4 %collective-permute-start.4 = (bf16[64,1408]{1,0:T(8,128)(2,1)S(1)}, bf16[64,1408]{1,0:T(8,128)(2,1)S(1)}, u32[]{:S(2)}, u32[]{:S(2)}) collective-permute-start(bf16[64,1408]{1,0:T(8,128)(2,1)S(1)} %collective-permute-done), channel_id=1, source_target_pairs={{0,6},{1,25},{2,0},{3,27},{4,2},{5,29},{6,4},{7,31},{8,14},{9,1},{... | collective-permute-start | bytes 540680 | tf_op jit(solution)/shard_map/ppermute | solution.py:55
  21.0 6.1 %collective-permute-start.3 = (bf16[64,1408]{1,0:T(8,128)(2,1)S(1)}, bf16[64,1408]{1,0:T(8,128)(2,1)S(1)}, u32[]{:S(2)}, u32[]{:S(2)}) collective-permute-start(bf16[64,1408]{1,0:T(8,128)(2,1)S(1)} %collective-permute-done), channel_id=1, source_target_pairs={{0,4},{1,17},{2,6},{3,19},{4,0},{5,21},{6,2},{7,23},{8,12},{9,25},... | collective-permute-start | bytes 540680 | tf_op jit(solution)/shard_map/ppermute | solution.py:55
  21.0 7.9 %collective-permute-start.2 = (bf16[64,1408]{1,0:T(8,128)(2,1)S(1)}, bf16[64,1408]{1,0:T(8,128)(2,1)S(1)}, u32[]{:S(2)}, u32[]{:S(2)}) collective-permute-start(bf16[64,1408]{1,0:T(8,128)(2,1)S(1)} %collective-permute-done), channel_id=1, source_target_pairs={{0,2},{1,9},{2,4},{3,11},{4,6},{5,13},{6,0},{7,15},{8,10},{9,17},{... | collective-permute-start | bytes 540680 | tf_op jit(solution)/shard_map/ppermute | solution.py:55
  21.6 13.6 %collective-permute-start.7 = (bf16[64,4096]{1,0:T(8,128)(2,1)S(1)}, bf16[64,4096]{1,0:T(8,128)(2,1)S(1)}, u32[]{:S(2)}, u32[]{:S(2)}) collective-permute-start(bf16[64,4096]{1,0:T(8,128)(2,1)S(1)} %bitcast.23), channel_id=1, source_target_pairs={{0,224},{1,225},{2,226},{3,227},{4,228},{5,229},{6,230},{7,231},{8... | collective-permute-start | bytes 1572872 | tf_op jit(solution)/shard_map/ppermute | solution.py:55
  25.6 3.3 %copy-start.5 = (bf16[64,1408]{1,0:T(8,128)(2,1)}, bf16[64,1408]{1,0:T(8,128)(2,1)S(1)}, u32[]{:S(2)}) copy-start(bf16[64,1408]{1,0:T(8,128)(2,1)S(1)} %collective-permute-done.4) | copy-start | bytes 540676
  25.6 13.5 %collective-permute-start.6 = (bf16[64,4096]{1,0:T(8,128)(2,1)S(1)}, bf16[64,4096]{1,0:T(8,128)(2,1)S(1)}, u32[]{:S(2)}, u32[]{:S(2)}) collective-permute-start(bf16[64,4096]{1,0:T(8,128)(2,1)S(1)} %bitcast.24), channel_id=1, source_target_pairs={{0,32},{1,33},{2,34},{3,35},{4,36},{5,37},{6,38},{7,39},{8,40},{9,... | collective-permute-start | bytes 1572872 | tf_op jit(solution)/shard_map/ppermute | solution.py:55
  30.0 21.6 %collective-permute-start.10 = (bf16[4,64,1408]{2,1,0:T(8,128)(2,1)S(1)}, bf16[4,64,1408]{2,1,0:T(8,128)(2,1)}, u32[]{:S(2)}, u32[]{:S(2)}) collective-permute-start(bf16[4,64,1408]{2,1,0:T(8,128)(2,1)S(1)} %pad_maximum_fusion.part0), channel_id=1, source_target_pairs={{0,16},{1,5},{2,18},{3,7},{4,20},{5,1},{6,22},{7,3},{8,24},{9,13},... | collective-permute-start | bytes 2162696 | tf_op jit(solution)/shard_map/ppermute | solution.py:55
  32.9 18.8 %collective-permute-start.9 = (bf16[4,64,1408]{2,1,0:T(8,128)(2,1)S(1)}, bf16[4,64,1408]{2,1,0:T(8,128)(2,1)}, u32[]{:S(2)}, u32[]{:S(2)}) collective-permute-start(bf16[4,64,1408]{2,1,0:T(8,128)(2,1)S(1)} %pad_maximum_fusion.part0), channel_id=1, source_target_pairs={{0,8},{1,3},{2,10},{3,5},{4,12},{5,7},{6,14},{7,1},{8,16},{9,11},{... | collective-permute-start | bytes 2162696 | tf_op jit(solution)/shard_map/ppermute | solution.py:55
  39.2 12.2 %collective-permute-start.8 = (s32[5,32]{1,0:T(8,128)S(1)}, s32[5,32]{1,0:T(8,128)S(1)}, u32[]{:S(2)}, u32[]{:S(2)}) collective-permute-start(s32[5,32]{1,0:T(8,128)S(1)} %stack.53), channel_id=1, source_target_pairs={{0,1},{1,0},{2,3},{3,2},{4,5},{5,4},{6,7},{7,6},{8,9},{9,8},{10,11... | collective-permute-start | bytes 1928 | tf_op jit(solution)/shard_map/ppermute | solution.py:55
  39.3 12.3 %collective-permute-start.11 = (bf16[4,64,1408]{2,1,0:T(8,128)(2,1)S(1)}, bf16[4,64,1408]{2,1,0:T(8,128)(2,1)S(1)}, u32[]{:S(2)}, u32[]{:S(2)}) collective-permute-start(bf16[4,64,1408]{2,1,0:T(8,128)(2,1)S(1)} %pad_maximum_fusion.part0), channel_id=1, source_target_pairs={{0,24},{1,7},{2,26},{3,1},{4,28},{5,3},{6,30},{7,5},{8,0},{9,15},{... | collective-permute-start | bytes 2162696 | tf_op jit(solution)/shard_map/ppermute | solution.py:55
  42.2 2.2 %copy-start.1 = (bf16[4,128,4096]{2,1,0:T(8,128)(2,1)S(1)}, bf16[4,128,4096]{2,1,0:T(8,128)(2,1)}, u32[]{:S(2)}) copy-start(bf16[4,128,4096]{2,1,0:T(8,128)(2,1)} %reshape.215.right_own) | copy-start | bytes 12582916
  44.4 0.9 copy-start.3
  45.3 6.1 %copy-start.8 = (s32[5]{0:T(128)S(1)}, s32[5]{0:T(128)}, u32[]{:S(2)}) copy-start(s32[5]{0:T(128)} %constant.187) | copy-start | bytes 64
  57.7 32.8 %copy-start.2 = (bf16[4,128,4096]{2,1,0:T(8,128)(2,1)S(1)}, bf16[4,128,4096]{2,1,0:T(8,128)(2,1)}, u32[]{:S(2)}) copy-start(bf16[4,128,4096]{2,1,0:T(8,128)(2,1)} %reshape.215.right_own) | copy-start | bytes 12582916
  57.7 12.9 %collective-permute-start.12 = (bf16[32,64,128]{2,1,0:T(8,128)(2,1)S(1)}, bf16[32,64,128]{2,1,0:T(8,128)(2,1)S(1)}, u32[]{:S(2)}, u32[]{:S(2)}) collective-permute-start(bf16[32,64,128]{2,1,0:T(8,128)(2,1)S(1)} %get-tuple-element.43), channel_id=1, source_target_pairs={{0,2},{1,9},{2,4},{3,11},{4,6},{5,13},{6,0},{7,15},{8,10},{9,17},{... | collective-permute-start | bytes 1572872 | tf_op jit(solution)/shard_map/ppermute | solution.py:55
  61.5 16.0 %collective-permute-start.13 = (bf16[32,64,128]{2,1,0:T(8,128)(2,1)S(1)}, bf16[32,64,128]{2,1,0:T(8,128)(2,1)S(1)}, u32[]{:S(2)}, u32[]{:S(2)}) collective-permute-start(bf16[32,64,128]{2,1,0:T(8,128)(2,1)S(1)} %get-tuple-element.44), channel_id=1, source_target_pairs={{0,4},{1,17},{2,6},{3,19},{4,0},{5,21},{6,2},{7,23},{8,12},{9,25},... | collective-permute-start | bytes 1572872 | tf_op jit(solution)/shard_map/ppermute | solution.py:55
  65.0 12.5 %collective-permute-start.14 = (bf16[32,64,128]{2,1,0:T(8,128)(2,1)S(1)}, bf16[32,64,128]{2,1,0:T(8,128)(2,1)S(1)}, u32[]{:S(2)}, u32[]{:S(2)}) collective-permute-start(bf16[32,64,128]{2,1,0:T(8,128)(2,1)S(1)} %get-tuple-element.45), channel_id=1, source_target_pairs={{0,6},{1,25},{2,0},{3,27},{4,2},{5,29},{6,4},{7,31},{8,14},{9,1},{... | collective-permute-start | bytes 1572872 | tf_op jit(solution)/shard_map/ppermute | solution.py:55
  77.9 5.1 %collective-permute-start.15 = (bf16[8,64,128]{2,1,0:T(8,128)(2,1)S(1)}, bf16[8,64,128]{2,1,0:T(8,128)(2,1)S(1)}, u32[]{:S(2)}, u32[]{:S(2)}) collective-permute-start(bf16[8,64,128]{2,1,0:T(8,128)(2,1)S(1)} %get-tuple-element.62), channel_id=1, source_target_pairs={{0,8},{1,3},{2,10},{3,5},{4,12},{5,7},{6,14},{7,1},{8,16},{9,11},{... | collective-permute-start | bytes 393224 | tf_op jit(solution)/shard_map/ppermute | solution.py:55
  77.9 6.0 %collective-permute-start.17 = (bf16[8,64,128]{2,1,0:T(8,128)(2,1)S(1)}, bf16[8,64,128]{2,1,0:T(8,128)(2,1)S(1)}, u32[]{:S(2)}, u32[]{:S(2)}) collective-permute-start(bf16[8,64,128]{2,1,0:T(8,128)(2,1)S(1)} %get-tuple-element.63), channel_id=1, source_target_pairs={{0,24},{1,7},{2,26},{3,1},{4,28},{5,3},{6,30},{7,5},{8,0},{9,15},{... | collective-permute-start | bytes 393224 | tf_op jit(solution)/shard_map/ppermute | solution.py:55
  80.6 5.3 %collective-permute-start.16 = (bf16[8,64,128]{2,1,0:T(8,128)(2,1)S(1)}, bf16[8,64,128]{2,1,0:T(8,128)(2,1)S(1)}, u32[]{:S(2)}, u32[]{:S(2)}) collective-permute-start(bf16[8,64,128]{2,1,0:T(8,128)(2,1)S(1)} %get-tuple-element.64), channel_id=1, source_target_pairs={{0,16},{1,5},{2,18},{3,7},{4,20},{5,1},{6,22},{7,3},{8,24},{9,13},... | collective-permute-start | bytes 393224 | tf_op jit(solution)/shard_map/ppermute | solution.py:55
  86.0 4.4 %collective-permute-start.18 = (bf16[8,64,128]{2,1,0:T(8,128)(2,1)S(1)}, bf16[8,64,128]{2,1,0:T(8,128)(2,1)S(1)}, u32[]{:S(2)}, u32[]{:S(2)}) collective-permute-start(bf16[8,64,128]{2,1,0:T(8,128)(2,1)S(1)} %subtract_convert_fusion.1.own_rows), channel_id=1, source_target_pairs={{0,1},{1,0},{2,3},{3,2},{4,5},{5,4},{6,7},{7,6},{8,9},{9,8},{10,11... | collective-permute-start | bytes 393224 | tf_op jit(solution)/shard_map/ppermute | solution.py:55
  100.8 9.6 %collective-permute-start.19 = (bf16[32,64,128]{2,1,0:T(8,128)(2,1)S(1)}, bf16[32,64,128]{2,1,0:T(8,128)(2,1)S(1)}, u32[]{:S(2)}, u32[]{:S(2)}) collective-permute-start(bf16[32,64,128]{2,1,0:T(8,128)(2,1)S(1)} %get-tuple-element.48), channel_id=1, source_target_pairs={{0,2},{1,9},{2,4},{3,11},{4,6},{5,13},{6,0},{7,15},{8,10},{9,17},{... | collective-permute-start | bytes 1572872 | tf_op jit(solution)/shard_map/ppermute | solution.py:55
  101.2 14.9 %collective-permute-start.20 = (bf16[32,64,128]{2,1,0:T(8,128)(2,1)S(1)}, bf16[32,64,128]{2,1,0:T(8,128)(2,1)S(1)}, u32[]{:S(2)}, u32[]{:S(2)}) collective-permute-start(bf16[32,64,128]{2,1,0:T(8,128)(2,1)S(1)} %get-tuple-element.49), channel_id=1, source_target_pairs={{0,4},{1,17},{2,6},{3,19},{4,0},{5,21},{6,2},{7,23},{8,12},{9,25},... | collective-permute-start | bytes 1572872 | tf_op jit(solution)/shard_map/ppermute | solution.py:55
  103.6 13.1 %collective-permute-start.21 = (bf16[32,64,128]{2,1,0:T(8,128)(2,1)S(1)}, bf16[32,64,128]{2,1,0:T(8,128)(2,1)S(1)}, u32[]{:S(2)}, u32[]{:S(2)}) collective-permute-start(bf16[32,64,128]{2,1,0:T(8,128)(2,1)S(1)} %get-tuple-element.50), channel_id=1, source_target_pairs={{0,6},{1,25},{2,0},{3,27},{4,2},{5,29},{6,4},{7,31},{8,14},{9,1},{... | collective-permute-start | bytes 1572872 | tf_op jit(solution)/shard_map/ppermute | solution.py:55
  117.1 5.1 %collective-permute-start.22 = (bf16[8,64,128]{2,1,0:T(8,128)(2,1)S(1)}, bf16[8,64,128]{2,1,0:T(8,128)(2,1)S(1)}, u32[]{:S(2)}, u32[]{:S(2)}) collective-permute-start(bf16[8,64,128]{2,1,0:T(8,128)(2,1)S(1)} %get-tuple-element.59), channel_id=1, source_target_pairs={{0,8},{1,3},{2,10},{3,5},{4,12},{5,7},{6,14},{7,1},{8,16},{9,11},{... | collective-permute-start | bytes 393224 | tf_op jit(solution)/shard_map/ppermute | solution.py:55
  118.2 4.0 %collective-permute-start.24 = (bf16[8,64,128]{2,1,0:T(8,128)(2,1)S(1)}, bf16[8,64,128]{2,1,0:T(8,128)(2,1)S(1)}, u32[]{:S(2)}, u32[]{:S(2)}) collective-permute-start(bf16[8,64,128]{2,1,0:T(8,128)(2,1)S(1)} %get-tuple-element.60), channel_id=1, source_target_pairs={{0,24},{1,7},{2,26},{3,1},{4,28},{5,3},{6,30},{7,5},{8,0},{9,15},{... | collective-permute-start | bytes 393224 | tf_op jit(solution)/shard_map/ppermute | solution.py:55
  119.8 5.3 %collective-permute-start.23 = (bf16[8,64,128]{2,1,0:T(8,128)(2,1)S(1)}, bf16[8,64,128]{2,1,0:T(8,128)(2,1)S(1)}, u32[]{:S(2)}, u32[]{:S(2)}) collective-permute-start(bf16[8,64,128]{2,1,0:T(8,128)(2,1)S(1)} %get-tuple-element.61), channel_id=1, source_target_pairs={{0,16},{1,5},{2,18},{3,7},{4,20},{5,1},{6,22},{7,3},{8,24},{9,13},... | collective-permute-start | bytes 393224 | tf_op jit(solution)/shard_map/ppermute | solution.py:55
  125.3 4.2 %collective-permute-start.25 = (bf16[4,64,128]{2,1,0:T(8,128)(2,1)S(1)}, bf16[4,64,128]{2,1,0:T(8,128)(2,1)S(1)}, u32[]{:S(2)}, u32[]{:S(2)}) collective-permute-start(bf16[4,64,128]{2,1,0:T(8,128)(2,1)S(1)} %broadcast_select_fusion.6), channel_id=1, source_target_pairs={{0,1},{1,0},{2,3},{3,2},{4,5},{5,4},{6,7},{7,6},{8,9},{9,8},{10,11... | collective-permute-start | bytes 196616 | tf_op jit(solution)/shard_map/ppermute | solution.py:55

commit v5 on v3

--- a/solution.py
+++ b/solution.py
@@ -321,12 +321,12 @@
                 ),
                 name="contract_second",
             )(pairs, own_rows, other_rows, *rights, left)
-        got = [send(sums[k + 1], first(d)) for k, d in enumerate(shifts)]
+        got = [send(sums[k + 1], first(shifts[k])) for k in (1, 0, 2)]
         summed = sums[0].astype(f32)
         for g in got:
             summed = summed + g.astype(f32)
         summed = summed.astype(bf16).reshape(4, blocks, half, side)
-        got = [send(summed[k + 1], second(d)) for k, d in enumerate(shifts)]
+        got = [send(summed[k + 1], second(shifts[k])) for k in (1, 0, 2)]
         gradient = summed[0].astype(f32)
         for g in got:
             gradient = gradient + g.astype(f32)

time: 131 us -> 129 us (0.985)
    ppermute x26, starting transfers between devices: 40.9 us -> 39.6 us  [send(): return lax.ppermute(a, axes, perm)]
  transfers between devices with their start and end apart: 26 -> 26, of which waited for: 16 -> 17; matrix products, arithmetic and copies ran while one was open for 8% -> 8% of each run, Pallas kernels for 5% -> 5%
where the time goes in v5:
time: 129 us; the launch traced here: 128 us
  waiting for transfers between devices  52.4 us (41%)
  starting transfers between devices  39.6 us (31%)
  Pallas kernels  21.8 us (17%)
  local copies, waits for them, and re-layouts  10.7 us (8%)
  other arithmetic  3.52 us (3%)
    ppermute x26, waiting for transfers between devices, send(): return lax.ppermute(a, axes, perm)  52.4 us
    ppermute x26, starting transfers between devices, send(): return lax.ppermute(a, axes, perm)  39.6 us
    pallas_call x1, Pallas kernels, on_device(): pl.pallas_call(second_kernel, out_shape=sums_shape, in_specs=[smem] + [vm...  10.4 us
    reshape x1, local copies, waits for them, and re-layouts, on_device(): right_own = right_env.reshape(nb, side, wide)  7.29 us
    pallas_call x1, Pallas kernels, on_device(): pl.pallas_call(product_kernel, out_shape=[jax.ShapeDtypeStruct((wide, blo...  6.09 us
    pallas_call x1, Pallas kernels, on_device(): pl.pallas_call(first_kernel, out_shape=sums_shape + [jax.ShapeDtypeStruct...  5.3 us
  transfers between devices with their start and end apart: 26, of which 17 were waited for; matrix products, arithmetic and copies ran while one was open for 8% of the time, Pallas kernels for 5%

profile of v5, /device:TPU:1, one launch (start us, length us, event | category | flops | bytes accessed | tf_op | source)
XLA Modules:
  0.0 128.3 jit_solution(2861032530930651371)
XLA Ops:
  0.0 3.2 %collective-permute-start.1 = (bf16[4,128,128]{2,1,0:T(8,128)(2,1)}, bf16[4,128,128]{2,1,0:T(8,128)(2,1)S(1)}, u32[]{:S(2)}, u32[]{:S(2)}) collective-permute-start(bf16[4,128,128]{2,1,0:T(8,128)(2,1)} %param.9), channel_id=1, source_target_pairs={{0,1},{1,0},{2,3},{3,2},{4,5},{5,4},{6,7},{7,6},{8,9},{9,8},{10,11... | collective-permute-start | bytes 393224 | tf_op jit(solution)/shard_map/ppermute | solution.py:55
  3.3 0.2 copy.12
  3.5 1.9 %collective-permute-start = (bf16[64,1408]{1,0:T(8,128)(2,1)S(1)}, bf16[64,1408]{1,0:T(8,128)(2,1)S(1)}, u32[]{:S(2)}, u32[]{:S(2)}) collective-permute-start(bf16[64,1408]{1,0:T(8,128)(2,1)S(1)} %pad_dynamic-slice_fusion), channel_id=1, source_target_pairs={{0,192},{1,65},{2,194},{3,67},{4,196},{5,69},{6,70},{7,199},{8,72}... | collective-permute-start | bytes 540680 | tf_op jit(solution)/shard_map/ppermute | solution.py:55
  5.4 0.7 fusion.3
  6.1 0.7 add_bitcast_fusion
  6.8 0.7 stack.48
  7.5 0.0 copy-start.5
  7.5 4.1 %collective-permute-start.2 = (s32[5,32]{1,0:T(8,128)S(1)}, s32[5,32]{1,0:T(8,128)S(1)}, u32[]{:S(2)}, u32[]{:S(2)}) collective-permute-start(s32[5,32]{1,0:T(8,128)S(1)} %stack.48), channel_id=1, source_target_pairs={{0,1},{1,0},{2,3},{3,2},{4,5},{5,4},{6,7},{7,6},{8,9},{9,8},{10,11... | collective-permute-start | bytes 1928 | tf_op jit(solution)/shard_map/ppermute | solution.py:55
  11.6 7.3 %reshape.215.right_own = bf16[4,128,4096]{2,1,0:T(8,128)(2,1)} reshape(bf16[4,128,32,128]{3,2,1,0:T(8,128)(2,1)} %param.10) | data formatting | bytes 8388608 | tf_op jit(solution)/shard_map/reshape | solution.py:226
  18.9 0.1 collective-permute-start.6
  19.0 0.1 pad.16.clone
  19.1 0.1 select_add_fusion.1
  19.2 0.1 add.252
  19.2 0.1 add.256
  19.4 3.7 %collective-permute-start.5 = (bf16[64,1408]{1,0:T(8,128)(2,1)S(1)}, bf16[64,1408]{1,0:T(8,128)(2,1)S(1)}, u32[]{:S(2)}, u32[]{:S(2)}) collective-permute-start(bf16[64,1408]{1,0:T(8,128)(2,1)S(1)} %collective-permute-done), channel_id=1, source_target_pairs={{0,6},{1,25},{2,0},{3,27},{4,2},{5,29},{6,4},{7,31},{8,14},{9,1},{... | collective-permute-start | bytes 540680 | tf_op jit(solution)/shard_map/ppermute | solution.py:55
  23.1 1.8 %collective-permute-start.8 = (bf16[64,4096]{1,0:T(8,128)(2,1)S(1)}, bf16[64,4096]{1,0:T(8,128)(2,1)S(1)}, u32[]{:S(2)}, u32[]{:S(2)}) collective-permute-start(bf16[64,4096]{1,0:T(8,128)(2,1)S(1)} %bitcast.23), channel_id=1, source_target_pairs={{0,224},{1,225},{2,226},{3,227},{4,228},{5,229},{6,230},{7,231},{8... | collective-permute-start | bytes 1572872 | tf_op jit(solution)/shard_map/ppermute | solution.py:55
  24.9 0.1 broadcast_select_fusion.2
  25.0 2.5 %collective-permute-done.5 = bf16[64,1408]{1,0:T(8,128)(2,1)S(1)} collective-permute-done((bf16[64,1408]{1,0:T(8,128)(2,1)S(1)}, bf16[64,1408]{1,0:T(8,128)(2,1)S(1)}, u32[]{:S(2)}, u32[]{:S(2)}) %collective-permute-start.5) | collective-permute-done | bytes 180256 | tf_op jit(solution)/shard_map/ppermute | solution.py:55
  27.5 0.1 broadcast_add_fusion
  27.5 1.4 %collective-permute-done.4 = bf16[64,1408]{1,0:T(8,128)(2,1)S(1)} collective-permute-done((bf16[64,1408]{1,0:T(8,128)(2,1)S(1)}, bf16[64,1408]{1,0:T(8,128)(2,1)S(1)}, u32[]{:S(2)}, u32[]{:S(2)}) %collective-permute-start.4) | collective-permute-done | bytes 180256 | tf_op jit(solution)/shard_map/ppermute | solution.py:55
  28.9 4.8 %collective-permute-done.3 = bf16[64,1408]{1,0:T(8,128)(2,1)S(1)} collective-permute-done((bf16[64,1408]{1,0:T(8,128)(2,1)S(1)}, bf16[64,1408]{1,0:T(8,128)(2,1)S(1)}, u32[]{:S(2)}, u32[]{:S(2)}) %collective-permute-start.3) | collective-permute-done | bytes 180256 | tf_op jit(solution)/shard_map/ppermute | solution.py:55
  33.8 0.1 pad_maximum_fusion.part0
  33.9 3.0 %collective-permute-start.10 = (bf16[4,64,1408]{2,1,0:T(8,128)(2,1)S(1)}, bf16[4,64,1408]{2,1,0:T(8,128)(2,1)S(1)}, u32[]{:S(2)}, u32[]{:S(2)}) collective-permute-start(bf16[4,64,1408]{2,1,0:T(8,128)(2,1)S(1)} %pad_maximum_fusion.part0), channel_id=1, source_target_pairs={{0,16},{1,5},{2,18},{3,7},{4,20},{5,1},{6,22},{7,3},{8,24},{9,13},... | collective-permute-start | bytes 2162696 | tf_op jit(solution)/shard_map/ppermute | solution.py:55
  36.8 0.5 collective-permute-start.9
  37.3 2.6 %collective-permute-done.7.below = bf16[64,4096]{1,0:T(8,128)(2,1)S(1)} collective-permute-done((bf16[64,4096]{1,0:T(8,128)(2,1)S(1)}, bf16[64,4096]{1,0:T(8,128)(2,1)S(1)}, u32[]{:S(2)}, u32[]{:S(2)}) %collective-permute-start.7) | collective-permute-done | bytes 524320 | tf_op jit(solution)/shard_map/ppermute | solution.py:55
  39.9 1.1 collective-permute-start.11
  41.0 0.1 pad_add_fusion
  41.1 0.1 add_add_fusion.pairs
  41.2 2.2 %copy-done.1 = bf16[4,128,4096]{2,1,0:T(8,128)(2,1)S(1)} copy-done((bf16[4,128,4096]{2,1,0:T(8,128)(2,1)S(1)}, bf16[4,128,4096]{2,1,0:T(8,128)(2,1)}, u32[]{:S(2)}) %copy-start.1) | copy-done | bytes 4194328
  43.3 6.1 %product.1 = (bf16[4096,1024]{1,0:T(8,128)(2,1)S(1)}, bf16[8,192,128]{2,1,0:T(8,128)(2,1)S(1)}) custom-call(s32[1]{0:T(128)} %bitcast.10.core, bf16[8,64,128]{2,1,0:T(8,128)(2,1)S(1)} %get-tuple-element.68.own_rows, bf16[8,64,128]{2,1,0:T(8,128)(2,1)S(1)} %get-tuple-element.67.other_rows, bf16[4,128,4096]{2,1,0:T(8,128)(2,1)S(1)} %copy-done.1, ...), custom_call_target="tpu_custom_call" | custom-call | flops 2684354560 | tf_op jit(solution)/shard_map/product/pallas_call | solution.py:279
  49.4 4.6 %collective-permute-done.11.part3 = bf16[4,64,1408]{2,1,0:T(8,128)(2,1)S(1)} collective-permute-done((bf16[4,64,1408]{2,1,0:T(8,128)(2,1)S(1)}, bf16[4,64,1408]{2,1,0:T(8,128)(2,1)S(1)}, u32[]{:S(2)}, u32[]{:S(2)}) %collective-permute-start.11) | collective-permute-done | bytes 720928 | tf_op jit(solution)/shard_map/ppermute | solution.py:55
  54.1 5.3 %contract_first.1 = (bf16[32,64,128]{2,1,0:T(8,128)(2,1)S(1)}, bf16[32,64,128]{2,1,0:T(8,128)(2,1)S(1)}, bf16[32,64,128]{2,1,0:T(8,128)(2,1)S(1)}, bf16[32,64,128]{2,1,0:T(8,128)(2,1)S(1)}, bf16[576,4224]{1,0:T(8,128)(2,1)S(1)}) custom-call(s32[4,64]{1,0:T(4,128)S(1)} %add_add_fusion.pairs, s32[2,16]{1,0:T(2,128)S(1)} %pad_add_fusion.1.places, ...), custom_call_target="tpu_custom_call" | custom-call | flops 2684354560 | tf_op jit(solution)/shard_map/contract_first/pallas_call | solution.py:297
  59.4 0.5 collective-permute-start.12
  59.9 1.6 %collective-permute-start.13 = (bf16[32,64,128]{2,1,0:T(8,128)(2,1)S(1)}, bf16[32,64,128]{2,1,0:T(8,128)(2,1)S(1)}, u32[]{:S(2)}, u32[]{:S(2)}) collective-permute-start(bf16[32,64,128]{2,1,0:T(8,128)(2,1)S(1)} %get-tuple-element.46), channel_id=1, source_target_pairs={{0,2},{1,9},{2,4},{3,11},{4,6},{5,13},{6,0},{7,15},{8,10},{9,17},{... | collective-permute-start | bytes 1572872 | tf_op jit(solution)/shard_map/ppermute | solution.py:55
  61.5 1.0 collective-permute-start.14
  62.5 6.8 %collective-permute-done.12 = bf16[32,64,128]{2,1,0:T(8,128)(2,1)S(1)} collective-permute-done((bf16[32,64,128]{2,1,0:T(8,128)(2,1)S(1)}, bf16[32,64,128]{2,1,0:T(8,128)(2,1)S(1)}, u32[]{:S(2)}, u32[]{:S(2)}) %collective-permute-start.12) | collective-permute-done | bytes 524320 | tf_op jit(solution)/shard_map/ppermute | solution.py:55
  69.3 5.6 %collective-permute-done.13 = bf16[32,64,128]{2,1,0:T(8,128)(2,1)S(1)} collective-permute-done((bf16[32,64,128]{2,1,0:T(8,128)(2,1)S(1)}, bf16[32,64,128]{2,1,0:T(8,128)(2,1)S(1)}, u32[]{:S(2)}, u32[]{:S(2)}) %collective-permute-start.13) | collective-permute-done | bytes 524320 | tf_op jit(solution)/shard_map/ppermute | solution.py:55
  74.9 0.4 add_convert_fusion.1
  75.3 1.5 %collective-permute-start.15 = (bf16[8,64,128]{2,1,0:T(8,128)(2,1)S(1)}, bf16[8,64,128]{2,1,0:T(8,128)(2,1)S(1)}, u32[]{:S(2)}, u32[]{:S(2)}) collective-permute-start(bf16[8,64,128]{2,1,0:T(8,128)(2,1)S(1)} %get-tuple-element.64), channel_id=1, source_target_pairs={{0,16},{1,5},{2,18},{3,7},{4,20},{5,1},{6,22},{7,3},{8,24},{9,13},... | collective-permute-start | bytes 393224 | tf_op jit(solution)/shard_map/ppermute | solution.py:55
  76.8 1.4 %collective-permute-start.17 = (bf16[8,64,128]{2,1,0:T(8,128)(2,1)S(1)}, bf16[8,64,128]{2,1,0:T(8,128)(2,1)S(1)}, u32[]{:S(2)}, u32[]{:S(2)}) collective-permute-start(bf16[8,64,128]{2,1,0:T(8,128)(2,1)S(1)} %get-tuple-element.65), channel_id=1, source_target_pairs={{0,24},{1,7},{2,26},{3,1},{4,28},{5,3},{6,30},{7,5},{8,0},{9,15},{... | collective-permute-start | bytes 393224 | tf_op jit(solution)/shard_map/ppermute | solution.py:55
  78.2 0.1 collective-permute-start.16
  78.3 2.4 %collective-permute-done.15 = bf16[8,64,128]{2,1,0:T(8,128)(2,1)S(1)} collective-permute-done((bf16[8,64,128]{2,1,0:T(8,128)(2,1)S(1)}, bf16[8,64,128]{2,1,0:T(8,128)(2,1)S(1)}, u32[]{:S(2)}, u32[]{:S(2)}) %collective-permute-start.15) | collective-permute-done | bytes 131104 | tf_op jit(solution)/shard_map/ppermute | solution.py:55
  80.7 1.1 collective-permute-done.17
  81.8 1.4 %collective-permute-done.16 = bf16[8,64,128]{2,1,0:T(8,128)(2,1)S(1)} collective-permute-done((bf16[8,64,128]{2,1,0:T(8,128)(2,1)S(1)}, bf16[8,64,128]{2,1,0:T(8,128)(2,1)S(1)}, u32[]{:S(2)}, u32[]{:S(2)}) %collective-permute-start.16) | collective-permute-done | bytes 131104 | tf_op jit(solution)/shard_map/ppermute | solution.py:55
  83.2 0.1 subtract_convert_fusion.1.own_rows
  83.3 6.7 %collective-permute-start.18 = (bf16[8,64,128]{2,1,0:T(8,128)(2,1)S(1)}, bf16[8,64,128]{2,1,0:T(8,128)(2,1)S(1)}, u32[]{:S(2)}, u32[]{:S(2)}) collective-permute-start(bf16[8,64,128]{2,1,0:T(8,128)(2,1)S(1)} %subtract_convert_fusion.1.own_rows), channel_id=1, source_target_pairs={{0,1},{1,0},{2,3},{3,2},{4,5},{5,4},{6,7},{7,6},{8,9},{9,8},{10,11... | collective-permute-start | bytes 393224 | tf_op jit(solution)/shard_map/ppermute | solution.py:55
  90.0 1.0 collective-permute-done.18.other_rows
  91.0 10.4 %contract_second.1 = (bf16[32,64,128]{2,1,0:T(8,128)(2,1)S(1)}, bf16[32,64,128]{2,1,0:T(8,128)(2,1)S(1)}, bf16[32,64,128]{2,1,0:T(8,128)(2,1)S(1)}, bf16[32,64,128]{2,1,0:T(8,128)(2,1)S(1)}) custom-call(s32[4,64]{1,0:T(4,128)S(1)} %add_add_fusion.pairs, bf16[8,64,128]{2,1,0:T(8,128)(2,1)S(1)} %subtract_convert_fusion.1.own_rows, ...), custom_call_target="tpu_custom_call" | custom-call | flops 5368709120 | tf_op jit(solution)/shard_map/contract_second/pallas_call | solution.py:312
  101.4 0.1 collective-permute-start.19
  101.5 0.3 collective-permute-start.20
  101.7 2.5 %collective-permute-start.21 = (bf16[32,64,128]{2,1,0:T(8,128)(2,1)S(1)}, bf16[32,64,128]{2,1,0:T(8,128)(2,1)S(1)}, u32[]{:S(2)}, u32[]{:S(2)}) collective-permute-start(bf16[32,64,128]{2,1,0:T(8,128)(2,1)S(1)} %get-tuple-element.52), channel_id=1, source_target_pairs={{0,6},{1,25},{2,0},{3,27},{4,2},{5,29},{6,4},{7,31},{8,14},{9,1},{... | collective-permute-start | bytes 1572872 | tf_op jit(solution)/shard_map/ppermute | solution.py:55
  104.2 7.1 %collective-permute-done.19 = bf16[32,64,128]{2,1,0:T(8,128)(2,1)S(1)} collective-permute-done((bf16[32,64,128]{2,1,0:T(8,128)(2,1)S(1)}, bf16[32,64,128]{2,1,0:T(8,128)(2,1)S(1)}, u32[]{:S(2)}, u32[]{:S(2)}) %collective-permute-start.19) | collective-permute-done | bytes 524320 | tf_op jit(solution)/shard_map/ppermute | solution.py:55
  111.3 5.4 %collective-permute-done.20 = bf16[32,64,128]{2,1,0:T(8,128)(2,1)S(1)} collective-permute-done((bf16[32,64,128]{2,1,0:T(8,128)(2,1)S(1)}, bf16[32,64,128]{2,1,0:T(8,128)(2,1)S(1)}, u32[]{:S(2)}, u32[]{:S(2)}) %collective-permute-start.20) | collective-permute-done | bytes 524320 | tf_op jit(solution)/shard_map/ppermute | solution.py:55
  116.7 0.4 add_convert_fusion
  117.1 0.7 collective-permute-start.22
  117.8 1.8 %collective-permute-start.24 = (bf16[8,64,128]{2,1,0:T(8,128)(2,1)S(1)}, bf16[8,64,128]{2,1,0:T(8,128)(2,1)S(1)}, u32[]{:S(2)}, u32[]{:S(2)}) collective-permute-start(bf16[8,64,128]{2,1,0:T(8,128)(2,1)S(1)} %get-tuple-element.62), channel_id=1, source_target_pairs={{0,24},{1,7},{2,26},{3,1},{4,28},{5,3},{6,30},{7,5},{8,0},{9,15},{... | collective-permute-start | bytes 393224 | tf_op jit(solution)/shard_map/ppermute | solution.py:55
  119.6 0.5 collective-permute-start.23
  120.1 2.4 %collective-permute-done.22 = bf16[8,64,128]{2,1,0:T(8,128)(2,1)S(1)} collective-permute-done((bf16[8,64,128]{2,1,0:T(8,128)(2,1)S(1)}, bf16[8,64,128]{2,1,0:T(8,128)(2,1)S(1)}, u32[]{:S(2)}, u32[]{:S(2)}) %collective-permute-start.22) | collective-permute-done | bytes 131104 | tf_op jit(solution)/shard_map/ppermute | solution.py:55
  122.5 1.7 %collective-permute-done.24 = bf16[8,64,128]{2,1,0:T(8,128)(2,1)S(1)} collective-permute-done((bf16[8,64,128]{2,1,0:T(8,128)(2,1)S(1)}, bf16[8,64,128]{2,1,0:T(8,128)(2,1)S(1)}, u32[]{:S(2)}, u32[]{:S(2)}) %collective-permute-start.24) | collective-permute-done | bytes 131104 | tf_op jit(solution)/shard_map/ppermute | solution.py:55
  124.1 0.7 collective-permute-done.23
  124.9 0.1 subtract_convert_fusion
  125.0 1.7 %collective-permute-start.25 = (bf16[4,64,128]{2,1,0:T(8,128)(2,1)S(1)}, bf16[4,64,128]{2,1,0:T(8,128)(2,1)S(1)}, u32[]{:S(2)}, u32[]{:S(2)}) collective-permute-start(bf16[4,64,128]{2,1,0:T(8,128)(2,1)S(1)} %broadcast_select_fusion.6), channel_id=1, source_target_pairs={{0,1},{1,0},{2,3},{3,2},{4,5},{5,4},{6,7},{7,6},{8,9},{9,8},{10,11... | collective-permute-start | bytes 196616 | tf_op jit(solution)/shard_map/ppermute | solution.py:55
  126.7 0.9 collective-permute-done.25
  127.6 0.7 pad_maximum_fusion.2
  (35 shorter events, 0.3 us)
Async XLA Ops:
  0.0 3.2 %copy-start = (bf16[1,128,32,128]{3,2,1,0:T(8,128)(2,1)S(1)}, bf16[1,128,32,128]{3,2,1,0:T(8,128)(2,1)}, u32[]{:S(2)}) copy-start(bf16[1,128,32,128]{3,2,1,0:T(8,128)(2,1)} %param.11) | copy-start | bytes 3145732
  0.0 18.9 %collective-permute-start.1 = (bf16[4,128,128]{2,1,0:T(8,128)(2,1)}, bf16[4,128,128]{2,1,0:T(8,128)(2,1)S(1)}, u32[]{:S(2)}, u32[]{:S(2)}) collective-permute-start(bf16[4,128,128]{2,1,0:T(8,128)(2,1)} %param.9), channel_id=1, source_target_pairs={{0,1},{1,0},{2,3},{3,2},{4,5},{5,4},{6,7},{7,6},{8,9},{9,8},{10,11... | collective-permute-start | bytes 393224 | tf_op jit(solution)/shard_map/ppermute | solution.py:55
  3.5 15.4 %collective-permute-start = (bf16[64,1408]{1,0:T(8,128)(2,1)S(1)}, bf16[64,1408]{1,0:T(8,128)(2,1)S(1)}, u32[]{:S(2)}, u32[]{:S(2)}) collective-permute-start(bf16[64,1408]{1,0:T(8,128)(2,1)S(1)} %pad_dynamic-slice_fusion), channel_id=1, source_target_pairs={{0,192},{1,65},{2,194},{3,67},{4,196},{5,69},{6,70},{7,199},{8,72}... | collective-permute-start | bytes 540680 | tf_op jit(solution)/shard_map/ppermute | solution.py:55
  7.5 11.6 %copy-start.4 = (s32[4]{0:T(128)S(1)}, s32[4]{0:T(128)}, u32[]{:S(2)}) copy-start(s32[4]{0:T(128)} %constant.176.clone) | copy-start | bytes 52
  7.5 17.4 %copy-start.3 = (bf16[4,128,128]{2,1,0:T(8,128)(2,1)S(1)}, bf16[4,128,128]{2,1,0:T(8,128)(2,1)}, u32[]{:S(2)}) copy-start(bf16[4,128,128]{2,1,0:T(8,128)(2,1)} %param.9) | copy-start | bytes 393220
  7.5 19.9 %copy-start.5 = (s32[5]{0:T(128)S(1)}, s32[5]{0:T(128)}, u32[]{:S(2)}) copy-start(s32[5]{0:T(128)} %constant.187) | copy-start | bytes 64
  7.5 11.4 %collective-permute-start.2 = (s32[5,32]{1,0:T(8,128)S(1)}, s32[5,32]{1,0:T(8,128)S(1)}, u32[]{:S(2)}, u32[]{:S(2)}) collective-permute-start(s32[5,32]{1,0:T(8,128)S(1)} %stack.48), channel_id=1, source_target_pairs={{0,1},{1,0},{2,3},{3,2},{4,5},{5,4},{6,7},{7,6},{8,9},{9,8},{10,11... | collective-permute-start | bytes 1928 | tf_op jit(solution)/shard_map/ppermute | solution.py:55
  18.9 15.0 %collective-permute-start.6 = (bf16[4,128,4096]{2,1,0:T(8,128)(2,1)}, bf16[4,128,4096]{2,1,0:T(8,128)(2,1)}, u32[]{:S(2)}, u32[]{:S(2)}) collective-permute-start(bf16[4,128,4096]{2,1,0:T(8,128)(2,1)} %reshape.215.right_own), channel_id=1, source_target_pairs={{0,1},{1,0},{2,3},{3,2},{4,5},{5,4},{6,7},{7,6},{8,9},{9,8},{10,11... | collective-permute-start | bytes 12582920 | tf_op jit(solution)/shard_map/ppermute | solution.py:55
  19.4 8.1 %collective-permute-start.5 = (bf16[64,1408]{1,0:T(8,128)(2,1)S(1)}, bf16[64,1408]{1,0:T(8,128)(2,1)S(1)}, u32[]{:S(2)}, u32[]{:S(2)}) collective-permute-start(bf16[64,1408]{1,0:T(8,128)(2,1)S(1)} %collective-permute-done), channel_id=1, source_target_pairs={{0,6},{1,25},{2,0},{3,27},{4,2},{5,29},{6,4},{7,31},{8,14},{9,1},{... | collective-permute-start | bytes 540680 | tf_op jit(solution)/shard_map/ppermute | solution.py:55
  23.1 5.8 %collective-permute-start.4 = (bf16[64,1408]{1,0:T(8,128)(2,1)S(1)}, bf16[64,1408]{1,0:T(8,128)(2,1)S(1)}, u32[]{:S(2)}, u32[]{:S(2)}) collective-permute-start(bf16[64,1408]{1,0:T(8,128)(2,1)S(1)} %collective-permute-done), channel_id=1, source_target_pairs={{0,4},{1,17},{2,6},{3,19},{4,0},{5,21},{6,2},{7,23},{8,12},{9,25},... | collective-permute-start | bytes 540680 | tf_op jit(solution)/shard_map/ppermute | solution.py:55
  23.1 14.2 %collective-permute-start.8 = (bf16[64,4096]{1,0:T(8,128)(2,1)S(1)}, bf16[64,4096]{1,0:T(8,128)(2,1)S(1)}, u32[]{:S(2)}, u32[]{:S(2)}) collective-permute-start(bf16[64,4096]{1,0:T(8,128)(2,1)S(1)} %bitcast.23), channel_id=1, source_target_pairs={{0,224},{1,225},{2,226},{3,227},{4,228},{5,229},{6,230},{7,231},{8... | collective-permute-start | bytes 1572872 | tf_op jit(solution)/shard_map/ppermute | solution.py:55
  24.9 15.1 %collective-permute-start.7 = (bf16[64,4096]{1,0:T(8,128)(2,1)S(1)}, bf16[64,4096]{1,0:T(8,128)(2,1)S(1)}, u32[]{:S(2)}, u32[]{:S(2)}) collective-permute-start(bf16[64,4096]{1,0:T(8,128)(2,1)S(1)} %bitcast.24), channel_id=1, source_target_pairs={{0,32},{1,33},{2,34},{3,35},{4,36},{5,37},{6,38},{7,39},{8,40},{9,... | collective-permute-start | bytes 1572872 | tf_op jit(solution)/shard_map/ppermute | solution.py:55
  27.5 6.3 %collective-permute-start.3 = (bf16[64,1408]{1,0:T(8,128)(2,1)S(1)}, bf16[64,1408]{1,0:T(8,128)(2,1)S(1)}, u32[]{:S(2)}, u32[]{:S(2)}) collective-permute-start(bf16[64,1408]{1,0:T(8,128)(2,1)S(1)} %collective-permute-done), channel_id=1, source_target_pairs={{0,2},{1,9},{2,4},{3,11},{4,6},{5,13},{6,0},{7,15},{8,10},{9,17},{... | collective-permute-start | bytes 540680 | tf_op jit(solution)/shard_map/ppermute | solution.py:55
  33.9 20.2 %collective-permute-start.10 = (bf16[4,64,1408]{2,1,0:T(8,128)(2,1)S(1)}, bf16[4,64,1408]{2,1,0:T(8,128)(2,1)S(1)}, u32[]{:S(2)}, u32[]{:S(2)}) collective-permute-start(bf16[4,64,1408]{2,1,0:T(8,128)(2,1)S(1)} %pad_maximum_fusion.part0), channel_id=1, source_target_pairs={{0,16},{1,5},{2,18},{3,7},{4,20},{5,1},{6,22},{7,3},{8,24},{9,13},... | collective-permute-start | bytes 2162696 | tf_op jit(solution)/shard_map/ppermute | solution.py:55
  36.8 17.2 %collective-permute-start.9 = (bf16[4,64,1408]{2,1,0:T(8,128)(2,1)S(1)}, bf16[4,64,1408]{2,1,0:T(8,128)(2,1)S(1)}, u32[]{:S(2)}, u32[]{:S(2)}) collective-permute-start(bf16[4,64,1408]{2,1,0:T(8,128)(2,1)S(1)} %pad_maximum_fusion.part0), channel_id=1, source_target_pairs={{0,8},{1,3},{2,10},{3,5},{4,12},{5,7},{6,14},{7,1},{8,16},{9,11},{... | collective-permute-start | bytes 2162696 | tf_op jit(solution)/shard_map/ppermute | solution.py:55
  39.9 14.1 %collective-permute-start.11 = (bf16[4,64,1408]{2,1,0:T(8,128)(2,1)S(1)}, bf16[4,64,1408]{2,1,0:T(8,128)(2,1)S(1)}, u32[]{:S(2)}, u32[]{:S(2)}) collective-permute-start(bf16[4,64,1408]{2,1,0:T(8,128)(2,1)S(1)} %pad_maximum_fusion.part0), channel_id=1, source_target_pairs={{0,24},{1,7},{2,26},{3,1},{4,28},{5,3},{6,30},{7,5},{8,0},{9,15},{... | collective-permute-start | bytes 2162696 | tf_op jit(solution)/shard_map/ppermute | solution.py:55
  41.2 2.2 %copy-start.1 = (bf16[4,128,4096]{2,1,0:T(8,128)(2,1)S(1)}, bf16[4,128,4096]{2,1,0:T(8,128)(2,1)}, u32[]{:S(2)}) copy-start(bf16[4,128,4096]{2,1,0:T(8,128)(2,1)} %reshape.215.right_own) | copy-start | bytes 12582916
  59.4 31.6 %copy-start.2 = (bf16[4,128,4096]{2,1,0:T(8,128)(2,1)S(1)}, bf16[4,128,4096]{2,1,0:T(8,128)(2,1)}, u32[]{:S(2)}) copy-start(bf16[4,128,4096]{2,1,0:T(8,128)(2,1)} %reshape.215.right_own) | copy-start | bytes 12582916
  59.4 10.0 %collective-permute-start.12 = (bf16[32,64,128]{2,1,0:T(8,128)(2,1)S(1)}, bf16[32,64,128]{2,1,0:T(8,128)(2,1)S(1)}, u32[]{:S(2)}, u32[]{:S(2)}) collective-permute-start(bf16[32,64,128]{2,1,0:T(8,128)(2,1)S(1)} %get-tuple-element.45), channel_id=1, source_target_pairs={{0,4},{1,17},{2,6},{3,19},{4,0},{5,21},{6,2},{7,23},{8,12},{9,25},... | collective-permute-start | bytes 1572872 | tf_op jit(solution)/shard_map/ppermute | solution.py:55
  59.9 15.0 %collective-permute-start.13 = (bf16[32,64,128]{2,1,0:T(8,128)(2,1)S(1)}, bf16[32,64,128]{2,1,0:T(8,128)(2,1)S(1)}, u32[]{:S(2)}, u32[]{:S(2)}) collective-permute-start(bf16[32,64,128]{2,1,0:T(8,128)(2,1)S(1)} %get-tuple-element.46), channel_id=1, source_target_pairs={{0,2},{1,9},{2,4},{3,11},{4,6},{5,13},{6,0},{7,15},{8,10},{9,17},{... | collective-permute-start | bytes 1572872 | tf_op jit(solution)/shard_map/ppermute | solution.py:55
  61.5 13.4 %collective-permute-start.14 = (bf16[32,64,128]{2,1,0:T(8,128)(2,1)S(1)}, bf16[32,64,128]{2,1,0:T(8,128)(2,1)S(1)}, u32[]{:S(2)}, u32[]{:S(2)}) collective-permute-start(bf16[32,64,128]{2,1,0:T(8,128)(2,1)S(1)} %get-tuple-element.47), channel_id=1, source_target_pairs={{0,6},{1,25},{2,0},{3,27},{4,2},{5,29},{6,4},{7,31},{8,14},{9,1},{... | collective-permute-start | bytes 1572872 | tf_op jit(solution)/shard_map/ppermute | solution.py:55
  75.3 5.4 %collective-permute-start.15 = (bf16[8,64,128]{2,1,0:T(8,128)(2,1)S(1)}, bf16[8,64,128]{2,1,0:T(8,128)(2,1)S(1)}, u32[]{:S(2)}, u32[]{:S(2)}) collective-permute-start(bf16[8,64,128]{2,1,0:T(8,128)(2,1)S(1)} %get-tuple-element.64), channel_id=1, source_target_pairs={{0,16},{1,5},{2,18},{3,7},{4,20},{5,1},{6,22},{7,3},{8,24},{9,13},... | collective-permute-start | bytes 393224 | tf_op jit(solution)/shard_map/ppermute | solution.py:55
  76.8 4.9 %collective-permute-start.17 = (bf16[8,64,128]{2,1,0:T(8,128)(2,1)S(1)}, bf16[8,64,128]{2,1,0:T(8,128)(2,1)S(1)}, u32[]{:S(2)}, u32[]{:S(2)}) collective-permute-start(bf16[8,64,128]{2,1,0:T(8,128)(2,1)S(1)} %get-tuple-element.65), channel_id=1, source_target_pairs={{0,24},{1,7},{2,26},{3,1},{4,28},{5,3},{6,30},{7,5},{8,0},{9,15},{... | collective-permute-start | bytes 393224 | tf_op jit(solution)/shard_map/ppermute | solution.py:55
  78.2 5.0 %collective-permute-start.16 = (bf16[8,64,128]{2,1,0:T(8,128)(2,1)S(1)}, bf16[8,64,128]{2,1,0:T(8,128)(2,1)S(1)}, u32[]{:S(2)}, u32[]{:S(2)}) collective-permute-start(bf16[8,64,128]{2,1,0:T(8,128)(2,1)S(1)} %get-tuple-element.66), channel_id=1, source_target_pairs={{0,8},{1,3},{2,10},{3,5},{4,12},{5,7},{6,14},{7,1},{8,16},{9,11},{... | collective-permute-start | bytes 393224 | tf_op jit(solution)/shard_map/ppermute | solution.py:55
  83.3 7.7 %collective-permute-start.18 = (bf16[8,64,128]{2,1,0:T(8,128)(2,1)S(1)}, bf16[8,64,128]{2,1,0:T(8,128)(2,1)S(1)}, u32[]{:S(2)}, u32[]{:S(2)}) collective-permute-start(bf16[8,64,128]{2,1,0:T(8,128)(2,1)S(1)} %subtract_convert_fusion.1.own_rows), channel_id=1, source_target_pairs={{0,1},{1,0},{2,3},{3,2},{4,5},{5,4},{6,7},{7,6},{8,9},{9,8},{10,11... | collective-permute-start | bytes 393224 | tf_op jit(solution)/shard_map/ppermute | solution.py:55
  101.4 10.0 %collective-permute-start.19 = (bf16[32,64,128]{2,1,0:T(8,128)(2,1)S(1)}, bf16[32,64,128]{2,1,0:T(8,128)(2,1)S(1)}, u32[]{:S(2)}, u32[]{:S(2)}) collective-permute-start(bf16[32,64,128]{2,1,0:T(8,128)(2,1)S(1)} %get-tuple-element.50), channel_id=1, source_target_pairs={{0,4},{1,17},{2,6},{3,19},{4,0},{5,21},{6,2},{7,23},{8,12},{9,25},... | collective-permute-start | bytes 1572872 | tf_op jit(solution)/shard_map/ppermute | solution.py:55
  101.5 15.2 %collective-permute-start.20 = (bf16[32,64,128]{2,1,0:T(8,128)(2,1)S(1)}, bf16[32,64,128]{2,1,0:T(8,128)(2,1)S(1)}, u32[]{:S(2)}, u32[]{:S(2)}) collective-permute-start(bf16[32,64,128]{2,1,0:T(8,128)(2,1)S(1)} %get-tuple-element.51), channel_id=1, source_target_pairs={{0,2},{1,9},{2,4},{3,11},{4,6},{5,13},{6,0},{7,15},{8,10},{9,17},{... | collective-permute-start | bytes 1572872 | tf_op jit(solution)/shard_map/ppermute | solution.py:55
  101.7 14.9 %collective-permute-start.21 = (bf16[32,64,128]{2,1,0:T(8,128)(2,1)S(1)}, bf16[32,64,128]{2,1,0:T(8,128)(2,1)S(1)}, u32[]{:S(2)}, u32[]{:S(2)}) collective-permute-start(bf16[32,64,128]{2,1,0:T(8,128)(2,1)S(1)} %get-tuple-element.52), channel_id=1, source_target_pairs={{0,6},{1,25},{2,0},{3,27},{4,2},{5,29},{6,4},{7,31},{8,14},{9,1},{... | collective-permute-start | bytes 1572872 | tf_op jit(solution)/shard_map/ppermute | solution.py:55
  117.1 5.4 %collective-permute-start.22 = (bf16[8,64,128]{2,1,0:T(8,128)(2,1)S(1)}, bf16[8,64,128]{2,1,0:T(8,128)(2,1)S(1)}, u32[]{:S(2)}, u32[]{:S(2)}) collective-permute-start(bf16[8,64,128]{2,1,0:T(8,128)(2,1)S(1)} %get-tuple-element.61), channel_id=1, source_target_pairs={{0,16},{1,5},{2,18},{3,7},{4,20},{5,1},{6,22},{7,3},{8,24},{9,13},... | collective-permute-start | bytes 393224 | tf_op jit(solution)/shard_map/ppermute | solution.py:55
  117.8 6.4 %collective-permute-start.24 = (bf16[8,64,128]{2,1,0:T(8,128)(2,1)S(1)}, bf16[8,64,128]{2,1,0:T(8,128)(2,1)S(1)}, u32[]{:S(2)}, u32[]{:S(2)}) collective-permute-start(bf16[8,64,128]{2,1,0:T(8,128)(2,1)S(1)} %get-tuple-element.62), channel_id=1, source_target_pairs={{0,24},{1,7},{2,26},{3,1},{4,28},{5,3},{6,30},{7,5},{8,0},{9,15},{... | collective-permute-start | bytes 393224 | tf_op jit(solution)/shard_map/ppermute | solution.py:55
  119.6 5.3 %collective-permute-start.23 = (bf16[8,64,128]{2,1,0:T(8,128)(2,1)S(1)}, bf16[8,64,128]{2,1,0:T(8,128)(2,1)S(1)}, u32[]{:S(2)}, u32[]{:S(2)}) collective-permute-start(bf16[8,64,128]{2,1,0:T(8,128)(2,1)S(1)} %get-tuple-element.63), channel_id=1, source_target_pairs={{0,8},{1,3},{2,10},{3,5},{4,12},{5,7},{6,14},{7,1},{8,16},{9,11},{... | collective-permute-start | bytes 393224 | tf_op jit(solution)/shard_map/ppermute | solution.py:55
  125.0 2.6 %collective-permute-start.25 = (bf16[4,64,128]{2,1,0:T(8,128)(2,1)S(1)}, bf16[4,64,128]{2,1,0:T(8,128)(2,1)S(1)}, u32[]{:S(2)}, u32[]{:S(2)}) collective-permute-start(bf16[4,64,128]{2,1,0:T(8,128)(2,1)S(1)} %broadcast_select_fusion.6), channel_id=1, source_target_pairs={{0,1},{1,0},{2,3},{3,2},{4,5},{5,4},{6,7},{7,6},{8,9},{9,8},{10,11... | collective-permute-start | bytes 196616 | tf_op jit(solution)/shard_map/ppermute | solution.py:55
